TPU v7x, 256 devices: a whole 4x4x8 slice. The times are simulated.
256 devices in a mesh: space: 32 (over y, x, core), dp: 8 (over z).
Axes of the slice: x: 4, y: 4, z: 8, core: 2. Of those that a mesh axis runs over, the one named last changes fastest.
Arguments:
- features: bfloat16 [8, 32, 512, 256], P('dp', 'space'), may hold values from -6 to 6
- grad_out: bfloat16 [8, 32, 512, 256], P('dp', 'space'), may hold values from -6 to 6
- weight: bfloat16 [27, 256, 256], replicated, may hold values from -0.078125 to 0.078125
- neighbours: int32 [8, 32, 27], P('dp', 'space'), may hold values from -1 to 31, as said below
Outputs:
- conv_out: bfloat16 [8, 32, 512, 256], P('dp', 'space')
- grad_in: bfloat16 [8, 32, 512, 256], P('dp', 'space')
- grad_weight: float32 [6912, 256], P('dp')
Inputs may be any that keep to these rules, and one draw needn't show every extreme that they name: Each scene's occupied bricks lie in a corridor two bricks wide in x and y, taken in the order z * 4 + y * 2 + x and given in that order to the slots, device by device along space; every device holds exactly one brick slot, and it is occupied. An entry names a slot of the same scene; neighbours are symmetric (slot m at offset k of slot n means slot n at offset 26 - k of slot m), offset 13 of an occupied slot is the slot itself, and a neighbour's device differs from the slot's device by at most 7 along space.
All inputs are finite; a program needn't handle non-finite values.
Results may differ from a plain program's by a relative error of at most 0.001.
Values may be sent and summed in bfloat16 or wider, within the bound.
No kernel may reach another device: no remote copies, remote signals or barrier semaphores. Data moves between devices by JAX's collectives and lax.ppermute only.
A program may use at most 128 MiB of HBM per device.

v0:
```python
import math

import jax
import jax.numpy as jnp
from jax import lax
from jax.sharding import PartitionSpec as P

reach_limit = 7


def shifted(shard, axis, by):
    devices = lax.axis_size(axis)
    pairs = [(i, i + by) for i in range(devices) if 0 <= i + by < devices]
    return lax.ppermute(shard, axis, pairs)


def faces_of(tiles, layer):
    count = tiles.shape[0]
    channels = tiles.shape[-1]
    cube = tiles.reshape(count, 8, 8, 8, channels)
    face_x = cube[:, layer].reshape(count, 64, channels)
    face_y = cube[:, :, layer].reshape(count, 64, channels)
    face_z = cube[:, :, :, layer].reshape(count, 64, channels)
    return jnp.stack([face_x, face_y, face_z], axis=1)


def source_range(offset):
    if offset < 0:
        return slice(7, 8)
    if offset == 0:
        return slice(0, 8)
    return slice(0, 1)


def target_range(offset):
    if offset < 0:
        return slice(0, 1)
    if offset == 0:
        return slice(1, 9)
    return slice(9, 10)


def build_padded(own_tiles, high_band, low_band, pos_high, pos_low, live):
    count = own_tiles.shape[0]
    channels = own_tiles.shape[-1]
    zero_value = jnp.zeros((), own_tiles.dtype)
    padded = jnp.zeros((count, 10, 10, 10, channels), own_tiles.dtype)
    own_cube = jnp.where(live[:, 13][:, None, None], own_tiles, zero_value).reshape(
        count, 8, 8, 8, channels
    )
    padded = padded.at[:, 1:9, 1:9, 1:9].set(own_cube)
    for k in range(27):
        if k != 13:
            shift_now = (k // 9 - 1, k // 3 % 3 - 1, k % 3 - 1)
            if shift_now[2] != 0:
                face_axis = 2
            elif shift_now[1] != 0:
                face_axis = 1
            else:
                face_axis = 0
            if shift_now[face_axis] < 0:
                face = high_band[pos_high[:, k], face_axis]
            else:
                face = low_band[pos_low[:, k], face_axis]
            face = jnp.where(live[:, k][:, None, None], face, zero_value)
            others = [d for d in range(3) if d != face_axis]
            plane = face.reshape(count, 8, 8, channels)
            piece = plane[:, source_range(shift_now[others[0]]), source_range(shift_now[others[1]])]
            piece = jnp.expand_dims(piece, face_axis + 1)
            targets = (
                slice(None),
                target_range(shift_now[0]),
                target_range(shift_now[1]),
                target_range(shift_now[2]),
            )
            padded = padded.at[targets].set(piece)
    return padded


def window_at(padded, start_x, start_y, start_z):
    channels = padded.shape[-1]
    piece = padded[:, start_x : start_x + 8, start_y : start_y + 8, start_z : start_z + 8, :]
    return piece.reshape(-1, channels)


def windows(padded, flipped):
    columns = []
    for i in range(3):
        for j in range(3):
            for l in range(3):
                if flipped:
                    columns.append(window_at(padded, 2 - i, 2 - j, 2 - l))
                else:
                    columns.append(window_at(padded, i, j, l))
    return jnp.concatenate(columns, axis=1)


def body(features, grad_out, weight, neighbours):
    brick_in = features[0]
    brick_cot = grad_out[0]
    link_rows = neighbours[0]
    slot_count = brick_in.shape[0]
    voxels = brick_in.shape[1]
    channels = brick_in.shape[-1]
    tap_count = weight.shape[0]
    space_count = lax.axis_size("space")
    reach_now = min(reach_limit, space_count - 1)
    listed_x = []
    listed_y = []
    for offset_dev in range(-reach_now, reach_now + 1):
        if offset_dev == 0:
            listed_x.append(brick_in)
            listed_y.append(brick_cot)
        else:
            received = shifted((brick_in, brick_cot), "space", -offset_dev)
            listed_x.append(received[0])
            listed_y.append(received[1])
    band_x = jnp.stack(listed_x, axis=0)
    band_y = jnp.stack(listed_y, axis=0)
    high_x = faces_of(band_x[: reach_now + 1].reshape(-1, voxels, channels), 7)
    high_y = faces_of(band_y[: reach_now + 1].reshape(-1, voxels, channels), 7)
    low_x = faces_of(band_x[reach_now:].reshape(-1, voxels, channels), 0)
    low_y = faces_of(band_y[reach_now:].reshape(-1, voxels, channels), 0)
    own_index = lax.axis_index("space")
    is_live = link_rows >= 0
    owner_dev = link_rows // slot_count
    slot_within = link_rows % slot_count
    band_limit = (reach_now + 1) * slot_count - 1
    pos_high = jnp.clip(
        (owner_dev - own_index + reach_now) * slot_count + slot_within, 0, band_limit
    )
    pos_high = jnp.where(is_live, pos_high, 0)
    pos_low = jnp.clip((owner_dev - own_index) * slot_count + slot_within, 0, band_limit)
    pos_low = jnp.where(is_live, pos_low, 0)
    padded_in = build_padded(brick_in, high_x, low_x, pos_high, pos_low, is_live)
    padded_cot = build_padded(brick_cot, high_y, low_y, pos_high, pos_low, is_live)
    stack_x = windows(padded_in, False)
    stacked_w = weight.reshape(tap_count * channels, channels)
    flipped_w = jnp.transpose(weight, (0, 2, 1)).reshape(tap_count * channels, channels)
    conv_sum = jnp.dot(stack_x, stacked_w, preferred_element_type=jnp.float32)
    grad_sum = jnp.dot(windows(padded_cot, True), flipped_w, preferred_element_type=jnp.float32)
    conv_out = conv_sum.astype(jnp.bfloat16).reshape(brick_in.shape)
    grad_in = grad_sum.astype(jnp.bfloat16).reshape(brick_in.shape)
    own_cot = brick_cot.reshape(-1, channels)
    scene_count = lax.axis_size("dp")
    grad_scale = 1.0 / math.sqrt(scene_count * slot_count * space_count * voxels)
    row_count = tap_count * channels // scene_count
    term_full = jnp.dot(stack_x.T, own_cot, preferred_element_type=jnp.float32) * grad_scale
    summed = lax.psum(term_full, ("space", "dp"))
    grad_weight = lax.dynamic_slice_in_dim(summed, lax.axis_index("dp") * row_count, row_count, 0)
    return (conv_out[None], grad_in[None], grad_weight)


def solution(mesh):
    placed = (
        P("dp", "space", None, None),
        P("dp", "space", None, None),
        P(),
        P("dp", "space", None),
    )
    return jax.shard_map(
        body,
        mesh=mesh,
        in_specs=placed,
        out_specs=(P("dp", "space", None, None), P("dp", "space", None, None), P("dp", None)),
        check_vma=False,
    )
```

profile of v0, /device:TPU:1, one launch (start us, length us, event | category | flops | bytes accessed | tf_op | source)
XLA Modules:
  0.0 558.8 jit_solution(15700183369990992389)
XLA Ops:
  7.2 4.7 collective-permute-start
  12.0 4.4 collective-permute-start.1
  16.4 3.4 collective-permute-start.2
  19.8 4.4 collective-permute-start.3
  24.2 3.7 collective-permute-start.4
  64.2 5.7 %copy.64 = bf16[27,256,256]{1,2,0:T(8,128)(2,1)} copy(bf16[27,256,256]{2,1,0:T(8,128)(2,1)} %param.114) | data formatting | bytes 7077888 | tf_op args[2]
  86.0 2.5 collective-permute-start.5
  88.6 2.8 collective-permute-start.6
  93.0 3.3 collective-permute-start.15
  96.3 2.2 collective-permute-start.16
  100.6 6.6 %collective-permute-start.18 = (bf16[1,512,256]{2,1,0:T(8,128)(2,1)S(1)}, bf16[1,512,256]{2,1,0:T(8,128)(2,1)S(1)}, u32[]{:S(2)}, u32[]{:S(2)}) collective-permute-start(bf16[1,512,256]{2,1,0:T(8,128)(2,1)S(1)} %bitcast.510), channel_id=1, source_target_pairs={{0,24},{8,32},{16,40},{24,48},{32,56},{40,64},{48,72},{56,80},{64,... | collective-permute-start | bytes 786440 | tf_op jit(solution)/shard_map/ppermute | solution.py:14
  108.7 18.3 %collective-permute-done.14 = bf16[1,512,256]{2,1,0:T(8,128)(2,1)S(1)} collective-permute-done((bf16[1,512,256]{2,1,0:T(8,128)(2,1)S(1)}, bf16[1,512,256]{2,1,0:T(8,128)(2,1)S(1)}, u32[]{:S(2)}, u32[]{:S(2)}) %collective-permute-start.14) | collective-permute-done | bytes 262176 | tf_op jit(solution)/shard_map/ppermute | solution.py:14
  130.4 2.4 collective-permute-start.7
  140.2 2.9 collective-permute-done.8
  144.4 4.6 collective-permute-start.21
  151.1 6.9 %collective-permute-done.11 = bf16[1,512,256]{2,1,0:T(8,128)(2,1)S(1)} collective-permute-done((bf16[1,512,256]{2,1,0:T(8,128)(2,1)S(1)}, bf16[1,512,256]{2,1,0:T(8,128)(2,1)S(1)}, u32[]{:S(2)}, u32[]{:S(2)}) %collective-permute-start.11) | collective-permute-done | bytes 262176 | tf_op jit(solution)/shard_map/ppermute | solution.py:14
  160.6 8.8 %collective-permute-done.13 = bf16[1,512,256]{2,1,0:T(8,128)(2,1)S(1)} collective-permute-done((bf16[1,512,256]{2,1,0:T(8,128)(2,1)S(1)}, bf16[1,512,256]{2,1,0:T(8,128)(2,1)S(1)}, u32[]{:S(2)}, u32[]{:S(2)}) %collective-permute-start.13) | collective-permute-done | bytes 262176 | tf_op jit(solution)/shard_map/ppermute | solution.py:14
  174.6 2.4 collective-permute-done.24
  177.1 9.0 %collective-permute-done.25 = bf16[1,512,256]{2,1,0:T(8,128)(2,1)S(1)} collective-permute-done((bf16[1,512,256]{2,1,0:T(8,128)(2,1)S(1)}, bf16[1,512,256]{2,1,0:T(8,128)(2,1)S(1)}, u32[]{:S(2)}, u32[]{:S(2)}) %collective-permute-start.25) | collective-permute-done | bytes 262176 | tf_op jit(solution)/shard_map/ppermute | solution.py:14
  186.1 24.0 %collective-permute-done.26 = bf16[1,512,256]{2,1,0:T(8,128)(2,1)S(1)} collective-permute-done((bf16[1,512,256]{2,1,0:T(8,128)(2,1)S(1)}, bf16[1,512,256]{2,1,0:T(8,128)(2,1)S(1)}, u32[]{:S(2)}, u32[]{:S(2)}) %collective-permute-start.26) | collective-permute-done | bytes 262176 | tf_op jit(solution)/shard_map/ppermute | solution.py:14
  212.6 3.1 select_bitcast_fusion.21
  216.0 3.2 select_bitcast_fusion.17
  219.3 5.7 %select_bitcast_fusion.2 = (bf16[1,8,8,256]{3,2,1,0:T(8,128)(2,1)S(1)}, bf16[1,8,8,256]{3,2,1,0:T(8,128)(2,1)S(1)}, bf16[1,8,8,256]{3,2,1,0:T(8,128)(2,1)S(1)}, ...) fusion(bf16[8,3,64,256]{3,2,0,1:T(8,128)(2,1)S(1)} %pad_maximum, ...), kind=kLoop, calls=%fused_computation.112 | loop fusion | flops 147456 | bytes 589869 | tf_op jit(solution)/shard_map/jit(_where)/select_n | solution.py:65
  225.1 5.7 %select_bitcast_fusion = (bf16[1,8,8,256]{3,2,1,0:T(8,128)(2,1)S(1)}, bf16[1,8,8,256]{3,2,1,0:T(8,128)(2,1)S(1)}, bf16[1,8,8,256]{3,2,1,0:T(8,128)(2,1)S(1)}, bf...) fusion(bf16[8,3,64,256]{3,2,0,1:T(8,128)(2,1)S(1)} %pad_maximum, ...), kind=kLoop, calls=%fused_computation.110 | loop fusion | flops 147456 | bytes 589869 | tf_op jit(solution)/shard_map/jit(_where)/select_n | solution.py:65
  236.6 2.3 fusion.3
  238.9 5.7 %select_bitcast_fusion.26 = (bf16[1,8,8,256]{3,2,1,0:T(8,128)(2,1)S(1)}, bf16[1,8,8,256]{3,2,1,0:T(8,128)(2,1)S(1)}, bf16[1,8,8,256]{3,2,1,0:T(8,128)(2,1)S(1)},...) fusion(bf16[8,3,64,256]{3,2,0,1:T(8,128)(2,1)S(1)} %pad_maximum, ...), kind=kLoop, calls=%fused_computation.136 | loop fusion | flops 147456 | bytes 589869 | tf_op jit(solution)/shard_map/jit(_where)/select_n | solution.py:65
  244.6 5.7 %select_bitcast_fusion.28 = (bf16[1,8,8,256]{3,2,1,0:T(8,128)(2,1)S(1)}, bf16[1,8,8,256]{3,2,1,0:T(8,128)(2,1)S(1)}, bf16[1,8,8,256]{3,2,1,0:T(8,128)(2,1)S(1)},...) fusion(bf16[8,3,64,256]{3,2,0,1:T(8,128)(2,1)S(1)} %pad_maximum, ...), kind=kLoop, calls=%fused_computation.138 | loop fusion | flops 147456 | bytes 589869 | tf_op jit(solution)/shard_map/jit(_where)/select_n | solution.py:65
  260.7 2.9 copy-done.18
  263.6 5.0 convolution_multiply_fusion
  300.0 5.9 %fusion = bf16[1,1,512,256]{3,2,1,0:T(8,128)(2,1)} fusion(bf16[512,6912]{1,0:T(8,128)(2,1)} %copy-done.18, bf16[6912,256]{1,0:T(8,128)(2,1)S(1)} %bitcast.403), kind=kOutput, calls=%fused_computation.3 | convolution fusion | flops 1812070400 | bytes 10878976 | tf_op jit(solution)/shard_map/dot_general | solution.py:140
  305.9 2.7 fusion.1
  308.6 241.2 %all-reduce.4.cloned.1.call-done = f32[6912,256]{1,0:T(8,128)} async-done(((f32[6912,256]{1,0:T(8,128)}), f32[6912,256]{1,0:T(8,128)}) %all-reduce.4.cloned.1.call-update) | async-done | bytes 7077904 | tf_op jit(solution)/shard_map/psum | solution.py:149
  (284 shorter events, 82.7 us)
Async XLA Ops:
  7.2 78.8 %copy-start.14 = (bf16[1,1,512,256]{3,2,1,0:T(8,128)(2,1)S(1)}, bf16[1,1,512,256]{3,2,1,0:T(8,128)(2,1)}, u32[]{:S(2)}) copy-start(bf16[1,1,512,256]{3,2,1,0:T(8,128)(2,1)} %param.112) | copy-start | bytes 786436
  7.2 84.2 %copy-start.15 = (bf16[1,1,512,256]{3,2,1,0:T(8,128)(2,1)S(1)}, bf16[1,1,512,256]{3,2,1,0:T(8,128)(2,1)}, u32[]{:S(2)}) copy-start(bf16[1,1,512,256]{3,2,1,0:T(8,128)(2,1)} %param.113) | copy-start | bytes 786436
  7.2 542.6 %all-reduce.4.cloned.1.call-start = ((), (), s32[]{:S(2)}) async-start(), calls=%async_computation | async-start | bytes 14155776 | tf_op jit(solution)/shard_map/psum | solution.py:149
  7.2 78.8 %collective-permute-start = (bf16[1,512,256]{2,1,0:T(8,128)(2,1)}, bf16[1,512,256]{2,1,0:T(8,128)(2,1)S(1)}, u32[]{:S(2)}, u32[]{:S(2)}) collective-permute-start(bf16[1,512,256]{2,1,0:T(8,128)(2,1)} %bitcast.491), channel_id=1, source_target_pairs={{0,56},{8,64},{16,72},{24,80},{32,88},{40,96},{48,104},{56,112},{6... | collective-permute-start | bytes 786440 | tf_op jit(solution)/shard_map/ppermute | solution.py:14
  12.0 76.6 %collective-permute-start.1 = (bf16[1,512,256]{2,1,0:T(8,128)(2,1)}, bf16[1,512,256]{2,1,0:T(8,128)(2,1)S(1)}, u32[]{:S(2)}, u32[]{:S(2)}) collective-permute-start(bf16[1,512,256]{2,1,0:T(8,128)(2,1)} %bitcast.492), channel_id=1, source_target_pairs={{0,48},{8,56},{16,64},{24,72},{32,80},{40,88},{48,96},{56,104},{64... | collective-permute-start | bytes 786440 | tf_op jit(solution)/shard_map/ppermute | solution.py:14
  16.4 75.0 %collective-permute-start.2 = (bf16[1,512,256]{2,1,0:T(8,128)(2,1)}, bf16[1,512,256]{2,1,0:T(8,128)(2,1)S(1)}, u32[]{:S(2)}, u32[]{:S(2)}) collective-permute-start(bf16[1,512,256]{2,1,0:T(8,128)(2,1)} %bitcast.493), channel_id=1, source_target_pairs={{0,40},{8,48},{16,56},{24,64},{32,72},{40,80},{48,88},{56,96},{64,... | collective-permute-start | bytes 786440 | tf_op jit(solution)/shard_map/ppermute | solution.py:14
  19.8 73.1 %collective-permute-start.3 = (bf16[1,512,256]{2,1,0:T(8,128)(2,1)}, bf16[1,512,256]{2,1,0:T(8,128)(2,1)S(1)}, u32[]{:S(2)}, u32[]{:S(2)}) collective-permute-start(bf16[1,512,256]{2,1,0:T(8,128)(2,1)} %bitcast.494), channel_id=1, source_target_pairs={{0,32},{8,40},{16,48},{24,56},{32,64},{40,72},{48,80},{56,88},{64,... | collective-permute-start | bytes 786440 | tf_op jit(solution)/shard_map/ppermute | solution.py:14
  24.2 72.1 %collective-permute-start.4 = (bf16[1,512,256]{2,1,0:T(8,128)(2,1)}, bf16[1,512,256]{2,1,0:T(8,128)(2,1)S(1)}, u32[]{:S(2)}, u32[]{:S(2)}) collective-permute-start(bf16[1,512,256]{2,1,0:T(8,128)(2,1)} %bitcast.495), channel_id=1, source_target_pairs={{0,24},{8,32},{16,40},{24,48},{32,56},{40,64},{48,72},{56,80},{64,... | collective-permute-start | bytes 786440 | tf_op jit(solution)/shard_map/ppermute | solution.py:14
  86.0 12.5 %collective-permute-start.5 = (bf16[1,512,256]{2,1,0:T(8,128)(2,1)S(1)}, bf16[1,512,256]{2,1,0:T(8,128)(2,1)S(1)}, u32[]{:S(2)}, u32[]{:S(2)}) collective-permute-start(bf16[1,512,256]{2,1,0:T(8,128)(2,1)S(1)} %bitcast.496), channel_id=1, source_target_pairs={{0,16},{8,24},{16,32},{24,40},{32,48},{40,56},{48,64},{56,72},{64,... | collective-permute-start | bytes 786440 | tf_op jit(solution)/shard_map/ppermute | solution.py:14
  88.6 12.0 %collective-permute-start.6 = (bf16[1,512,256]{2,1,0:T(8,128)(2,1)S(1)}, bf16[1,512,256]{2,1,0:T(8,128)(2,1)S(1)}, u32[]{:S(2)}, u32[]{:S(2)}) collective-permute-start(bf16[1,512,256]{2,1,0:T(8,128)(2,1)S(1)} %bitcast.497), channel_id=1, source_target_pairs={{0,8},{8,16},{16,24},{24,32},{32,40},{40,48},{48,56},{56,64},{64,7... | collective-permute-start | bytes 786440 | tf_op jit(solution)/shard_map/ppermute | solution.py:14
  91.4 35.7 %collective-permute-start.14 = (bf16[1,512,256]{2,1,0:T(8,128)(2,1)S(1)}, bf16[1,512,256]{2,1,0:T(8,128)(2,1)S(1)}, u32[]{:S(2)}, u32[]{:S(2)}) collective-permute-start(bf16[1,512,256]{2,1,0:T(8,128)(2,1)S(1)} %bitcast.506), channel_id=1, source_target_pairs={{0,56},{8,64},{16,72},{24,80},{32,88},{40,96},{48,104},{56,112},{6... | collective-permute-start | bytes 786440 | tf_op jit(solution)/shard_map/ppermute | solution.py:14
  93.0 35.4 %collective-permute-start.15 = (bf16[1,512,256]{2,1,0:T(8,128)(2,1)S(1)}, bf16[1,512,256]{2,1,0:T(8,128)(2,1)S(1)}, u32[]{:S(2)}, u32[]{:S(2)}) collective-permute-start(bf16[1,512,256]{2,1,0:T(8,128)(2,1)S(1)} %bitcast.507), channel_id=1, source_target_pairs={{0,48},{8,56},{16,64},{24,72},{32,80},{40,88},{48,96},{56,104},{64... | collective-permute-start | bytes 786440 | tf_op jit(solution)/shard_map/ppermute | solution.py:14
  96.3 34.1 %collective-permute-start.16 = (bf16[1,512,256]{2,1,0:T(8,128)(2,1)S(1)}, bf16[1,512,256]{2,1,0:T(8,128)(2,1)S(1)}, u32[]{:S(2)}, u32[]{:S(2)}) collective-permute-start(bf16[1,512,256]{2,1,0:T(8,128)(2,1)S(1)} %bitcast.508), channel_id=1, source_target_pairs={{0,40},{8,48},{16,56},{24,64},{32,72},{40,80},{48,88},{56,96},{64,... | collective-permute-start | bytes 786440 | tf_op jit(solution)/shard_map/ppermute | solution.py:14
  98.5 34.3 %collective-permute-start.17 = (bf16[1,512,256]{2,1,0:T(8,128)(2,1)S(1)}, bf16[1,512,256]{2,1,0:T(8,128)(2,1)S(1)}, u32[]{:S(2)}, u32[]{:S(2)}) collective-permute-start(bf16[1,512,256]{2,1,0:T(8,128)(2,1)S(1)} %bitcast.509), channel_id=1, source_target_pairs={{0,32},{8,40},{16,48},{24,56},{32,64},{40,72},{48,80},{56,88},{64,... | collective-permute-start | bytes 786440 | tf_op jit(solution)/shard_map/ppermute | solution.py:14
  100.6 33.5 %collective-permute-start.18 = (bf16[1,512,256]{2,1,0:T(8,128)(2,1)S(1)}, bf16[1,512,256]{2,1,0:T(8,128)(2,1)S(1)}, u32[]{:S(2)}, u32[]{:S(2)}) collective-permute-start(bf16[1,512,256]{2,1,0:T(8,128)(2,1)S(1)} %bitcast.510), channel_id=1, source_target_pairs={{0,24},{8,32},{16,40},{24,48},{32,56},{40,64},{48,72},{56,80},{64,... | collective-permute-start | bytes 786440 | tf_op jit(solution)/shard_map/ppermute | solution.py:14
  127.1 8.4 %collective-permute-start.19 = (bf16[1,512,256]{2,1,0:T(8,128)(2,1)S(1)}, bf16[1,512,256]{2,1,0:T(8,128)(2,1)S(1)}, u32[]{:S(2)}, u32[]{:S(2)}) collective-permute-start(bf16[1,512,256]{2,1,0:T(8,128)(2,1)S(1)} %bitcast.511), channel_id=1, source_target_pairs={{0,16},{8,24},{16,32},{24,40},{32,48},{40,56},{48,64},{56,72},{64,... | collective-permute-start | bytes 786440 | tf_op jit(solution)/shard_map/ppermute | solution.py:14
  128.4 8.4 %collective-permute-start.20 = (bf16[1,512,256]{2,1,0:T(8,128)(2,1)S(1)}, bf16[1,512,256]{2,1,0:T(8,128)(2,1)S(1)}, u32[]{:S(2)}, u32[]{:S(2)}) collective-permute-start(bf16[1,512,256]{2,1,0:T(8,128)(2,1)S(1)} %bitcast.512), channel_id=1, source_target_pairs={{0,8},{8,16},{16,24},{24,32},{32,40},{40,48},{48,56},{56,64},{64,7... | collective-permute-start | bytes 786440 | tf_op jit(solution)/shard_map/ppermute | solution.py:14
  130.4 8.5 %collective-permute-start.7 = (bf16[1,512,256]{2,1,0:T(8,128)(2,1)S(1)}, bf16[1,512,256]{2,1,0:T(8,128)(2,1)S(1)}, u32[]{:S(2)}, u32[]{:S(2)}) collective-permute-start(bf16[1,512,256]{2,1,0:T(8,128)(2,1)S(1)} %bitcast.499), channel_id=1, source_target_pairs={{8,0},{16,8},{24,16},{32,24},{40,32},{48,40},{56,48},{64,56},{72,6... | collective-permute-start | bytes 786440 | tf_op jit(solution)/shard_map/ppermute | solution.py:14
  132.8 10.3 %collective-permute-start.8 = (bf16[1,512,256]{2,1,0:T(8,128)(2,1)S(1)}, bf16[1,512,256]{2,1,0:T(8,128)(2,1)S(1)}, u32[]{:S(2)}, u32[]{:S(2)}) collective-permute-start(bf16[1,512,256]{2,1,0:T(8,128)(2,1)S(1)} %bitcast.500), channel_id=1, source_target_pairs={{16,0},{24,8},{32,16},{40,24},{48,32},{56,40},{64,48},{72,56},{80,... | collective-permute-start | bytes 786440 | tf_op jit(solution)/shard_map/ppermute | solution.py:14
  134.2 10.3 %collective-permute-start.9 = (bf16[1,512,256]{2,1,0:T(8,128)(2,1)S(1)}, bf16[1,512,256]{2,1,0:T(8,128)(2,1)S(1)}, u32[]{:S(2)}, u32[]{:S(2)}) collective-permute-start(bf16[1,512,256]{2,1,0:T(8,128)(2,1)S(1)} %bitcast.501), channel_id=1, source_target_pairs={{24,0},{32,8},{40,16},{48,24},{56,32},{64,40},{72,48},{80,56},{88,... | collective-permute-start | bytes 786440 | tf_op jit(solution)/shard_map/ppermute | solution.py:14
  135.5 14.2 %collective-permute-start.10 = (bf16[1,512,256]{2,1,0:T(8,128)(2,1)S(1)}, bf16[1,512,256]{2,1,0:T(8,128)(2,1)S(1)}, u32[]{:S(2)}, u32[]{:S(2)}) collective-permute-start(bf16[1,512,256]{2,1,0:T(8,128)(2,1)S(1)} %bitcast.502), channel_id=1, source_target_pairs={{32,0},{40,8},{48,16},{56,24},{64,32},{72,40},{80,48},{88,56},{96,... | collective-permute-start | bytes 786440 | tf_op jit(solution)/shard_map/ppermute | solution.py:14
  136.8 21.1 %collective-permute-start.11 = (bf16[1,512,256]{2,1,0:T(8,128)(2,1)S(1)}, bf16[1,512,256]{2,1,0:T(8,128)(2,1)S(1)}, u32[]{:S(2)}, u32[]{:S(2)}) collective-permute-start(bf16[1,512,256]{2,1,0:T(8,128)(2,1)S(1)} %bitcast.503), channel_id=1, source_target_pairs={{40,0},{48,8},{56,16},{64,24},{72,32},{80,40},{88,48},{96,56},{104... | collective-permute-start | bytes 786440 | tf_op jit(solution)/shard_map/ppermute | solution.py:14
  138.9 20.4 %collective-permute-start.12 = (bf16[1,512,256]{2,1,0:T(8,128)(2,1)S(1)}, bf16[1,512,256]{2,1,0:T(8,128)(2,1)S(1)}, u32[]{:S(2)}, u32[]{:S(2)}) collective-permute-start(bf16[1,512,256]{2,1,0:T(8,128)(2,1)S(1)} %bitcast.504), channel_id=1, source_target_pairs={{48,0},{56,8},{64,16},{72,24},{80,32},{88,40},{96,48},{104,56},{11... | collective-permute-start | bytes 786440 | tf_op jit(solution)/shard_map/ppermute | solution.py:14
  143.1 26.3 %collective-permute-start.13 = (bf16[1,512,256]{2,1,0:T(8,128)(2,1)S(1)}, bf16[1,512,256]{2,1,0:T(8,128)(2,1)S(1)}, u32[]{:S(2)}, u32[]{:S(2)}) collective-permute-start(bf16[1,512,256]{2,1,0:T(8,128)(2,1)S(1)} %bitcast.505), channel_id=1, source_target_pairs={{56,0},{64,8},{72,16},{80,24},{88,32},{96,40},{104,48},{112,56},{1... | collective-permute-start | bytes 786440 | tf_op jit(solution)/shard_map/ppermute | solution.py:14
  144.4 27.0 %collective-permute-start.21 = (bf16[1,512,256]{2,1,0:T(8,128)(2,1)S(1)}, bf16[1,512,256]{2,1,0:T(8,128)(2,1)S(1)}, u32[]{:S(2)}, u32[]{:S(2)}) collective-permute-start(bf16[1,512,256]{2,1,0:T(8,128)(2,1)S(1)} %bitcast.513), channel_id=1, source_target_pairs={{8,0},{16,8},{24,16},{32,24},{40,32},{48,40},{56,48},{64,56},{72,6... | collective-permute-start | bytes 786440 | tf_op jit(solution)/shard_map/ppermute | solution.py:14
  149.8 23.1 %collective-permute-start.22 = (bf16[1,512,256]{2,1,0:T(8,128)(2,1)S(1)}, bf16[1,512,256]{2,1,0:T(8,128)(2,1)S(1)}, u32[]{:S(2)}, u32[]{:S(2)}) collective-permute-start(bf16[1,512,256]{2,1,0:T(8,128)(2,1)S(1)} %bitcast.514), channel_id=1, source_target_pairs={{16,0},{24,8},{32,16},{40,24},{48,32},{56,40},{64,48},{72,56},{80,... | collective-permute-start | bytes 786440 | tf_op jit(solution)/shard_map/ppermute | solution.py:14
  158.0 16.6 %collective-permute-start.23 = (bf16[1,512,256]{2,1,0:T(8,128)(2,1)S(1)}, bf16[1,512,256]{2,1,0:T(8,128)(2,1)S(1)}, u32[]{:S(2)}, u32[]{:S(2)}) collective-permute-start(bf16[1,512,256]{2,1,0:T(8,128)(2,1)S(1)} %bitcast.515), channel_id=1, source_target_pairs={{24,0},{32,8},{40,16},{48,24},{56,32},{64,40},{72,48},{80,56},{88,... | collective-permute-start | bytes 786440 | tf_op jit(solution)/shard_map/ppermute | solution.py:14
  159.3 17.7 %collective-permute-start.24 = (bf16[1,512,256]{2,1,0:T(8,128)(2,1)S(1)}, bf16[1,512,256]{2,1,0:T(8,128)(2,1)S(1)}, u32[]{:S(2)}, u32[]{:S(2)}) collective-permute-start(bf16[1,512,256]{2,1,0:T(8,128)(2,1)S(1)} %bitcast.516), channel_id=1, source_target_pairs={{32,0},{40,8},{48,16},{56,24},{64,32},{72,40},{80,48},{88,56},{96,... | collective-permute-start | bytes 786440 | tf_op jit(solution)/shard_map/ppermute | solution.py:14
  169.4 16.7 %collective-permute-start.25 = (bf16[1,512,256]{2,1,0:T(8,128)(2,1)S(1)}, bf16[1,512,256]{2,1,0:T(8,128)(2,1)S(1)}, u32[]{:S(2)}, u32[]{:S(2)}) collective-permute-start(bf16[1,512,256]{2,1,0:T(8,128)(2,1)S(1)} %bitcast.517), channel_id=1, source_target_pairs={{40,0},{48,8},{56,16},{64,24},{72,32},{80,40},{88,48},{96,56},{104... | collective-permute-start | bytes 786440 | tf_op jit(solution)/shard_map/ppermute | solution.py:14
  171.5 38.7 %collective-permute-start.26 = (bf16[1,512,256]{2,1,0:T(8,128)(2,1)S(1)}, bf16[1,512,256]{2,1,0:T(8,128)(2,1)S(1)}, u32[]{:S(2)}, u32[]{:S(2)}) collective-permute-start(bf16[1,512,256]{2,1,0:T(8,128)(2,1)S(1)} %bitcast.519), channel_id=1, source_target_pairs={{48,0},{56,8},{64,16},{72,24},{80,32},{88,40},{96,48},{104,56},{11... | collective-permute-start | bytes 786440 | tf_op jit(solution)/shard_map/ppermute | solution.py:14
  172.8 39.0 %collective-permute-start.27 = (bf16[1,512,256]{2,1,0:T(8,128)(2,1)S(1)}, bf16[1,512,256]{2,1,0:T(8,128)(2,1)S(1)}, u32[]{:S(2)}, u32[]{:S(2)}) collective-permute-start(bf16[1,512,256]{2,1,0:T(8,128)(2,1)S(1)} %bitcast.520), channel_id=1, source_target_pairs={{56,0},{64,8},{72,16},{80,24},{88,32},{96,40},{104,48},{112,56},{1... | collective-permute-start | bytes 786440 | tf_op jit(solution)/shard_map/ppermute | solution.py:14
  268.7 31.3 %copy-start = (bf16[27,256,256]{2,1,0:T(8,128)(2,1)S(1)}, bf16[27,256,256]{2,1,0:T(8,128)(2,1)}, u32[]{:S(2)}) copy-start(bf16[27,256,256]{2,1,0:T(8,128)(2,1)} %param.114) | copy-start | bytes 10616836
  (16 other events, 280.2 us)
Sparse Core Ops, SparseCore 0:
  268.8 280.9 all-reduce.3
where the time goes:
time: 562 us; the launch traced here: 559 us
  waiting for transfers between devices  315 us (56%)
  starting transfers between devices  67.3 us (12%)
  local copies, waits for them, and re-layouts  65.7 us (12%)
  between operations  63.8 us (11%)
  other arithmetic  33 us (6%)
  matrix products  13.6 us (2%)
    psum x1, waiting for transfers between devices, body(): summed = lax.psum(term_full, ('space', 'dp'))  241 us
    ppermute x28, waiting for transfers between devices, shifted(): return lax.ppermute(shard, axis, pairs)  74.1 us
    ppermute x28, starting transfers between devices, shifted(): return lax.ppermute(shard, axis, pairs)  67.3 us
    unnamed x121, local copies, waits for them, and re-layouts  41.1 us
    select_n x6, other arithmetic, build_padded(): face = jnp.where(live[:, k][:, None, None], face, zero_value)  29.1 us
  transfers between devices with their start and end apart: 29, of which 11 were waited for; matrix products, arithmetic and copies ran while one was open for 10% of the time, Pallas kernels for 0%

commit v1 on v0

v1 whole, which is shorter than its diff:
```python
import functools
import math

import jax
import jax.numpy as jnp
from jax import lax
from jax.experimental import pallas as pl
from jax.experimental.pallas import tpu as pltpu
from jax.sharding import PartitionSpec as P

f32 = jnp.float32
bf16 = jnp.bfloat16
i16 = jnp.int16
i32 = jnp.int32

SPACE = 32
SCENES = 8
CHIPS = 16
HALF = 128
LEVELS = 32766.0
VMEM_LIMIT = 56 * 1024 * 1024

OFFSETS = [(k, k // 9 - 1, k // 3 % 3 - 1, k % 3 - 1) for k in range(27) if k != 13]


def vmem():
    return pl.BlockSpec(memory_space=pltpu.VMEM)


def smem():
    return pl.BlockSpec(memory_space=pltpu.SMEM)


def hbm():
    return pl.BlockSpec(memory_space=pl.ANY)


def side(shift):
    return 7 if shift > 0 else 0


def region(ref, shifts):
    dx, dy, dz = shifts
    kinds = (dx != 0, dy != 0, dz != 0)
    if kinds == (True, False, False):
        return ref[pl.ds(side(dx) * 64, 64), :]
    if kinds == (False, True, False):
        return jnp.concatenate([ref[pl.ds(x * 64 + side(dy) * 8, 8), :] for x in range(8)], axis=0)
    if kinds == (False, False, True):
        return ref[pl.ds(side(dz), 64, stride=8), :]
    if kinds == (True, True, False):
        rows = ref[pl.ds(side(dx) * 64 + side(dy) * 8, 8), :]
    elif kinds == (True, False, True):
        rows = ref[pl.ds(side(dx) * 64 + side(dz), 8, stride=8), :]
    elif kinds == (False, True, True):
        rows = ref[pl.ds(side(dy) * 8 + side(dz), 8, stride=64), :]
    else:
        row = ref[pl.ds(side(dx) * 64 + side(dy) * 8 + side(dz), 1), :]
        rows = jnp.broadcast_to(row, (8, HALF))
    return jnp.concatenate([rows, rows], axis=0)


def pack_kernel(own_ref, links_ref, x_ref, c_ref, out_ref, pair_ref, parts):
    core = lax.rem(own_ref[0], 2)
    for half in range(2):
        lanes = pl.ds(half * HALF, HALF)
        parts[2 * half] = x_ref[:, lanes].astype(f32)
        parts[2 * half + 1] = c_ref[:, lanes].astype(f32)
    pair_ref[:, 0:256] = x_ref[...]

    @pl.when(core == 0)
    def _():
        pair_ref[:, 256:384] = c_ref[:, 128:256]

    @pl.when(core == 1)
    def _():
        pair_ref[:, 256:384] = c_ref[:, 0:128]

    for k, *shifts in OFFSETS:
        target = links_ref[k]

        @pl.when(target >= 0)
        def _(target=target, shifts=tuple(shifts)):
            chip = target // 2
            brick = lax.rem(target, 2)
            for half in range(2):
                for tensor in range(2):
                    rows = region(parts.at[2 * half + tensor], shifts)
                    count = rows.shape[0]
                    out_ref[2 * chip + half, brick, 0:count, tensor * HALF : (tensor + 1) * HALF] = rows.astype(bf16)


def pack(own, links, x, c):
    return pl.pallas_call(
        pack_kernel,
        out_shape=(
            jax.ShapeDtypeStruct((SPACE, 2, 64, 256), bf16),
            jax.ShapeDtypeStruct((512, 384), bf16),
        ),
        in_specs=[smem(), smem(), vmem(), vmem()],
        out_specs=(vmem(), vmem()),
        scratch_shapes=[pltpu.VMEM((4, 512, HALF), f32)],
        compiler_params=pltpu.CompilerParams(vmem_limit_bytes=VMEM_LIMIT),
    )(own, links, x, c)


def target_plane(shift):
    return 9 if shift > 0 else 0


def quantise(values, peak):
    code = jnp.ceil(jnp.log2(jnp.maximum(peak, 2.0**-110)) * 256.0) + 1.0
    factor = LEVELS * jnp.exp2(code * (-1.0 / 256.0))
    return jnp.round(values * factor).astype(i32).astype(i16), code


def code_rows(code):
    return jnp.broadcast_to(code, (16, HALF)).astype(i32).astype(i16)


def step_of(code_row):
    return jnp.exp2(code_row * (1.0 / 256.0)) * (1.0 / LEVELS)


def fill(brick, links_ref, halo_ref, tensor, own_rows, plane, low, high, shifted_low, shifted_high, padded):
    lanes = slice(tensor * HALF, (tensor + 1) * HALF)
    plane[...] = jnp.zeros_like(plane)
    low[...] = jnp.zeros_like(low)
    high[...] = jnp.zeros_like(high)
    for x in range(8):
        plane[pl.ds((x + 1) * 80 + 8, 64), :] = own_rows(x * 64)
    for k, dx, dy, dz in OFFSETS:
        source = links_ref[k]

        @pl.when(source >= 0)
        def _(source=source, dx=dx, dy=dy, dz=dz):
            at_x, at_y = target_plane(dx), target_plane(dy)
            face = (dx != 0) + (dy != 0) + (dz != 0) == 1
            got = halo_ref[source, brick, 0 : 64 if face else 16, lanes].astype(f32)
            if dz == 0:
                if dy == 0:
                    plane[pl.ds(at_x * 80 + 8, 64), :] = got
                elif dx == 0:
                    for x in range(8):
                        plane[pl.ds((x + 1) * 80 + at_y * 8, 8), :] = got[x * 8 : x * 8 + 8]
                else:
                    plane[pl.ds(at_x * 80 + at_y * 8, 8), :] = got[0:8]
            else:
                rim = low if dz < 0 else high
                if dx == 0 and dy == 0:
                    for x in range(8):
                        rim[pl.ds((x + 1) * 10 + 1, 8), :] = got[x * 8 : x * 8 + 8]
                elif dy == 0:
                    rim[pl.ds(at_x * 10 + 1, 8), :] = got[0:8]
                elif dx == 0:
                    rim[pl.ds(10 + at_y, 8, stride=10), :] = got[0:8]
                else:
                    rim[pl.ds(at_x * 10 + at_y, 1), :] = got[0:1]

    shifted_low[pl.ds(1, 800), :] = plane[pl.ds(0, 800), :]
    shifted_low[pl.ds(0, 104, stride=8), :] = low[...]
    shifted_high[pl.ds(0, 800), :] = plane[pl.ds(1, 800), :]
    shifted_high[pl.ds(7, 104, stride=8), :] = high[...]
    for j in range(3):
        for l, source in enumerate((shifted_low, plane, shifted_high)):
            at = (3 * j + l) * HALF
            for x in range(10):
                padded[tensor, brick, x * 64 : x * 64 + 64, at : at + HALF] = source[
                    pl.ds(x * 80 + j * 8, 64), :
                ].astype(bf16)


def main_kernel(
    own_ref, links_ref, mate_links_ref, x_ref, c_ref, pair_ref, halo_ref, weight_ref,
    sums_ref, terms_ref,
    plane, low, high, shifted_low, shifted_high, padded, x_turned, grads, w_in, w_out, sems,
):
    core = lax.rem(own_ref[0], 2)
    start = pl.multiple_of(core * HALF, HALF)
    copies = [
        pltpu.make_async_copy(weight_ref.at[:, pl.ds(start, HALF), :], w_in, sems.at[0])
    ]
    for kk in range(27):
        copies.append(
            pltpu.make_async_copy(
                weight_ref.at[26 - kk, :, pl.ds(start, HALF)],
                w_out.at[:, pl.ds(kk * HALF, HALF)],
                sems.at[1 + kk],
            )
        )
    for copy in copies:
        copy.start()

    def assemble(brick, links, rows_of):
        for tensor in range(2):
            fill(brick, links, halo_ref, tensor, rows_of[tensor], plane, low, high, shifted_low, shifted_high, padded)

    def own_rows(ref, at):
        def rows(first):
            return ref[pl.ds(first, 64), at : at + HALF].astype(f32)

        return rows

    for here in range(2):

        @pl.when(core == here)
        def _(here=here):
            at = here * HALF
            assemble(here, links_ref, (own_rows(x_ref, at), own_rows(c_ref, at)))
            assemble(1 - here, mate_links_ref, (own_rows(pair_ref, at), own_rows(pair_ref, 256)))
            x_turned[here] = x_ref[...].T
            x_turned[1 - here] = pair_ref[:, 0:256].T

    for i in range(3):
        window = slice(i * 64, i * 64 + 512)
        term = jnp.dot(x_turned[0], padded[1, 0, window, :], preferred_element_type=f32)
        term += jnp.dot(x_turned[1], padded[1, 1, window, :], preferred_element_type=f32)
        for jl in range(9):
            grads[26 - (9 * i + jl)] = term[:, jl * HALF : (jl + 1) * HALF]
    for q in range(CHIPS):
        rows = slice(q * 16, q * 16 + 16)
        peak = jnp.abs(grads[0, rows, :])
        for k in range(1, 27):
            peak = jnp.maximum(peak, jnp.abs(grads[k, rows, :]))
        peak = jnp.max(peak, axis=0, keepdims=True)
        coded, code = quantise(grads[:, rows, :].reshape(432, HALF), peak)
        terms_ref[q, 0:432, :] = coded
        terms_ref[q, 432:448, :] = code_rows(code)

    for copy in copies:
        copy.wait()
    for brick in range(2):
        for part in range(2):
            total = jnp.zeros((512, 256), f32)
            for i in range(3):
                block = padded[part, brick, i * 64 : i * 64 + 512, :]
                if part == 0:
                    taps = w_in[9 * i : 9 * i + 9].reshape(9 * HALF, 256)
                    total += jnp.dot(block, taps, preferred_element_type=f32)
                else:
                    taps = w_out[:, i * 9 * HALF : (i + 1) * 9 * HALF]
                    total += lax.dot_general(block, taps, (((1,), (1,)), ((), ())), preferred_element_type=f32)
            sums_ref[lax.rem(core + brick, 2), part] = total


def main(own, links, mate_links, x, c, pair, halo, weight):
    return pl.pallas_call(
        main_kernel,
        out_shape=(
            jax.ShapeDtypeStruct((2, 2, 512, 256), f32),
            jax.ShapeDtypeStruct((CHIPS, 448, HALF), i16),
        ),
        in_specs=[smem(), smem(), smem(), vmem(), vmem(), vmem(), vmem(), hbm()],
        out_specs=(vmem(), vmem()),
        scratch_shapes=[
            pltpu.VMEM((832, HALF), f32),
            pltpu.VMEM((104, HALF), f32),
            pltpu.VMEM((104, HALF), f32),
            pltpu.VMEM((832, HALF), f32),
            pltpu.VMEM((832, HALF), f32),
            pltpu.VMEM((2, 2, 640, 9 * HALF), bf16),
            pltpu.VMEM((2, 256, 512), bf16),
            pltpu.VMEM((27, 256, HALF), f32),
            pltpu.VMEM((27, HALF, 256), bf16),
            pltpu.VMEM((256, 27 * HALF), bf16),
            pltpu.SemaphoreType.DMA((28,)),
        ],
        compiler_params=pltpu.CompilerParams(vmem_limit_bytes=VMEM_LIMIT),
    )(own, links, mate_links, x, c, pair, halo, weight)


def scene_kernel(own_ref, got_ref, out_ref, total):
    chip = own_ref[0] // 2
    steps = [step_of(got_ref[source, 432:448, :].astype(i32).astype(f32)) for source in range(CHIPS)]
    for k in range(27):
        unit = jnp.zeros((16, HALF), f32)
        for source in range(CHIPS):
            unit += got_ref[source, k * 16 : k * 16 + 16, :].astype(i32).astype(f32) * steps[source]
        total[k] = unit
    total[27] = jnp.zeros((16, HALF), f32)
    for scene in range(SCENES):
        rest = lax.rem(chip - 6 * scene + 96, 16)
        first = (54 * scene + rest - chip) // 16
        units = [total[jnp.minimum(first + t, 27)] for t in range(4)]
        peak = jnp.abs(units[0])
        for unit in units[1:]:
            peak = jnp.maximum(peak, jnp.abs(unit))
        peak = jnp.max(peak, axis=0, keepdims=True)
        for t in range(4):
            coded, code = quantise(units[t], peak)
            out_ref[scene, t * 16 : t * 16 + 16, :] = coded
        out_ref[scene, 64:80, :] = code_rows(code)


def scene_sum(own, got):
    return pl.pallas_call(
        scene_kernel,
        out_shape=jax.ShapeDtypeStruct((SCENES, 80, HALF), i16),
        in_specs=[smem(), vmem()],
        out_specs=vmem(),
        scratch_shapes=[pltpu.VMEM((28, 16, HALF), f32)],
        compiler_params=pltpu.CompilerParams(vmem_limit_bytes=VMEM_LIMIT),
    )(own, got)


def whole_kernel(scale, got_ref, out_ref):
    total = jnp.zeros((64, HALF), f32)
    for scene in range(SCENES):
        step = step_of(got_ref[scene, 64:80, :].astype(i32).astype(f32))
        total += got_ref[scene, 0:64, :].astype(i32).astype(f32) * step[0:1]
    total *= scale
    peak = jnp.max(jnp.abs(total), axis=0, keepdims=True)
    coded, code = quantise(total, peak)
    codes = code_rows(code)
    for target in range(SPACE):
        out_ref[target, 0:64, :] = coded
        out_ref[target, 64:80, :] = codes


def whole_sum(scale, got):
    return pl.pallas_call(
        functools.partial(whole_kernel, scale),
        out_shape=jax.ShapeDtypeStruct((SPACE, 80, HALF), i16),
        in_specs=[vmem()],
        out_specs=vmem(),
        compiler_params=pltpu.CompilerParams(vmem_limit_bytes=VMEM_LIMIT),
    )(got)


def place_kernel(own_ref, got_ref, out_ref):
    scene = own_ref[1]
    for chip in range(CHIPS):
        rest = lax.rem(chip - 6 * scene + 96, 16)
        for half in range(2):
            lanes = slice(half * HALF, (half + 1) * HALF)
            source = 2 * chip + half
            step = step_of(got_ref[source, 64:80, :].astype(i32).astype(f32))
            for t in range(4):
                values = got_ref[source, t * 16 : t * 16 + 16, :].astype(i32).astype(f32) * step
                if t < 3:
                    out_ref[pl.ds(pl.multiple_of((16 * t + rest) * 16, 16), 16), lanes] = values
                else:

                    @pl.when(rest < 6)
                    def _(values=values, t=t, rest=rest, lanes=lanes):
                        out_ref[pl.ds(pl.multiple_of((16 * t + rest) * 16, 16), 16), lanes] = values


def place(own, got):
    return pl.pallas_call(
        place_kernel,
        out_shape=jax.ShapeDtypeStruct((864, 256), f32),
        in_specs=[smem(), vmem()],
        out_specs=vmem(),
        compiler_params=pltpu.CompilerParams(vmem_limit_bytes=VMEM_LIMIT),
    )(own, got)


def body(features, grad_out, weight, neighbours):
    x = features[0, 0]
    c = grad_out[0, 0]
    links = neighbours[0, 0]
    own = jnp.stack([lax.axis_index("space"), lax.axis_index("dp")]).astype(i32)
    mates = [(i, i ^ 1) for i in range(SPACE)]
    same_core = [[2 * q + core for q in range(CHIPS)] for core in range(2)]
    grad_scale = 1.0 / math.sqrt(SCENES * SPACE * 512)

    mate_links = lax.ppermute(links, "space", mates)
    outgoing, pair = pack(own, links, x, c)
    pair = lax.ppermute(pair, "space", mates)
    halo = lax.all_to_all(outgoing, "space", 0, 0, tiled=True)
    sums, terms = main(own, links, mate_links, x, c, pair, halo, weight)
    mate_sums = lax.ppermute(sums[1], "space", mates)
    terms = lax.all_to_all(terms, "space", 0, 0, tiled=True, axis_index_groups=same_core)
    scene_terms = lax.all_to_all(scene_sum(own, terms), "dp", 0, 0, tiled=True)
    whole = lax.all_to_all(whole_sum(grad_scale, scene_terms), "space", 0, 0, tiled=True)
    grad_weight = place(own, whole)
    both = (sums[0] + mate_sums).astype(bf16)
    return both[0][None, None], both[1][None, None], grad_weight


def solution(mesh):
    placed = (
        P("dp", "space", None, None),
        P("dp", "space", None, None),
        P(),
        P("dp", "space", None),
    )
    return jax.shard_map(
        body,
        mesh=mesh,
        in_specs=placed,
        out_specs=(P("dp", "space", None, None), P("dp", "space", None, None), P("dp", None)),
        check_vma=False,
    )
```

time: 562 us -> 133 us (0.24)
  waiting for transfers between devices: 315 us -> 60.1 us
  between operations: 63.8 us -> 0.71 us
  local copies, waits for them, and re-layouts: 65.7 us -> 6.53 us
  starting transfers between devices: 67.3 us -> 23.3 us
  other arithmetic: 33 us -> 1.99 us
  Pallas kernels: 0 us -> 22.7 us
  blocking collectives: 0 us -> 16.8 us
  matrix products: 13.6 us -> 0 us
    psum x1 -> x0, waiting for transfers between devices: 241 us -> none  [body(): summed = lax.psum(term_full, ('space', 'dp'))]
    ppermute x28 -> x3, waiting for transfers between devices: 74.1 us -> 1.21 us  [the longest x1 1.21 us: body(): mate_links = lax.ppermute(links, 'space', mates)]
    ppermute x28 -> x3, starting transfers between devices: 67.3 us -> 1.92 us  [the longest x1 1.32 us: body(): mate_sums = lax.ppermute(sums[1], 'space', mates)]
    all_to_all x0 -> x3, waiting for transfers between devices: none -> 58.8 us  [the longest x1 26 us: body(): halo = lax.all_to_all(outgoing, 'space', 0, 0, tiled=True)]
    unnamed x121 -> x16, local copies, waits for them, and re-layouts: 41.1 us -> 3.42 us
    select_n x7 -> x0, other arithmetic: 29.8 us -> none  [the longest x6 29.1 us: build_padded(): face = jnp.where(live[:, k][:, None, None], face, zero_value)]
    pallas_call x0 -> x5, Pallas kernels: none -> 22.7 us  [the longest x1 12.7 us: main(): pl.pallas_call(main_kernel, out_shape=(jax.ShapeDtypeStruct((2, 2, 512, 2...]
    all_to_all x0 -> x3, starting transfers between devices: none -> 21.4 us  [the longest x1 8.78 us: body(): halo = lax.all_to_all(outgoing, 'space', 0, 0, tiled=True)]
  transfers between devices with their start and end apart: 29 -> 6, of which waited for: 11 -> 4; matrix products, arithmetic and copies ran while one was open for 10% -> 3% of each run, Pallas kernels for 0% -> 4%
where the time goes in v1:
time: 133 us; the launch traced here: 132 us
  waiting for transfers between devices  60.1 us (45%)
  starting transfers between devices  23.3 us (18%)
  Pallas kernels  22.7 us (17%)
  blocking collectives  16.8 us (13%)
  local copies, waits for them, and re-layouts  6.53 us (5%)
  other arithmetic  1.99 us (1%)
    all_to_all x1, waiting for transfers between devices, body(): halo = lax.all_to_all(outgoing, 'space', 0, 0, tiled=True)  26 us
    all_to_all x1, waiting for transfers between devices, body(): lax.all_to_all(terms, 'space', 0, 0, tiled=True, axis_index_groups=same_c...  22 us
    all_to_all x1, blocking collectives, body(): scene_terms = lax.all_to_all(scene_sum(own, terms), 'dp', 0, 0, tiled=True)  16.8 us
    pallas_call x1, Pallas kernels, main(): pl.pallas_call(main_kernel, out_shape=(jax.ShapeDtypeStruct((2, 2, 512, 2...  12.7 us
    all_to_all x1, waiting for transfers between devices, body(): lax.all_to_all(whole_sum(grad_scale, scene_terms), 'space', 0, 0, tiled=T...  10.8 us
    all_to_all x1, starting transfers between devices, body(): halo = lax.all_to_all(outgoing, 'space', 0, 0, tiled=True)  8.78 us
    all_to_all x1, starting transfers between devices, body(): lax.all_to_all(whole_sum(grad_scale, scene_terms), 'space', 0, 0, tiled=T...  7.88 us
    all_to_all x1, starting transfers between devices, body(): lax.all_to_all(terms, 'space', 0, 0, tiled=True, axis_index_groups=same_c...  4.75 us
  transfers between devices with their start and end apart: 6, of which 4 were waited for; matrix products, arithmetic and copies ran while one was open for 3% of the time, Pallas kernels for 4%

profile of v1, /device:TPU:1, one launch (start us, length us, event | category | flops | bytes accessed | tf_op | source)
XLA Modules:
  0.0 132.1 jit_solution(16507898911337890926)
XLA Ops:
  0.6 0.7 pad_add_fusion.own_ref
  1.3 2.9 %shard_map.67 = (bf16[32,2,64,256]{3,2,1,0:T(8,128)(2,1)}, bf16[512,384]{1,0:T(8,128)(2,1)}) custom-call(s32[2]{0:T(128)} %pad_add_fusion.own_ref, s32[27]{0:T(128)} %bitcast.19, bf16[512,256]{1,0:T(8,128)(2,1)} %bitcast.15, bf16[512,256]{1,0:T(8,128)(2,1)} %bitcast.17), custom_call_target="tpu_custom_call" | custom-call | tf_op jit(solution)/shard_map/pallas_call | solution.py:94
  4.2 0.0 copy-start.7
  4.2 0.0 copy-start.5
  4.2 8.8 %all-to-all-start = ((bf16[32,2,64,256]{3,2,1,0:T(8,128)(2,1)}), bf16[32,2,64,256]{3,2,1,0:T(8,128)(2,1)S(1)}, u32[]{:S(2)}, u32[]{:S(2)}) async-start(bf16[32,2,64,256]{3,2,1,0:T(8,128)(2,1)} %get-tuple-element.8), calls=%async_computation | async-start | bytes 4194304 | tf_op jit(solution)/shard_map/all_to_all | solution.py:371
  12.9 0.0 copy-done.7
  12.9 0.3 collective-permute-start.1
  13.3 0.0 copy-done.5
  13.3 0.3 collective-permute-start
  13.5 1.2 collective-permute-done.mate_links_ref
  14.8 0.0 collective-permute-done.1.pair_ref
  14.8 26.0 %all-to-all-done.halo_ref = bf16[32,2,64,256]{3,2,1,0:T(8,128)(2,1)S(1)} async-done(((bf16[32,2,64,256]{3,2,1,0:T(8,128)(2,1)}), bf16[32,2,64,256]{3,2,1,0:T(8,128)(2,1)S(1)}, u32[]{:S(2)}, u32[]{:S(2)}) %all-to-all-start) | async-done | bytes 2097184 | tf_op jit(solution)/shard_map/all_to_all | solution.py:371
  40.8 0.0 copy-done.6
  40.8 0.0 copy-done.4
  40.8 1.3 copy-done
  42.1 12.7 %shard_map.68 = (f32[2,2,512,256]{3,2,1,0:T(8,128)}, s16[16,448,128]{2,1,0:T(8,128)(2,1)}) custom-call(s32[2]{0:T(128)} %pad_add_fusion.own_ref, s32[27]{0:T(128)} %bitcast.20, s32[27]{0:T(128)} %copy-done.6, bf16[512,256]{1,0:T(8,128)(2,1)} %bitcast.16, bf16[512,256]{1,0:T(8,128)(2,1)} %bitcast.18, bf16[512,384]{1,0:T(8,128)(2,1)} %copy-done.4, ...), custom_call_target="tpu_custom_call" | custom-call | tf_op jit(solution)/shard_map/pallas_call | solution.py:247
  54.8 4.8 %all-to-all-start.1 = ((s16[16,448,128]{2,1,0:T(8,128)(2,1)}), s16[16,448,128]{2,1,0:T(8,128)(2,1)S(1)}, u32[]{:S(2)}, u32[]{:S(2)}) async-start(s16[16,448,128]{2,1,0:T(8,128)(2,1)} %get-tuple-element.10), calls=%async_computation.1 | async-start | bytes 3670016 | tf_op jit(solution)/shard_map/all_to_all | solution.py:374
  59.6 2.3 %slice_bitcast_fusion = f32[2,512,256]{2,1,0:T(8,128)} fusion(f32[2,2,512,256]{3,2,1,0:T(8,128)} %get-tuple-element.9), kind=kLoop, calls=%fused_computation.2 | loop fusion | bytes 2097152 | tf_op jit(solution)/shard_map/squeeze | solution.py:373
  61.8 1.3 collective-permute-start.2
  63.2 22.0 %all-to-all-done.1.got_ref = s16[16,448,128]{2,1,0:T(8,128)(2,1)S(1)} async-done(((s16[16,448,128]{2,1,0:T(8,128)(2,1)}), s16[16,448,128]{2,1,0:T(8,128)(2,1)S(1)}, u32[]{:S(2)}, u32[]{:S(2)}) %all-to-all-start.1) | async-done | bytes 1835040 | tf_op jit(solution)/shard_map/all_to_all | solution.py:374
  85.1 1.2 copy-done.1
  86.4 2.8 %shard_map.69 = s16[8,80,128]{2,1,0:T(8,128)(2,1)} custom-call(s32[2]{0:T(128)} %pad_add_fusion.own_ref, s16[16,448,128]{2,1,0:T(8,128)(2,1)} %copy-done.1), custom_call_target="tpu_custom_call" | custom-call | tf_op jit(solution)/shard_map/pallas_call | solution.py:296
  89.2 16.8 %all_to_all.20.got_ref = s16[8,80,128]{2,1,0:T(8,128)(2,1)} all-to-all(s16[8,80,128]{2,1,0:T(8,128)(2,1)} %shard_map.69), channel_id=1, replica_groups=mesh['space'=32,'dp'=8] {'dp'}, dimensions={0} | all-to-all | bytes 327680 | tf_op jit(solution)/shard_map/all_to_all | solution.py:375
  106.0 1.9 %shard_map.70 = s16[32,80,128]{2,1,0:T(8,128)(2,1)} custom-call(s16[8,80,128]{2,1,0:T(8,128)(2,1)} %all_to_all.20.got_ref), custom_call_target="tpu_custom_call" | custom-call | tf_op jit(solution)/shard_map/pallas_call | solution.py:321
  107.9 7.9 %all-to-all-start.3 = ((s16[32,80,128]{2,1,0:T(8,128)(2,1)}), s16[32,80,128]{2,1,0:T(8,128)(2,1)S(1)}, u32[]{:S(2)}, u32[]{:S(2)}) async-start(s16[32,80,128]{2,1,0:T(8,128)(2,1)} %shard_map.70), calls=%async_computation.3 | async-start | bytes 1310720 | tf_op jit(solution)/shard_map/all_to_all | solution.py:376
  115.8 0.0 collective-permute-done.2
  115.8 0.0 copy-done.3
  115.8 1.3 %fusion = bf16[2,512,256]{2,1,0:T(8,128)(2,1)S(1)} fusion(f32[2,512,256]{2,1,0:T(8,128)} %collective-permute-done.2, f32[2,2,512,256]{3,2,1,0:T(8,128)S(1)} %copy-done.3), kind=kLoop, calls=%fused_computation.1 | loop fusion | flops 524288 | bytes 2621440 | tf_op jit(solution)/shard_map/convert_element_type | solution.py:378
  117.2 0.8 slice_bitcast_fusion.1
  118.0 10.8 %all-to-all-done.3.got_ref = s16[32,80,128]{2,1,0:T(8,128)(2,1)S(1)} async-done(((s16[32,80,128]{2,1,0:T(8,128)(2,1)}), s16[32,80,128]{2,1,0:T(8,128)(2,1)S(1)}, u32[]{:S(2)}, u32[]{:S(2)}) %all-to-all-start.3) | async-done | bytes 655392 | tf_op jit(solution)/shard_map/all_to_all | solution.py:376
  128.8 0.8 copy-done.2
  129.7 2.5 %shard_map.71 = f32[864,256]{1,0:T(8,128)} custom-call(s32[2]{0:T(128)} %pad_add_fusion.own_ref, s16[32,80,128]{2,1,0:T(8,128)(2,1)} %copy-done.2), custom_call_target="tpu_custom_call" | custom-call | tf_op jit(solution)/shard_map/pallas_call | solution.py:350
  (6 shorter events, 0.0 us)
Async XLA Ops:
  4.2 8.8 %copy-start.7 = (bf16[512,384]{1,0:T(8,128)(2,1)S(1)}, bf16[512,384]{1,0:T(8,128)(2,1)}, u32[]{:S(2)}) copy-start(bf16[512,384]{1,0:T(8,128)(2,1)} %get-tuple-element.7) | copy-start | bytes 1179652
  4.2 9.1 %copy-start.5 = (s32[1,1,27]{2,1,0:T(1,128)S(1)}, s32[1,1,27]{2,1,0:T(1,128)}, u32[]{:S(2)}) copy-start(s32[1,1,27]{2,1,0:T(1,128)} %param.7) | copy-start | bytes 328
  4.2 36.6 %all-to-all-start = ((bf16[32,2,64,256]{3,2,1,0:T(8,128)(2,1)}), bf16[32,2,64,256]{3,2,1,0:T(8,128)(2,1)S(1)}, u32[]{:S(2)}, u32[]{:S(2)}) async-start(bf16[32,2,64,256]{3,2,1,0:T(8,128)(2,1)} %get-tuple-element.8), calls=%async_computation | async-start | bytes 4194304 | tf_op jit(solution)/shard_map/all_to_all | solution.py:371
  12.9 1.8 %collective-permute-start.1 = (bf16[512,384]{1,0:T(8,128)(2,1)S(1)}, bf16[512,384]{1,0:T(8,128)(2,1)S(1)}, u32[]{:S(2)}, u32[]{:S(2)}) collective-permute-start(bf16[512,384]{1,0:T(8,128)(2,1)S(1)} %copy-done.7), channel_id=1, source_target_pairs={{0,8},{8,0},{16,24},{24,16},{32,40},{40,32},{48,56},{56,48},{64,72... | collective-permute-start | bytes 1179656 | tf_op jit(solution)/shard_map/ppermute | solution.py:370
  13.3 1.5 %collective-permute-start = (s32[27]{0:T(128)S(1)}, s32[27]{0:T(128)S(1)}, u32[]{:S(2)}, u32[]{:S(2)}) collective-permute-start(s32[27]{0:T(128)S(1)} %bitcast.21), channel_id=1, source_target_pairs={{0,8},{8,0},{16,24},{24,16},{32,40},{40,32},{48,56},{56,48},{64,72... | collective-permute-start | bytes 332 | tf_op jit(solution)/shard_map/ppermute | solution.py:368
  14.8 26.0 %copy-start.6 = (s32[27]{0:T(128)}, s32[27]{0:T(128)S(1)}, u32[]{:S(2)}) copy-start(s32[27]{0:T(128)S(1)} %collective-permute-done.mate_links_ref) | copy-start | bytes 328
  14.8 26.0 %copy-start.4 = (bf16[512,384]{1,0:T(8,128)(2,1)}, bf16[512,384]{1,0:T(8,128)(2,1)S(1)}, u32[]{:S(2)}) copy-start(bf16[512,384]{1,0:T(8,128)(2,1)S(1)} %collective-permute-done.1.pair_ref) | copy-start | bytes 1179652
  40.8 1.3 copy-start
  54.8 30.4 %all-to-all-start.1 = ((s16[16,448,128]{2,1,0:T(8,128)(2,1)}), s16[16,448,128]{2,1,0:T(8,128)(2,1)S(1)}, u32[]{:S(2)}, u32[]{:S(2)}) async-start(s16[16,448,128]{2,1,0:T(8,128)(2,1)} %get-tuple-element.10), calls=%async_computation.1 | async-start | bytes 3670016 | tf_op jit(solution)/shard_map/all_to_all | solution.py:374
  61.8 54.0 %collective-permute-start.2 = (f32[2,512,256]{2,1,0:T(8,128)}, f32[2,512,256]{2,1,0:T(8,128)}, u32[]{:S(2)}, u32[]{:S(2)}) collective-permute-start(f32[2,512,256]{2,1,0:T(8,128)} %slice_bitcast_fusion), channel_id=1, source_target_pairs={{0,8},{8,0},{16,24},{24,16},{32,40},{40,32},{48,56},{56,48},{64,72... | collective-permute-start | bytes 3145736 | tf_op jit(solution)/shard_map/ppermute | solution.py:373
  85.1 1.2 copy-start.1
  89.2 26.6 %copy-start.3 = (f32[2,2,512,256]{3,2,1,0:T(8,128)S(1)}, f32[2,2,512,256]{3,2,1,0:T(8,128)}, u32[]{:S(2)}) copy-start(f32[2,2,512,256]{3,2,1,0:T(8,128)} %get-tuple-element.9) | copy-start | bytes 6291460
  107.9 20.9 %all-to-all-start.3 = ((s16[32,80,128]{2,1,0:T(8,128)(2,1)}), s16[32,80,128]{2,1,0:T(8,128)(2,1)S(1)}, u32[]{:S(2)}, u32[]{:S(2)}) async-start(s16[32,80,128]{2,1,0:T(8,128)(2,1)} %shard_map.70), calls=%async_computation.3 | async-start | bytes 1310720 | tf_op jit(solution)/shard_map/all_to_all | solution.py:376
  128.8 0.8 copy-start.2

commit v2 on v1

v2 whole, which is shorter than its diff:
```python
import functools
import math

import jax
import jax.numpy as jnp
from jax import lax
from jax.experimental import pallas as pl
from jax.experimental.pallas import tpu as pltpu
from jax.sharding import PartitionSpec as P

f32 = jnp.float32
bf16 = jnp.bfloat16
i16 = jnp.int16
i32 = jnp.int32

SPACE = 32
LG, LS, LW, LP = 51, 50, 50, 51

SCENES = 8
CHIPS = 16
HALF = 128
LEVELS = 32766.0

FAR = 3
HOPS = (-2, -1, 1, 2)

OFFSETS = [(k, k // 9 - 1, k // 3 % 3 - 1, k % 3 - 1) for k in range(27) if k != 13]


def position():
    return lax.axis_index("space"), lax.axis_index("dp")


def params(mib):
    return pltpu.CompilerParams(vmem_limit_bytes=mib << 20)


def cost(us):
    return pl.CostEstimate(flops=int(us * 1e9), bytes_accessed=1 << 20, transcendentals=0)


def vmem():
    return pl.BlockSpec(memory_space=pltpu.VMEM)


def smem():
    return pl.BlockSpec(memory_space=pltpu.SMEM)


def hbm():
    return pl.BlockSpec(memory_space=pltpu.HBM)


def anywhere():
    return pl.BlockSpec(memory_space=pl.ANY)


def side(shift):
    return 7 if shift > 0 else 0


def region(ref, shifts):
    dx, dy, dz = shifts
    kinds = (dx != 0, dy != 0, dz != 0)
    if kinds == (True, False, False):
        return ref[pl.ds(side(dx) * 64, 64), :]
    if kinds == (False, True, False):
        return jnp.concatenate([ref[pl.ds(x * 64 + side(dy) * 8, 8), :] for x in range(8)], axis=0)
    if kinds == (False, False, True):
        return ref[pl.ds(side(dz), 64, stride=8), :]
    if kinds == (True, True, False):
        rows = ref[pl.ds(side(dx) * 64 + side(dy) * 8, 8), :]
    elif kinds == (True, False, True):
        rows = ref[pl.ds(side(dx) * 64 + side(dz), 8, stride=8), :]
    elif kinds == (False, True, True):
        rows = ref[pl.ds(side(dy) * 8 + side(dz), 8, stride=64), :]
    else:
        row = ref[pl.ds(side(dx) * 64 + side(dy) * 8 + side(dz), 1), :]
        rows = jnp.broadcast_to(row, (8, HALF))
    return jnp.concatenate([rows, rows], axis=0)


def pack_kernel(links_ref, x_ref, c_ref, out_ref, parts):
    chip = position()[0] // 2
    for half in range(2):
        lanes = slice(half * HALF, (half + 1) * HALF)
        parts[half] = c_ref[:, lanes].astype(f32)
        parts[2 + half] = x_ref[:, lanes].astype(f32)
    for k, *shifts in OFFSETS:
        target = links_ref[k]

        @pl.when(target >= 0)
        def _(target=target, shifts=tuple(shifts)):
            to = target // 2
            brick = lax.rem(target, 2)
            for half in range(2):
                rows = region(parts.at[half], shifts)
                out_ref[2 * to + half, brick, 0 : rows.shape[0], :] = rows.astype(bf16)
            if sum(map(abs, shifts)) > 1:

                @pl.when(jnp.abs(to - chip) >= FAR)
                def _():
                    for half in range(2):
                        out_ref[2 * to + half, brick, 16:32, :] = region(parts.at[2 + half], shifts).astype(bf16)


def pack(links, x, c):
    return pl.pallas_call(
        pack_kernel,
        out_shape=jax.ShapeDtypeStruct((SPACE, 2, 64, HALF), bf16),
        in_specs=[smem(), vmem(), vmem()],
        out_specs=vmem(),
        scratch_shapes=[pltpu.VMEM((4, 512, HALF), f32)],
        compiler_params=params(56),
    )(links, x, c)


def pair_kernel(x_ref, c_ref, _, out_ref):
    core = lax.rem(position()[0], 2)
    out_ref[:, 0:256] = x_ref[...]
    for here in range(2):

        @pl.when(core == here)
        def _(here=here):
            out_ref[:, 256:384] = c_ref[:, (1 - here) * HALF : (2 - here) * HALF]


def pair_rows(x, c, after):
    return pl.pallas_call(
        pair_kernel,
        out_shape=jax.ShapeDtypeStruct((512, 384), bf16),
        in_specs=[vmem(), vmem(), anywhere()],
        out_specs=vmem(),
        compiler_params=params(56),
        cost_estimate=cost(1.0),
    )(x, c, after)


def prepare_kernel(links_ref, mate_links_ref, x_ref, c_ref, pair_ref, *rest):
    outs, turned_ref, x_half_ref, c_half_ref, parts, slots, sems = rest[:5], *rest[5:]
    own = position()[0]
    core = lax.rem(own, 2)
    chip = own // 2
    mate = 1 - core
    for here in range(2):

        @pl.when(core == here)
        def _(here=here):
            lanes = slice(here * HALF, (here + 1) * HALF)
            x_half_ref[here] = x_ref[:, lanes]
            x_half_ref[1 - here] = pair_ref[:, lanes]
            c_half_ref[here] = c_ref[:, lanes]
            c_half_ref[1 - here] = pair_ref[:, 256:384]

    turned_ref[core] = x_ref[...].T
    turned_ref[mate] = pair_ref[:, 0:256].T
    for brick in range(2):
        parts[brick] = x_half_ref[brick].astype(f32)
        for k, *shifts in OFFSETS:
            target = jnp.where(core == brick, links_ref[k], mate_links_ref[k])

            @pl.when(target >= 0)
            def _(brick=brick, target=target, shifts=tuple(shifts)):
                rows = region(parts.at[brick], shifts)
                slots[target // 2 - chip + 4, 2 * brick + lax.rem(target, 2), 0 : rows.shape[0], :] = rows.astype(bf16)

    copies = [
        pltpu.make_async_copy(slots.at[hop + 4], out, sems.at[n])
        for n, (hop, out) in enumerate(zip(HOPS + (0,), outs))
    ]
    for copy in copies:
        copy.start()
    for copy in copies:
        copy.wait()


def prepare(links, mate_links, x, c, pair):
    half = jax.ShapeDtypeStruct((2, 512, HALF), bf16)
    got = pl.pallas_call(
        prepare_kernel,
        out_shape=tuple(jax.ShapeDtypeStruct((4, 64, HALF), bf16) for hop in HOPS + (0,))
        + (jax.ShapeDtypeStruct((2, 256, 512), bf16), half, half),
        in_specs=[smem(), smem(), vmem(), vmem(), vmem()],
        out_specs=(anywhere(),) * 5 + (vmem(),) * 3,
        scratch_shapes=[
            pltpu.VMEM((2, 512, HALF), f32),
            pltpu.VMEM((9, 4, 64, HALF), bf16),
            pltpu.SemaphoreType.DMA((5,)),
        ],
        compiler_params=params(LP),
        cost_estimate=cost(2.5),
    )(links, mate_links, x, c, pair)
    return got[:5], *got[5:]


def target_plane(shift):
    return 9 if shift > 0 else 0


def scaling(peak):
    code = jnp.ceil(jnp.log2(jnp.maximum(peak, 2.0**-110)) * 256.0) + 1.0
    return LEVELS * jnp.exp2(code * (-1.0 / 256.0)), code


def fixed(values):
    return jnp.round(values).astype(i32).astype(i16)


def plain(coded):
    return coded.astype(i32).astype(f32)


def step_of(code):
    return jnp.exp2(code * (1.0 / 256.0)) * (1.0 / LEVELS)


def fill(brick, links, fetch, own_rows, plane, low, high, shifted_low, shifted_high, padded):
    plane[...] = jnp.zeros_like(plane)
    low[...] = jnp.zeros_like(low)
    high[...] = jnp.zeros_like(high)
    for x in range(8):
        plane[pl.ds((x + 1) * 80 + 8, 64), :] = own_rows(x * 64)
    for k, dx, dy, dz in OFFSETS:
        source = links[k]

        @pl.when(source >= 0)
        def _(source=source, k=k, dx=dx, dy=dy, dz=dz):
            at_x, at_y = target_plane(dx), target_plane(dy)
            face = (dx != 0) + (dy != 0) + (dz != 0) == 1
            got = fetch(source, brick, k, 64 if face else 16).astype(f32)
            if dz == 0:
                if dy == 0:
                    plane[pl.ds(at_x * 80 + 8, 64), :] = got
                elif dx == 0:
                    for x in range(8):
                        plane[pl.ds((x + 1) * 80 + at_y * 8, 8), :] = got[x * 8 : x * 8 + 8]
                else:
                    plane[pl.ds(at_x * 80 + at_y * 8, 8), :] = got[0:8]
            else:
                rim = low if dz < 0 else high
                if dx == 0 and dy == 0:
                    for x in range(8):
                        rim[pl.ds((x + 1) * 10 + 1, 8), :] = got[x * 8 : x * 8 + 8]
                elif dy == 0:
                    rim[pl.ds(at_x * 10 + 1, 8), :] = got[0:8]
                elif dx == 0:
                    rim[pl.ds(10 + at_y, 8, stride=10), :] = got[0:8]
                else:
                    rim[pl.ds(at_x * 10 + at_y, 1), :] = got[0:1]

    shifted_low[pl.ds(1, 800), :] = plane[pl.ds(0, 800), :]
    shifted_low[pl.ds(0, 104, stride=8), :] = low[...]
    shifted_high[pl.ds(0, 800), :] = plane[pl.ds(1, 800), :]
    shifted_high[pl.ds(7, 104, stride=8), :] = high[...]
    for j in range(3):
        for l, source in enumerate((shifted_low, plane, shifted_high)):
            at = (3 * j + l) * HALF
            for x in range(10):
                padded[brick, x * 64 : x * 64 + 64, at : at + HALF] = source[pl.ds(x * 80 + j * 8, 64), :].astype(bf16)


def fill_both(core, links_ref, mate_links_ref, half_ref, fetch, scratch):
    for brick in range(2):

        def rows(first, brick=brick):
            return half_ref[brick, pl.ds(first, 64), :].astype(f32)

        fill(brick, [jnp.where(core == brick, links_ref[k], mate_links_ref[k]) for k in range(27)], fetch, rows, *scratch)


def by_distance(halo_ref, chip):
    return lambda source, brick, k, count: halo_ref[source // 2 - chip + 4, 2 * lax.rem(source, 2) + brick, 0:count, :]


FILL_SCRATCH = [
    pltpu.VMEM((832, HALF), f32),
    pltpu.VMEM((104, HALF), f32),
    pltpu.VMEM((104, HALF), f32),
    pltpu.VMEM((832, HALF), f32),
    pltpu.VMEM((832, HALF), f32),
    pltpu.VMEM((2, 640, 9 * HALF), bf16),
]


def by_device(halo_ref):
    return lambda source, brick, k, count: halo_ref[source, brick, 0:count, :]


def kernel_grad_kernel(links_ref, mate_links_ref, c_half_ref, turned_ref, halo_ref, terms_ref, grads, coded, sems, *scratch):
    core = lax.rem(position()[0], 2)
    padded = scratch[-1]
    fill_both(core, links_ref, mate_links_ref, c_half_ref, by_device(halo_ref), scratch)
    for i in range(3):
        window = slice(i * 64, i * 64 + 512)
        term = jnp.dot(turned_ref[0], padded[0, window, :], preferred_element_type=f32)
        term += jnp.dot(turned_ref[1], padded[1, window, :], preferred_element_type=f32)
        for jl in range(9):
            grads[26 - (9 * i + jl)] = term[:, jl * HALF : (jl + 1) * HALF]
    copies = []
    for q in range(CHIPS):
        def rows(k, q=q):
            return jnp.concatenate([grads[k, pl.ds(at + q * 8, 8), :] for at in (0, 128)], axis=0)

        peak = jnp.abs(rows(0))
        for k in range(1, 27):
            peak = jnp.maximum(peak, jnp.abs(rows(k)))
        factor, code = scaling(jnp.max(peak, axis=0, keepdims=True))
        for k in range(27):
            coded[q, k * 16 : k * 16 + 16, :] = fixed(rows(k) * factor)
        coded[q, 432:448, :] = fixed(jnp.broadcast_to(code, (16, HALF)))
        copies.append(pltpu.make_async_copy(coded.at[q], terms_ref.at[q], sems.at[q]))
        copies[-1].start()
    for copy in copies:
        copy.wait()


def kernel_grad(links, mate_links, c_half, turned, halo):
    return pl.pallas_call(
        kernel_grad_kernel,
        out_shape=jax.ShapeDtypeStruct((CHIPS, 448, HALF), i16),
        in_specs=[smem(), smem(), vmem(), vmem(), vmem()],
        out_specs=anywhere(),
        scratch_shapes=[
            pltpu.VMEM((27, 256, HALF), f32),
            pltpu.VMEM((CHIPS, 448, HALF), i16),
            pltpu.SemaphoreType.DMA((CHIPS,)),
        ]
        + FILL_SCRATCH,
        compiler_params=params(LG),
        cost_estimate=cost(6.0),
    )(links, mate_links, c_half, turned, halo)


def taps_kernel(turned, links_ref, mate_links_ref, half_ref, weight_ref, halo_ref, *rest):
    own = position()[0]
    core = lax.rem(own, 2)
    start = pl.multiple_of(core * HALF, HALF)
    if turned:
        _, out_ref, mate_out_ref, taps, sems, *scratch = rest
        fetch = by_device(halo_ref)
        halo_copies = []
        copies = [
            pltpu.make_async_copy(
                weight_ref.at[26 - k, :, pl.ds(start, HALF)], taps.at[:, pl.ds(k * HALF, HALF)], sems.at[k]
            )
            for k in range(27)
        ]
    else:
        halos, (out_ref, mate_out_ref, taps, sems, slots, far_sems, *scratch) = rest[:5], rest[5:]
        chip = own // 2
        fetch = by_distance(slots, chip)
        halo_copies = [
            pltpu.make_async_copy(halo, slots.at[4 - hop], sems.at[1 + n])
            for n, (hop, halo) in enumerate(zip(HOPS + (0,), halos))
        ]
        for hop in (-4, -3, 3, 4):
            source = jnp.clip(chip + hop, 0, CHIPS - 1)
            for side_by in range(4):
                halo_copies.append(
                    pltpu.make_async_copy(
                        halo_ref.at[2 * source + side_by // 2, side_by % 2, pl.ds(16, 16), :],
                        slots.at[4 + hop, side_by, pl.ds(0, 16), :],
                        far_sems.at[4 + hop, side_by],
                    )
                )
        copies = [pltpu.make_async_copy(weight_ref.at[:, pl.ds(start, HALF), :], taps, sems.at[0])]
    padded = scratch[-1]
    for copy in halo_copies + copies:
        copy.start()
    for copy in halo_copies:
        copy.wait()
    fill_both(core, links_ref, mate_links_ref, half_ref, fetch, scratch)
    for copy in copies:
        copy.wait()
    for to_mate, out in ((0, out_ref), (1, mate_out_ref)):
        brick = lax.rem(core + to_mate, 2)
        total = jnp.zeros((512, 256), f32)
        for i in range(3):
            block = padded[brick, i * 64 : i * 64 + 512, :]
            if turned:
                now = taps[:, i * 9 * HALF : (i + 1) * 9 * HALF]
                total += lax.dot_general(block, now, (((1,), (1,)), ((), ())), preferred_element_type=f32)
            else:
                now = taps[9 * i : 9 * i + 9].reshape(9 * HALF, 256)
                total += jnp.dot(block, now, preferred_element_type=f32)
        out[...] = total


def taps_product(turned, links, mate_links, half, weight, halo, *rest):
    taps = pltpu.VMEM((256, 27 * HALF) if turned else (27, HALF, 256), bf16)
    slots = [] if turned else [pltpu.VMEM((9, 4, 64, HALF), bf16), pltpu.SemaphoreType.DMA((9, 4))]
    return pl.pallas_call(
        functools.partial(taps_kernel, turned),
        out_shape=(jax.ShapeDtypeStruct((512, 256), f32),) * 2,
        in_specs=[smem(), smem(), vmem(), hbm(), vmem() if turned else hbm()] + [anywhere()] * len(rest),
        out_specs=(vmem(), vmem()),
        scratch_shapes=[taps, pltpu.SemaphoreType.DMA((28,))] + slots + FILL_SCRATCH,
        compiler_params=params(56),
        cost_estimate=cost(6.0),
    )(links, mate_links, half, weight, halo, *rest)


def first_unit(chip, scene):
    return lax.rem(chip - 12 * scene + 96, 16)


def coded_block(values):
    factor, code = scaling(jnp.max(jnp.abs(values), axis=0, keepdims=True))
    return fixed(jnp.concatenate([values * factor, jnp.broadcast_to(code, (8, HALF))], axis=0))


def plain_block(coded):
    values = plain(coded)
    return values[0:56] * step_of(values[56:57])


def scene_kernel(got_ref, out_ref, total):
    chip = position()[0] // 2
    steps = [step_of(plain(got_ref[source, 432:448, :])) for source in range(CHIPS)]
    for k in range(27):
        sums = jnp.zeros((16, HALF), f32)
        for source in range(CHIPS):
            sums += plain(got_ref[source, k * 16 : k * 16 + 16, :]) * steps[source]
        total[2 * k] = sums[0:8]
        total[2 * k + 1] = sums[8:16]
    total[54] = jnp.zeros((8, HALF), f32)
    for scene in range(SCENES):
        first = (108 * scene + first_unit(chip, scene) - chip) // 16
        units = [total[jnp.minimum(first + t, 54)] for t in range(7)]
        out_ref[scene] = coded_block(jnp.concatenate(units, axis=0))


def scene_sum(got):
    return pl.pallas_call(
        scene_kernel,
        out_shape=jax.ShapeDtypeStruct((SCENES, 64, HALF), i16),
        in_specs=[vmem()],
        out_specs=vmem(),
        scratch_shapes=[pltpu.VMEM((55, 8, HALF), f32)],
        compiler_params=params(LS),
        cost_estimate=cost(2.5),
    )(got)


def whole_kernel(scale, got_ref, out_ref):
    total = plain_block(got_ref[0])
    for scene in range(1, SCENES):
        total += plain_block(got_ref[scene])
    block = coded_block(total * scale)
    for target in range(SPACE):
        out_ref[target] = block


def whole_sum(scale, got):
    return pl.pallas_call(
        functools.partial(whole_kernel, scale),
        out_shape=jax.ShapeDtypeStruct((SPACE, 64, HALF), i16),
        in_specs=[vmem()],
        out_specs=vmem(),
        compiler_params=params(LW),
        cost_estimate=cost(1.5),
    )(got)


def place_kernel(got_ref, out_ref, whole, sems):
    scene = position()[1]
    outs = [
        pltpu.make_async_copy(whole.at[pl.ds(t * 128, size), :], out_ref.at[pl.ds(t * 128, size), :], sems.at[t])
        for t, size in enumerate((128,) * 6 + (96,))
    ]
    steps = [step_of(plain(got_ref[source, 48:64, :])[8:9]) for source in range(SPACE)]
    for t in range(0, 7, 2):
        for chip in range(CHIPS):
            rest = first_unit(chip, scene)
            for half in range(2):
                source = 2 * chip + half
                lanes = slice(half * HALF, (half + 1) * HALF)
                values = plain(got_ref[source, t * 8 : t * 8 + 16, :]) * steps[source]
                for now in range(t, min(t + 2, 7)):
                    at = pl.multiple_of((16 * now + rest) * 8, 8)
                    whole[pl.ds(at, 8), lanes] = values[(now - t) * 8 : (now - t + 1) * 8]
        for now in range(t, min(t + 2, 7)):
            outs[now].start()
    for copy in outs:
        copy.wait()


def place(got):
    return pl.pallas_call(
        place_kernel,
        out_shape=jax.ShapeDtypeStruct((864, 256), f32),
        in_specs=[vmem()],
        out_specs=hbm(),
        scratch_shapes=[pltpu.VMEM((896, 256), f32), pltpu.SemaphoreType.DMA((7,))],
        compiler_params=params(8),
    )(got)


def body(features, grad_out, weight, neighbours):
    x = features[0, 0]
    c = grad_out[0, 0]
    links = neighbours[0, 0]
    mates = [(i, i ^ 1) for i in range(SPACE)]
    same_core = [[2 * q + core for q in range(CHIPS)] for core in range(2)]
    grad_scale = 1.0 / math.sqrt(SCENES * SPACE * 512)

    mate_links = lax.ppermute(links, "space", mates)
    outgoing_c = pack(links, x, c)
    halo_c = lax.all_to_all(outgoing_c, "space", 0, 0, tiled=True)
    pair = lax.ppermute(pair_rows(x, c, outgoing_c), "space", mates)
    outgoing_x, turned, x_half, c_half = prepare(links, mate_links, x, c, pair)
    halo_x = [
        lax.ppermute(rows, "space", [(i, i + 2 * hop) for i in range(SPACE) if 0 <= i + 2 * hop < SPACE])
        for hop, rows in zip(HOPS, outgoing_x)
    ]
    terms = kernel_grad(links, mate_links, c_half, turned, halo_c)
    got_terms = lax.all_to_all(terms, "space", 0, 0, tiled=True, axis_index_groups=same_core)
    grad_in, mate_grad_in = taps_product(True, links, mate_links, c_half, weight, halo_c, terms)
    got_terms, grad_in, mate_grad_in = lax.optimization_barrier((got_terms, grad_in, mate_grad_in))
    scene_terms = lax.all_to_all(scene_sum(got_terms), "dp", 0, 0, tiled=True)
    conv_out, mate_conv_out = taps_product(False, links, mate_links, x_half, weight, halo_c, *halo_x, outgoing_x[4])
    scene_terms, conv_out, mate_conv_out = lax.optimization_barrier((scene_terms, conv_out, mate_conv_out))
    whole = lax.all_to_all(whole_sum(grad_scale, scene_terms), "space", 0, 0, tiled=True)
    grad_in = (grad_in + lax.ppermute(mate_grad_in, "space", mates)).astype(bf16)
    conv_out = (conv_out + lax.ppermute(mate_conv_out, "space", mates)).astype(bf16)
    return conv_out[None, None], grad_in[None, None], place(whole)


def solution(mesh):
    placed = (
        P("dp", "space", None, None),
        P("dp", "space", None, None),
        P(),
        P("dp", "space", None),
    )
    return jax.shard_map(
        body,
        mesh=mesh,
        in_specs=placed,
        out_specs=(P("dp", "space", None, None), P("dp", "space", None, None), P("dp", None)),
        check_vma=False,
    )
```

time: 133 us -> 107 us (0.80)
  waiting for transfers between devices: 60.1 us -> 33.2 us
  starting transfers between devices: 23.3 us -> 41.2 us
  blocking collectives: 16.8 us -> 0 us
  Pallas kernels: 22.7 us -> 27.6 us
  local copies, waits for them, and re-layouts: 6.53 us -> 2 us
    all_to_all x1 -> x0, blocking collectives: 16.8 us -> none  [body(): scene_terms = lax.all_to_all(scene_sum(own, terms), 'dp', 0, 0, tiled=True)]
    all_to_all x1 -> x2, waiting for transfers between devices: 26 us -> 10.2 us  [the longest x1 10.2 us: body(): halo_c = lax.all_to_all(outgoing_c, 'space', 0, 0, tiled=True)]
    ppermute x2 -> x7, starting transfers between devices: 1.64 us -> 16.5 us  [the longest x4 12.5 us: body(): lax.ppermute(rows, 'space', [(i, i + 2 * hop) for i in range(SPACE) if 0...]
    all_to_all x1, waiting for transfers between devices: 22 us -> 10.8 us  [body(): lax.all_to_all(terms, 'space', 0, 0, tiled=True, axis_index_groups=same_c...]
    all_to_all x1 -> x2, starting transfers between devices: 8.78 us -> 16.8 us  [the longest x1 8.64 us: body(): halo_c = lax.all_to_all(outgoing_c, 'space', 0, 0, tiled=True)]
    pallas_call x3 -> x7, Pallas kernels: 18.4 us -> 25.6 us  [the longest x2 13.1 us: taps_product(): pl.pallas_call(functools.partial(taps_kernel, turned), out_shape=(jax.Sha...]
    all_to_all x1, starting transfers between devices: 7.88 us -> 3.84 us  [body(): lax.all_to_all(whole_sum(grad_scale, scene_terms), 'space', 0, 0, tiled=T...]
    squeeze x1 -> x0, local copies, waits for them, and re-layouts: 2.29 us -> none  [body(): mate_sums = lax.ppermute(sums[1], 'space', mates)]
  transfers between devices with their start and end apart: 6 -> 12, of which waited for: 4 -> 5; matrix products, arithmetic and copies ran while one was open for 3% -> 1% of each run, Pallas kernels for 4% -> 19%
where the time goes in v2:
time: 107 us; the launch traced here: 106 us
  starting transfers between devices  41.2 us (39%)
  waiting for transfers between devices  33.2 us (31%)
  Pallas kernels  27.6 us (26%)
  local copies, waits for them, and re-layouts  2 us (2%)
  other arithmetic  1.51 us (1%)
    pallas_call x2, Pallas kernels, taps_product(): pl.pallas_call(functools.partial(taps_kernel, turned), out_shape=(jax.Sha...  13.1 us
    ppermute x4, starting transfers between devices, body(): lax.ppermute(rows, 'space', [(i, i + 2 * hop) for i in range(SPACE) if 0...  12.5 us
    all_to_all x1, waiting for transfers between devices, body(): lax.all_to_all(terms, 'space', 0, 0, tiled=True, axis_index_groups=same_c...  10.8 us
    all_to_all x1, waiting for transfers between devices, body(): lax.all_to_all(whole_sum(grad_scale, scene_terms), 'space', 0, 0, tiled=T...  10.8 us
    all_to_all x1, waiting for transfers between devices, body(): halo_c = lax.all_to_all(outgoing_c, 'space', 0, 0, tiled=True)  10.2 us
    all_to_all x1, starting transfers between devices, body(): halo_c = lax.all_to_all(outgoing_c, 'space', 0, 0, tiled=True)  8.64 us
    all_to_all x1, starting transfers between devices, body(): scene_terms = lax.all_to_all(scene_sum(got_terms), 'dp', 0, 0, tiled=True)  8.17 us
    pallas_call x1, Pallas kernels, kernel_grad(): pl.pallas_call(kernel_grad_kernel, out_shape=jax.ShapeDtypeStruct((CHIPS,...  5.21 us
  transfers between devices with their start and end apart: 12, of which 5 were waited for; matrix products, arithmetic and copies ran while one was open for 1% of the time, Pallas kernels for 19%

profile of v2, /device:TPU:1, one launch (start us, length us, event | category | flops | bytes accessed | tf_op | source)
XLA Modules:
  0.0 106.4 jit_solution(12760582597767250021)
XLA Ops:
  0.6 2.3 %shard_map.67._ = bf16[32,2,64,128]{3,2,1,0:T(8,128)(2,1)} custom-call(s32[27]{0:T(128)} %bitcast.13, bf16[512,256]{1,0:T(8,128)(2,1)} %bitcast.7, bf16[512,256]{1,0:T(8,128)(2,1)} %bitcast.10), custom_call_target="tpu_custom_call" | custom-call | tf_op jit(solution)/shard_map/pallas_call | solution.py:108
  2.9 8.6 %all-to-all-start = ((bf16[32,2,64,128]{3,2,1,0:T(8,128)(2,1)}), bf16[32,2,64,128]{3,2,1,0:T(8,128)(2,1)S(1)}, u32[]{:S(2)}, u32[]{:S(2)}) async-start(bf16[32,2,64,128]{3,2,1,0:T(8,128)(2,1)} %shard_map.67._), calls=%async_computation | async-start | bytes 2097152 | tf_op jit(solution)/shard_map/all_to_all | solution.py:509
  11.6 1.9 %shard_map.68 = bf16[512,384]{1,0:T(8,128)(2,1)} custom-call(bf16[512,256]{1,0:T(8,128)(2,1)} %bitcast.8, bf16[512,256]{1,0:T(8,128)(2,1)} %bitcast.11, bf16[32,2,64,128]{3,2,1,0:T(8,128)(2,1)} %shard_map.67._), custom_call_target="tpu_custom_call" | custom-call | flops 1000000000 | bytes 1048576 | tf_op jit(solution)/shard_map/pallas_call | solution.py:129
  13.5 0.2 collective-permute-start.1
  13.7 0.3 collective-permute-start
  14.0 1.2 %collective-permute-done.mate_links_ref = s32[27]{0:T(128)S(1)} collective-permute-done((s32[27]{0:T(128)S(1)}, s32[27]{0:T(128)S(1)}, u32[]{:S(2)}, u32[]{:S(2)}) %collective-permute-start) | collective-permute-done | bytes 140 | tf_op jit(solution)/shard_map/ppermute | solution.py:507
  15.2 0.2 collective-permute-done.1.pair_ref
  15.4 1.8 %shard_map.69 = (bf16[4,64,128]{2,1,0:T(8,128)(2,1)S(1)}, bf16[4,64,128]{2,1,0:T(8,128)(2,1)S(1)}, bf16[4,64,128]{2,1,0:T(8,128)(2,1)S(1)}, bf16[4,64,128]{2,1,0...) custom-call(s32[27]{0:T(128)S(1)} %bitcast.17, ...), custom_call_target="tpu_custom_call" | custom-call | flops 2500000000 | bytes 1048576 | tf_op jit(solution)/shard_map/pallas_call | solution.py:179
  17.3 0.7 copy-done.5
  18.0 0.6 copy-done.7
  18.6 10.2 %all-to-all-done.halo_ref = bf16[32,2,64,128]{3,2,1,0:T(8,128)(2,1)S(1)} async-done(((bf16[32,2,64,128]{3,2,1,0:T(8,128)(2,1)}), bf16[32,2,64,128]{3,2,1,0:T(8,128)(2,1)S(1)}, u32[]{:S(2)}, u32[]{:S(2)}) %all-to-all-start) | async-done | bytes 1048608 | tf_op jit(solution)/shard_map/all_to_all | solution.py:509
  28.8 5.2 %shard_map.70.rest_0_ = s16[16,448,128]{2,1,0:T(8,128)(2,1)} custom-call(s32[27]{0:T(128)S(1)} %bitcast.18, s32[27]{0:T(128)S(1)} %collective-permute-done.mate_links_ref, bf16[2,512,128]{2,1,0:T(8,128)(2,1)S(1)} %get-tuple-element.21.c_half_ref.half_ref, bf16[2,256,512]{2,1,0:T(8,128)(2,1)S(1)} %get-tuple-element.22.turned_ref, ...), custom_call_target="tpu_custom_call" | custom-call | flops 6000000000 | bytes 1048576 | tf_op jit(solution)/shard_map/pallas_call | solution.py:318
  34.0 3.7 %all-to-all-start.1 = ((s16[16,448,128]{2,1,0:T(8,128)(2,1)}), s16[16,448,128]{2,1,0:T(8,128)(2,1)S(1)}, u32[]{:S(2)}, u32[]{:S(2)}) async-start(s16[16,448,128]{2,1,0:T(8,128)(2,1)} %shard_map.70.rest_0_), calls=%async_computation.1 | async-start | bytes 3670016 | tf_op jit(solution)/shard_map/all_to_all | solution.py:517
  37.7 1.3 %collective-permute-start.2 = (bf16[4,64,128]{2,1,0:T(8,128)(2,1)S(1)}, bf16[4,64,128]{2,1,0:T(8,128)(2,1)S(1)}, u32[]{:S(2)}, u32[]{:S(2)}) collective-permute-start(bf16[4,64,128]{2,1,0:T(8,128)(2,1)S(1)} %get-tuple-element.27), channel_id=1, source_target_pairs={{32,0},{40,8},{48,16},{56,24},{64,32},{72,40},{80,48},{88,56},{96,... | collective-permute-start | bytes 196616 | tf_op jit(solution)/shard_map/ppermute | solution.py:513
  39.0 1.3 %collective-permute-start.3 = (bf16[4,64,128]{2,1,0:T(8,128)(2,1)S(1)}, bf16[4,64,128]{2,1,0:T(8,128)(2,1)S(1)}, u32[]{:S(2)}, u32[]{:S(2)}) collective-permute-start(bf16[4,64,128]{2,1,0:T(8,128)(2,1)S(1)} %get-tuple-element.28), channel_id=1, source_target_pairs={{16,0},{24,8},{32,16},{40,24},{48,32},{56,40},{64,48},{72,56},{80,... | collective-permute-start | bytes 196616 | tf_op jit(solution)/shard_map/ppermute | solution.py:513
  40.3 4.0 %collective-permute-start.4 = (bf16[4,64,128]{2,1,0:T(8,128)(2,1)S(1)}, bf16[4,64,128]{2,1,0:T(8,128)(2,1)S(1)}, u32[]{:S(2)}, u32[]{:S(2)}) collective-permute-start(bf16[4,64,128]{2,1,0:T(8,128)(2,1)S(1)} %get-tuple-element.29), channel_id=1, source_target_pairs={{0,16},{8,24},{16,32},{24,40},{32,48},{40,56},{48,64},{56,72},{64,... | collective-permute-start | bytes 196616 | tf_op jit(solution)/shard_map/ppermute | solution.py:513
  44.3 5.9 %collective-permute-start.5 = (bf16[4,64,128]{2,1,0:T(8,128)(2,1)S(1)}, bf16[4,64,128]{2,1,0:T(8,128)(2,1)S(1)}, u32[]{:S(2)}, u32[]{:S(2)}) collective-permute-start(bf16[4,64,128]{2,1,0:T(8,128)(2,1)S(1)} %get-tuple-element.30), channel_id=1, source_target_pairs={{0,32},{8,40},{16,48},{24,56},{32,64},{40,72},{48,80},{56,88},{64,... | collective-permute-start | bytes 196616 | tf_op jit(solution)/shard_map/ppermute | solution.py:513
  50.2 6.2 %shard_map.71 = (f32[512,256]{1,0:T(8,128)}, f32[512,256]{1,0:T(8,128)}) custom-call(s32[27]{0:T(128)} %bitcast.14, s32[27]{0:T(128)} %copy-done.4, bf16[2,512,128]{2,1,0:T(8,128)(2,1)} %copy-done.6, bf16[27,256,256]{2,1,0:T(8,128)(2,1)} %weight_ref.3, bf16[32,2,64,128]{3,2,1,0:T(8,128)(2,1)} %copy-done, s16[16,448,128]{2,1,0:T(8,128)(2,1)} %shard_map.70.rest_0_), custom_call_target="tpu_custom_call" | custom-call | flops 6000000000 | bytes 1048576 | tf_op jit(solution)/shard_map/pallas_call | solution.py:392
  56.5 10.8 %all-to-all-done.1.got_ref = s16[16,448,128]{2,1,0:T(8,128)(2,1)S(1)} async-done(((s16[16,448,128]{2,1,0:T(8,128)(2,1)}), s16[16,448,128]{2,1,0:T(8,128)(2,1)S(1)}, u32[]{:S(2)}, u32[]{:S(2)}) %all-to-all-start.1) | async-done | bytes 1835040 | tf_op jit(solution)/shard_map/all_to_all | solution.py:517
  67.3 1.3 %shard_map.72 = s16[8,64,128]{2,1,0:T(8,128)(2,1)} custom-call(s16[16,448,128]{2,1,0:T(8,128)(2,1)S(1)} %all-to-all-done.1.got_ref), custom_call_target="tpu_custom_call" | custom-call | flops 2500000000 | bytes 1048576 | tf_op jit(solution)/shard_map/pallas_call | solution.py:434
  68.6 8.2 %all-to-all-start.2 = ((s16[8,64,128]{2,1,0:T(8,128)(2,1)}), s16[8,64,128]{2,1,0:T(8,128)(2,1)S(1)}, u32[]{:S(2)}, u32[]{:S(2)}) async-start(s16[8,64,128]{2,1,0:T(8,128)(2,1)} %shard_map.72), calls=%async_computation.2 | async-start | bytes 262144 | tf_op jit(solution)/shard_map/all_to_all | solution.py:520
  76.8 2.4 %collective-permute-start.7 = (f32[512,256]{1,0:T(8,128)S(1)}, f32[512,256]{1,0:T(8,128)S(1)}, u32[]{:S(2)}, u32[]{:S(2)}) collective-permute-start(f32[512,256]{1,0:T(8,128)S(1)} %copy-done.10), channel_id=1, source_target_pairs={{0,8},{8,0},{16,24},{24,16},{32,40},{40,32},{48,56},{56,48},{64,72... | collective-permute-start | bytes 1572872 | tf_op jit(solution)/shard_map/ppermute | solution.py:524
  79.3 0.6 copy-done.11
  79.8 0.0 copy-done.12
  79.9 6.8 %shard_map.73 = (f32[512,256]{1,0:T(8,128)}, f32[512,256]{1,0:T(8,128)}) custom-call(s32[27]{0:T(128)} %bitcast.15, s32[27]{0:T(128)} %copy-done.4, bf16[2,512,128]{2,1,0:T(8,128)(2,1)} %copy-done.5, bf16[27,256,256]{2,1,0:T(8,128)(2,1)} %weight_ref.3, bf16[32,2,64,128]{3,2,1,0:T(8,128)(2,1)} %copy-done, bf16[4,64,128]{2,1,0:T(8,128)(2,1)} %copy-done.11, ...), custom_call_target="tpu_custom_call" | custom-call | flops 6000000000 | bytes 1048576 | tf_op jit(solution)/shard_map/pallas_call | solution.py:392
  86.8 1.4 %collective-permute-start.6 = (f32[512,256]{1,0:T(8,128)}, f32[512,256]{1,0:T(8,128)S(1)}, u32[]{:S(2)}, u32[]{:S(2)}) collective-permute-start(f32[512,256]{1,0:T(8,128)} %get-tuple-element.35), channel_id=1, source_target_pairs={{0,8},{8,0},{16,24},{24,16},{32,40},{40,32},{48,56},{56,48},{64,72... | collective-permute-start | bytes 1572872 | tf_op jit(solution)/shard_map/ppermute | solution.py:525
  88.2 0.9 shard_map.74
  89.1 3.8 %all-to-all-start.3 = ((s16[32,64,128]{2,1,0:T(8,128)(2,1)}), s16[32,64,128]{2,1,0:T(8,128)(2,1)S(1)}, u32[]{:S(2)}, u32[]{:S(2)}) async-start(s16[32,64,128]{2,1,0:T(8,128)(2,1)} %shard_map.74), calls=%async_computation.3 | async-start | bytes 1048576 | tf_op jit(solution)/shard_map/all_to_all | solution.py:523
  93.0 0.8 fusion.1
  93.8 10.8 %all-to-all-done.3.got_ref = s16[32,64,128]{2,1,0:T(8,128)(2,1)S(1)} async-done(((s16[32,64,128]{2,1,0:T(8,128)(2,1)}), s16[32,64,128]{2,1,0:T(8,128)(2,1)S(1)}, u32[]{:S(2)}, u32[]{:S(2)}) %all-to-all-start.3) | async-done | bytes 524320 | tf_op jit(solution)/shard_map/all_to_all | solution.py:523
  104.5 1.0 shard_map.75
  105.6 0.8 fusion
  (33 shorter events, 0.1 us)
Async XLA Ops:
  2.9 25.8 %all-to-all-start = ((bf16[32,2,64,128]{3,2,1,0:T(8,128)(2,1)}), bf16[32,2,64,128]{3,2,1,0:T(8,128)(2,1)S(1)}, u32[]{:S(2)}, u32[]{:S(2)}) async-start(bf16[32,2,64,128]{3,2,1,0:T(8,128)(2,1)} %shard_map.67._), calls=%async_computation | async-start | bytes 2097152 | tf_op jit(solution)/shard_map/all_to_all | solution.py:509
  11.6 2.1 %copy-start.3 = (s32[1,1,27]{2,1,0:T(1,128)S(1)}, s32[1,1,27]{2,1,0:T(1,128)}, u32[]{:S(2)}) copy-start(s32[1,1,27]{2,1,0:T(1,128)} %param.7) | copy-start | bytes 328
  11.6 3.8 %copy-start.1 = (bf16[1,1,512,256]{3,2,1,0:T(8,128)(2,1)S(1)}, bf16[1,1,512,256]{3,2,1,0:T(8,128)(2,1)}, u32[]{:S(2)}) copy-start(bf16[1,1,512,256]{3,2,1,0:T(8,128)(2,1)} %param.4) | copy-start | bytes 786436
  11.6 3.8 %copy-start.2 = (bf16[1,1,512,256]{3,2,1,0:T(8,128)(2,1)S(1)}, bf16[1,1,512,256]{3,2,1,0:T(8,128)(2,1)}, u32[]{:S(2)}) copy-start(bf16[1,1,512,256]{3,2,1,0:T(8,128)(2,1)} %param.5) | copy-start | bytes 786436
  13.5 1.9 %collective-permute-start.1 = (bf16[512,384]{1,0:T(8,128)(2,1)}, bf16[512,384]{1,0:T(8,128)(2,1)S(1)}, u32[]{:S(2)}, u32[]{:S(2)}) collective-permute-start(bf16[512,384]{1,0:T(8,128)(2,1)} %shard_map.68), channel_id=1, source_target_pairs={{0,8},{8,0},{16,24},{24,16},{32,40},{40,32},{48,56},{56,48},{64,72... | collective-permute-start | bytes 1179656 | tf_op jit(solution)/shard_map/ppermute | solution.py:510
  13.7 1.4 %collective-permute-start = (s32[27]{0:T(128)S(1)}, s32[27]{0:T(128)S(1)}, u32[]{:S(2)}, u32[]{:S(2)}) collective-permute-start(s32[27]{0:T(128)S(1)} %bitcast.16), channel_id=1, source_target_pairs={{0,8},{8,0},{16,24},{24,16},{32,40},{40,32},{48,56},{56,48},{64,72... | collective-permute-start | bytes 332 | tf_op jit(solution)/shard_map/ppermute | solution.py:507
  15.2 13.6 %copy-start.4 = (s32[27]{0:T(128)}, s32[27]{0:T(128)S(1)}, u32[]{:S(2)}) copy-start(s32[27]{0:T(128)S(1)} %collective-permute-done.mate_links_ref) | copy-start | bytes 328
  17.3 0.7 copy-start.5
  18.0 0.6 copy-start.7
  18.6 15.4 %copy-start.6 = (bf16[2,512,128]{2,1,0:T(8,128)(2,1)}, bf16[2,512,128]{2,1,0:T(8,128)(2,1)S(1)}, u32[]{:S(2)}) copy-start(bf16[2,512,128]{2,1,0:T(8,128)(2,1)S(1)} %get-tuple-element.21.c_half_ref.half_ref) | copy-start | bytes 786436
  28.8 5.2 %copy-start = (bf16[32,2,64,128]{3,2,1,0:T(8,128)(2,1)}, bf16[32,2,64,128]{3,2,1,0:T(8,128)(2,1)S(1)}, u32[]{:S(2)}) copy-start(bf16[32,2,64,128]{3,2,1,0:T(8,128)(2,1)S(1)} %all-to-all-done.halo_ref) | copy-start | bytes 3145732
  34.0 33.3 %all-to-all-start.1 = ((s16[16,448,128]{2,1,0:T(8,128)(2,1)}), s16[16,448,128]{2,1,0:T(8,128)(2,1)S(1)}, u32[]{:S(2)}, u32[]{:S(2)}) async-start(s16[16,448,128]{2,1,0:T(8,128)(2,1)} %shard_map.70.rest_0_), calls=%async_computation.1 | async-start | bytes 3670016 | tf_op jit(solution)/shard_map/all_to_all | solution.py:517
  37.7 41.5 %collective-permute-start.2 = (bf16[4,64,128]{2,1,0:T(8,128)(2,1)S(1)}, bf16[4,64,128]{2,1,0:T(8,128)(2,1)S(1)}, u32[]{:S(2)}, u32[]{:S(2)}) collective-permute-start(bf16[4,64,128]{2,1,0:T(8,128)(2,1)S(1)} %get-tuple-element.27), channel_id=1, source_target_pairs={{32,0},{40,8},{48,16},{56,24},{64,32},{72,40},{80,48},{88,56},{96,... | collective-permute-start | bytes 196616 | tf_op jit(solution)/shard_map/ppermute | solution.py:513
  39.0 40.2 %collective-permute-start.3 = (bf16[4,64,128]{2,1,0:T(8,128)(2,1)S(1)}, bf16[4,64,128]{2,1,0:T(8,128)(2,1)S(1)}, u32[]{:S(2)}, u32[]{:S(2)}) collective-permute-start(bf16[4,64,128]{2,1,0:T(8,128)(2,1)S(1)} %get-tuple-element.28), channel_id=1, source_target_pairs={{16,0},{24,8},{32,16},{40,24},{48,32},{56,40},{64,48},{72,56},{80,... | collective-permute-start | bytes 196616 | tf_op jit(solution)/shard_map/ppermute | solution.py:513
  40.3 38.9 %collective-permute-start.4 = (bf16[4,64,128]{2,1,0:T(8,128)(2,1)S(1)}, bf16[4,64,128]{2,1,0:T(8,128)(2,1)S(1)}, u32[]{:S(2)}, u32[]{:S(2)}) collective-permute-start(bf16[4,64,128]{2,1,0:T(8,128)(2,1)S(1)} %get-tuple-element.29), channel_id=1, source_target_pairs={{0,16},{8,24},{16,32},{24,40},{32,48},{40,56},{48,64},{56,72},{64,... | collective-permute-start | bytes 196616 | tf_op jit(solution)/shard_map/ppermute | solution.py:513
  44.3 34.9 %collective-permute-start.5 = (bf16[4,64,128]{2,1,0:T(8,128)(2,1)S(1)}, bf16[4,64,128]{2,1,0:T(8,128)(2,1)S(1)}, u32[]{:S(2)}, u32[]{:S(2)}) collective-permute-start(bf16[4,64,128]{2,1,0:T(8,128)(2,1)S(1)} %get-tuple-element.30), channel_id=1, source_target_pairs={{0,32},{8,40},{16,48},{24,56},{32,64},{40,72},{48,80},{56,88},{64,... | collective-permute-start | bytes 196616 | tf_op jit(solution)/shard_map/ppermute | solution.py:513
  67.3 9.5 %copy-start.10 = (f32[512,256]{1,0:T(8,128)S(1)}, f32[512,256]{1,0:T(8,128)}, u32[]{:S(2)}) copy-start(f32[512,256]{1,0:T(8,128)} %get-tuple-element.37) | copy-start | bytes 1572868
  68.6 18.2 %all-to-all-start.2 = ((s16[8,64,128]{2,1,0:T(8,128)(2,1)}), s16[8,64,128]{2,1,0:T(8,128)(2,1)S(1)}, u32[]{:S(2)}, u32[]{:S(2)}) async-start(s16[8,64,128]{2,1,0:T(8,128)(2,1)} %shard_map.72), calls=%async_computation.2 | async-start | bytes 262144 | tf_op jit(solution)/shard_map/all_to_all | solution.py:520
  76.8 16.2 %collective-permute-start.7 = (f32[512,256]{1,0:T(8,128)S(1)}, f32[512,256]{1,0:T(8,128)S(1)}, u32[]{:S(2)}, u32[]{:S(2)}) collective-permute-start(f32[512,256]{1,0:T(8,128)S(1)} %copy-done.10), channel_id=1, source_target_pairs={{0,8},{8,0},{16,24},{24,16},{32,40},{40,32},{48,56},{56,48},{64,72... | collective-permute-start | bytes 1572872 | tf_op jit(solution)/shard_map/ppermute | solution.py:524
  79.2 0.6 copy-start.11
  79.2 0.7 copy-start.12
  79.2 0.7 copy-start.13
  79.3 0.7 copy-start.14
  86.8 6.2 %copy-start.8 = (f32[512,256]{1,0:T(8,128)S(1)}, f32[512,256]{1,0:T(8,128)}, u32[]{:S(2)}) copy-start(f32[512,256]{1,0:T(8,128)} %get-tuple-element.36) | copy-start | bytes 1572868
  86.8 18.8 %collective-permute-start.6 = (f32[512,256]{1,0:T(8,128)}, f32[512,256]{1,0:T(8,128)S(1)}, u32[]{:S(2)}, u32[]{:S(2)}) collective-permute-start(f32[512,256]{1,0:T(8,128)} %get-tuple-element.35), channel_id=1, source_target_pairs={{0,8},{8,0},{16,24},{24,16},{32,40},{40,32},{48,56},{56,48},{64,72... | collective-permute-start | bytes 1572872 | tf_op jit(solution)/shard_map/ppermute | solution.py:525
  89.1 16.5 %copy-start.9 = (f32[512,256]{1,0:T(8,128)S(1)}, f32[512,256]{1,0:T(8,128)}, u32[]{:S(2)}) copy-start(f32[512,256]{1,0:T(8,128)} %get-tuple-element.34) | copy-start | bytes 1572868
  89.1 15.4 %all-to-all-start.3 = ((s16[32,64,128]{2,1,0:T(8,128)(2,1)}), s16[32,64,128]{2,1,0:T(8,128)(2,1)S(1)}, u32[]{:S(2)}, u32[]{:S(2)}) async-start(s16[32,64,128]{2,1,0:T(8,128)(2,1)} %shard_map.74), calls=%async_computation.3 | async-start | bytes 1048576 | tf_op jit(solution)/shard_map/all_to_all | solution.py:523

commit v3 on v2

--- a/solution.py
+++ b/solution.py
@@ -14,15 +14,17 @@
 i32 = jnp.int32
 
 SPACE = 32
-LG, LS, LW, LP = 51, 50, 50, 51
+LG, LS, LW, LP, LQ = 51, 50, 50, 51, 51
 
 SCENES = 8
 CHIPS = 16
 HALF = 128
 LEVELS = 32766.0
 
-FAR = 3
-HOPS = (-2, -1, 1, 2)
+ROWS = (256, 192, 64, 16)
+FIRST = (0, 256, 448, 512)
+BELOW = 528
+HERE = 1056
 
 OFFSETS = [(k, k // 9 - 1, k // 3 % 3 - 1, k % 3 - 1) for k in range(27) if k != 13]
 
@@ -80,117 +82,112 @@
     return jnp.concatenate([rows, rows], axis=0)
 
 
-def pack_kernel(links_ref, x_ref, c_ref, out_ref, parts):
-    chip = position()[0] // 2
-    for half in range(2):
-        lanes = slice(half * HALF, (half + 1) * HALF)
-        parts[half] = c_ref[:, lanes].astype(f32)
-        parts[2 + half] = x_ref[:, lanes].astype(f32)
-    for k, *shifts in OFFSETS:
-        target = links_ref[k]
-
-        @pl.when(target >= 0)
-        def _(target=target, shifts=tuple(shifts)):
-            to = target // 2
-            brick = lax.rem(target, 2)
-            for half in range(2):
-                rows = region(parts.at[half], shifts)
-                out_ref[2 * to + half, brick, 0 : rows.shape[0], :] = rows.astype(bf16)
-            if sum(map(abs, shifts)) > 1:
-
-                @pl.when(jnp.abs(to - chip) >= FAR)
-                def _():
-                    for half in range(2):
-                        out_ref[2 * to + half, brick, 16:32, :] = region(parts.at[2 + half], shifts).astype(bf16)
-
-
-def pack(links, x, c):
-    return pl.pallas_call(
-        pack_kernel,
-        out_shape=jax.ShapeDtypeStruct((SPACE, 2, 64, HALF), bf16),
-        in_specs=[smem(), vmem(), vmem()],
-        out_specs=vmem(),
-        scratch_shapes=[pltpu.VMEM((4, 512, HALF), f32)],
-        compiler_params=params(56),
-    )(links, x, c)
-
-
-def pair_kernel(x_ref, c_ref, _, out_ref):
-    core = lax.rem(position()[0], 2)
-    out_ref[:, 0:256] = x_ref[...]
-    for here in range(2):
-
-        @pl.when(core == here)
-        def _(here=here):
-            out_ref[:, 256:384] = c_ref[:, (1 - here) * HALF : (2 - here) * HALF]
-
-
-def pair_rows(x, c, after):
-    return pl.pallas_call(
-        pair_kernel,
-        out_shape=jax.ShapeDtypeStruct((512, 384), bf16),
-        in_specs=[vmem(), vmem(), anywhere()],
-        out_specs=vmem(),
-        compiler_params=params(56),
-        cost_estimate=cost(1.0),
-    )(x, c, after)
-
-
-def prepare_kernel(links_ref, mate_links_ref, x_ref, c_ref, pair_ref, *rest):
-    outs, turned_ref, x_half_ref, c_half_ref, parts, slots, sems = rest[:5], *rest[5:]
+def is_face(shifts):
+    return sum(map(abs, shifts)) == 1
+
+
+def reach(shifts):
+    return abs(shifts[0] + 2 * shifts[1] + 4 * shifts[2])
+
+
+def place_in_slots(distance, shifts, source, target):
+    if distance <= 1:
+        return 64 * (2 * source + target)
+    if distance == 2:
+        return 96 * source + (0 if is_face(shifts) else 64 + 16 * target)
+    return 16 * (2 * source + target) if distance == 3 else 0
+
+
+def pack_kernel(links_ref, mate_links_ref, own_ref, mate_x_ref, mate_c_ref, *rest):
+    outs, parts = rest[:4], rest[4]
     own = position()[0]
     core = lax.rem(own, 2)
     chip = own // 2
-    mate = 1 - core
+    for group in range(4):
+        lanes = slice(group * HALF, (group + 1) * HALF)
+        parts[core, group] = own_ref[:, lanes].astype(f32)
+        mate_ref, at = (mate_x_ref, lanes) if group < 2 else (mate_c_ref, slice(lanes.start - 256, lanes.stop - 256))
+        parts[1 - core, group] = mate_ref[:, at].astype(f32)
+    for brick in range(2):
+        for k, *shifts in OFFSETS:
+            target = jnp.where(core == brick, links_ref[k], mate_links_ref[k])
+            distance = (target // 2 - chip) * (1 - 2 * core)
+            to = lax.rem(target, 2)
+
+            @pl.when((target >= 0) & (distance > 0))
+            def _(brick=brick, distance=distance, to=to, shifts=tuple(shifts)):
+                for step in range(1, 5):
+                    if reach(shifts) >= 2 * step - 1:
+
+                        @pl.when(distance == step)
+                        def _(step=step):
+                            at = pl.multiple_of(place_in_slots(step, shifts, brick, to), 16)
+                            for group in range(4):
+                                rows = region(parts.at[brick, group], shifts)
+                                lanes = slice(group * HALF, (group + 1) * HALF)
+                                outs[step - 1][pl.ds(at, rows.shape[0]), lanes] = rows.astype(bf16)
+
+
+def pack(links, mate_links, own, mate_x, mate_c):
+    return pl.pallas_call(
+        pack_kernel,
+        out_shape=tuple(jax.ShapeDtypeStruct((rows, 512), bf16) for rows in ROWS),
+        in_specs=[smem(), smem()] + [vmem()] * 3,
+        out_specs=(vmem(),) * 4,
+        scratch_shapes=[pltpu.VMEM((2, 4, 512, HALF), f32)],
+        compiler_params=params(LQ),
+        cost_estimate=cost(2.5),
+    )(links, mate_links, own, mate_x, mate_c)
+
+
+def stage_kernel(
+    links_ref, mate_links_ref, own_ref, mate_x_ref, mate_c_ref, _, here_ref, turned_ref, x_half_ref, c_half_ref, parts
+):
+    own = position()[0]
+    core = lax.rem(own, 2)
     for here in range(2):
 
         @pl.when(core == here)
         def _(here=here):
             lanes = slice(here * HALF, (here + 1) * HALF)
-            x_half_ref[here] = x_ref[:, lanes]
-            x_half_ref[1 - here] = pair_ref[:, lanes]
-            c_half_ref[here] = c_ref[:, lanes]
-            c_half_ref[1 - here] = pair_ref[:, 256:384]
-
-    turned_ref[core] = x_ref[...].T
-    turned_ref[mate] = pair_ref[:, 0:256].T
+            x_half_ref[here] = own_ref[:, lanes]
+            x_half_ref[1 - here] = mate_x_ref[:, lanes]
+            c_half_ref[here] = own_ref[:, 256 + here * HALF : 256 + (here + 1) * HALF]
+            c_half_ref[1 - here] = mate_c_ref[:, lanes]
+
     for brick in range(2):
-        parts[brick] = x_half_ref[brick].astype(f32)
+        parts[brick, 0] = x_half_ref[brick].astype(f32)
+        parts[brick, 1] = c_half_ref[brick].astype(f32)
         for k, *shifts in OFFSETS:
             target = jnp.where(core == brick, links_ref[k], mate_links_ref[k])
 
-            @pl.when(target >= 0)
+            @pl.when((target >= 0) & (target // 2 == own // 2))
             def _(brick=brick, target=target, shifts=tuple(shifts)):
-                rows = region(parts.at[brick], shifts)
-                slots[target // 2 - chip + 4, 2 * brick + lax.rem(target, 2), 0 : rows.shape[0], :] = rows.astype(bf16)
-
-    copies = [
-        pltpu.make_async_copy(slots.at[hop + 4], out, sems.at[n])
-        for n, (hop, out) in enumerate(zip(HOPS + (0,), outs))
-    ]
-    for copy in copies:
-        copy.start()
-    for copy in copies:
-        copy.wait()
-
-
-def prepare(links, mate_links, x, c, pair):
+                at = pl.multiple_of(place_in_slots(0, shifts, brick, lax.rem(target, 2)), 16)
+                for tensor in range(2):
+                    rows = region(parts.at[brick, tensor], shifts)
+                    here_ref[pl.ds(at, rows.shape[0]), tensor * HALF : (tensor + 1) * HALF] = rows.astype(bf16)
+
+    turned_ref[core] = own_ref[:, 0:256].T
+    turned_ref[1 - core] = mate_x_ref[...].T
+
+
+def stage(links, mate_links, own, mate_x, mate_c, after):
     half = jax.ShapeDtypeStruct((2, 512, HALF), bf16)
-    got = pl.pallas_call(
-        prepare_kernel,
-        out_shape=tuple(jax.ShapeDtypeStruct((4, 64, HALF), bf16) for hop in HOPS + (0,))
-        + (jax.ShapeDtypeStruct((2, 256, 512), bf16), half, half),
-        in_specs=[smem(), smem(), vmem(), vmem(), vmem()],
-        out_specs=(anywhere(),) * 5 + (vmem(),) * 3,
-        scratch_shapes=[
-            pltpu.VMEM((2, 512, HALF), f32),
-            pltpu.VMEM((9, 4, 64, HALF), bf16),
-            pltpu.SemaphoreType.DMA((5,)),
-        ],
+    return pl.pallas_call(
+        stage_kernel,
+        out_shape=(
+            jax.ShapeDtypeStruct((256, 256), bf16),
+            jax.ShapeDtypeStruct((2, 256, 512), bf16),
+            half,
+            half,
+        ),
+        in_specs=[smem(), smem()] + [vmem()] * 3 + [anywhere()],
+        out_specs=(vmem(),) * 4,
+        scratch_shapes=[pltpu.VMEM((2, 2, 512, HALF), f32)],
         compiler_params=params(LP),
-        cost_estimate=cost(2.5),
-    )(links, mate_links, x, c, pair)
-    return got[:5], *got[5:]
+        cost_estimate=cost(1.5),
+    )(links, mate_links, own, mate_x, mate_c, after)
 
 
 def target_plane(shift):
@@ -224,10 +221,10 @@
         source = links[k]
 
         @pl.when(source >= 0)
-        def _(source=source, k=k, dx=dx, dy=dy, dz=dz):
+        def _(source=source, dx=dx, dy=dy, dz=dz):
             at_x, at_y = target_plane(dx), target_plane(dy)
             face = (dx != 0) + (dy != 0) + (dz != 0) == 1
-            got = fetch(source, brick, k, 64 if face else 16).astype(f32)
+            got = fetch(source, brick, (dx, dy, dz), 64 if face else 16).astype(f32)
             if dz == 0:
                 if dy == 0:
                     plane[pl.ds(at_x * 80 + 8, 64), :] = got
@@ -268,10 +265,34 @@
         fill(brick, [jnp.where(core == brick, links_ref[k], mate_links_ref[k]) for k in range(27)], fetch, rows, *scratch)
 
 
-def by_distance(halo_ref, chip):
-    return lambda source, brick, k, count: halo_ref[source // 2 - chip + 4, 2 * lax.rem(source, 2) + brick, 0:count, :]
-
-
+def take_halos(tensor, own, halos, slots, sems):
+    core = lax.rem(own, 2)
+    chip = own // 2
+    lanes = pl.ds(pl.multiple_of(2 * tensor * HALF + core * HALF, HALF), HALF)
+    copies = []
+    for n, (halo, rows, first) in enumerate(zip(halos[:8], ROWS * 2, FIRST * 2)):
+        side = (1 - core) if n < 4 else core
+        at = pl.multiple_of(side * BELOW + first, 16)
+        copies.append(pltpu.make_async_copy(halo.at[:, lanes], slots.at[pl.ds(at, rows), :], sems.at[n]))
+    copies.append(
+        pltpu.make_async_copy(halos[8].at[:, pl.ds(tensor * HALF, HALF)], slots.at[pl.ds(HERE, 256), :], sems.at[8])
+    )
+
+    def fetch(source, brick, shifts, count):
+        apart = source // 2 - chip
+        distance = jnp.abs(apart)
+        source = lax.rem(source, 2)
+        at = HERE + place_in_slots(0, shifts, source, brick)
+        for step in range(1, 5):
+            if reach(shifts) >= 2 * step - 1:
+                there = FIRST[step - 1] + place_in_slots(step, shifts, source, brick)
+                at = jnp.where(distance == step, there + jnp.where(apart < 0, BELOW, 0), at)
+        return slots[pl.ds(pl.multiple_of(at, 16), count), :]
+
+    return copies, fetch
+
+
+HALO_SCRATCH = [pltpu.VMEM((HERE + 256, HALF), bf16), pltpu.SemaphoreType.DMA((9,))]
 FILL_SCRATCH = [
     pltpu.VMEM((832, HALF), f32),
     pltpu.VMEM((104, HALF), f32),
@@ -282,14 +303,16 @@
 ]
 
 
-def by_device(halo_ref):
-    return lambda source, brick, k, count: halo_ref[source, brick, 0:count, :]
-
-
-def kernel_grad_kernel(links_ref, mate_links_ref, c_half_ref, turned_ref, halo_ref, terms_ref, grads, coded, sems, *scratch):
-    core = lax.rem(position()[0], 2)
+def kernel_grad_kernel(links_ref, mate_links_ref, c_half_ref, turned_ref, *rest):
+    halos, (terms_ref, grads, coded, sems, slots, halo_sems, *scratch) = rest[:9], rest[9:]
+    own = position()[0]
     padded = scratch[-1]
-    fill_both(core, links_ref, mate_links_ref, c_half_ref, by_device(halo_ref), scratch)
+    halo_copies, fetch = take_halos(1, own, halos, slots, halo_sems)
+    for copy in halo_copies:
+        copy.start()
+    for copy in halo_copies:
+        copy.wait()
+    fill_both(lax.rem(own, 2), links_ref, mate_links_ref, c_half_ref, fetch, scratch)
     for i in range(3):
         window = slice(i * 64, i * 64 + 512)
         term = jnp.dot(turned_ref[0], padded[0, window, :], preferred_element_type=f32)
@@ -314,31 +337,31 @@
         copy.wait()
 
 
-def kernel_grad(links, mate_links, c_half, turned, halo):
+def kernel_grad(links, mate_links, c_half, turned, halos):
     return pl.pallas_call(
         kernel_grad_kernel,
         out_shape=jax.ShapeDtypeStruct((CHIPS, 448, HALF), i16),
-        in_specs=[smem(), smem(), vmem(), vmem(), vmem()],
+        in_specs=[smem(), smem(), vmem(), vmem()] + [anywhere()] * 9,
         out_specs=anywhere(),
         scratch_shapes=[
             pltpu.VMEM((27, 256, HALF), f32),
             pltpu.VMEM((CHIPS, 448, HALF), i16),
             pltpu.SemaphoreType.DMA((CHIPS,)),
         ]
+        + HALO_SCRATCH
         + FILL_SCRATCH,
         compiler_params=params(LG),
         cost_estimate=cost(6.0),
-    )(links, mate_links, c_half, turned, halo)
-
-
-def taps_kernel(turned, links_ref, mate_links_ref, half_ref, weight_ref, halo_ref, *rest):
+    )(links, mate_links, c_half, turned, *halos)
+
+
+def taps_kernel(turned, links_ref, mate_links_ref, half_ref, weight_ref, *rest):
+    halos, (_, out_ref, mate_out_ref, taps, sems, slots, halo_sems, *scratch) = rest[:9], rest[9:]
     own = position()[0]
     core = lax.rem(own, 2)
     start = pl.multiple_of(core * HALF, HALF)
+    halo_copies, fetch = take_halos(1 if turned else 0, own, halos, slots, halo_sems)
     if turned:
-        _, out_ref, mate_out_ref, taps, sems, *scratch = rest
-        fetch = by_device(halo_ref)
-        halo_copies = []
         copies = [
             pltpu.make_async_copy(
                 weight_ref.at[26 - k, :, pl.ds(start, HALF)], taps.at[:, pl.ds(k * HALF, HALF)], sems.at[k]
@@ -346,23 +369,6 @@
             for k in range(27)
         ]
     else:
-        halos, (out_ref, mate_out_ref, taps, sems, slots, far_sems, *scratch) = rest[:5], rest[5:]
-        chip = own // 2
-        fetch = by_distance(slots, chip)
-        halo_copies = [
-            pltpu.make_async_copy(halo, slots.at[4 - hop], sems.at[1 + n])
-            for n, (hop, halo) in enumerate(zip(HOPS + (0,), halos))
-        ]
-        for hop in (-4, -3, 3, 4):
-            source = jnp.clip(chip + hop, 0, CHIPS - 1)
-            for side_by in range(4):
-                halo_copies.append(
-                    pltpu.make_async_copy(
-                        halo_ref.at[2 * source + side_by // 2, side_by % 2, pl.ds(16, 16), :],
-                        slots.at[4 + hop, side_by, pl.ds(0, 16), :],
-                        far_sems.at[4 + hop, side_by],
-                    )
-                )
         copies = [pltpu.make_async_copy(weight_ref.at[:, pl.ds(start, HALF), :], taps, sems.at[0])]
     padded = scratch[-1]
     for copy in halo_copies + copies:
@@ -386,18 +392,17 @@
         out[...] = total
 
 
-def taps_product(turned, links, mate_links, half, weight, halo, *rest):
+def taps_product(turned, links, mate_links, half, weight, halos, after):
     taps = pltpu.VMEM((256, 27 * HALF) if turned else (27, HALF, 256), bf16)
-    slots = [] if turned else [pltpu.VMEM((9, 4, 64, HALF), bf16), pltpu.SemaphoreType.DMA((9, 4))]
     return pl.pallas_call(
         functools.partial(taps_kernel, turned),
         out_shape=(jax.ShapeDtypeStruct((512, 256), f32),) * 2,
-        in_specs=[smem(), smem(), vmem(), hbm(), vmem() if turned else hbm()] + [anywhere()] * len(rest),
+        in_specs=[smem(), smem(), vmem(), hbm()] + [anywhere()] * 10,
         out_specs=(vmem(), vmem()),
-        scratch_shapes=[taps, pltpu.SemaphoreType.DMA((28,))] + slots + FILL_SCRATCH,
+        scratch_shapes=[taps, pltpu.SemaphoreType.DMA((27,))] + HALO_SCRATCH + FILL_SCRATCH,
         compiler_params=params(56),
         cost_estimate=cost(6.0),
-    )(links, mate_links, half, weight, halo, *rest)
+    )(links, mate_links, half, weight, *halos, after)
 
 
 def first_unit(chip, scene):
@@ -499,27 +504,30 @@
 def body(features, grad_out, weight, neighbours):
     x = features[0, 0]
     c = grad_out[0, 0]
-    links = neighbours[0, 0]
+    links = jnp.maximum(neighbours[0, 0], -1)
     mates = [(i, i ^ 1) for i in range(SPACE)]
     same_core = [[2 * q + core for q in range(CHIPS)] for core in range(2)]
     grad_scale = 1.0 / math.sqrt(SCENES * SPACE * 512)
 
-    mate_links = lax.ppermute(links, "space", mates)
-    outgoing_c = pack(links, x, c)
-    halo_c = lax.all_to_all(outgoing_c, "space", 0, 0, tiled=True)
-    pair = lax.ppermute(pair_rows(x, c, outgoing_c), "space", mates)
-    outgoing_x, turned, x_half, c_half = prepare(links, mate_links, x, c, pair)
-    halo_x = [
-        lax.ppermute(rows, "space", [(i, i + 2 * hop) for i in range(SPACE) if 0 <= i + 2 * hop < SPACE])
-        for hop, rows in zip(HOPS, outgoing_x)
-    ]
-    terms = kernel_grad(links, mate_links, c_half, turned, halo_c)
+    mate_links, mate_x, mate_c = [lax.ppermute(rows, "space", mates) for rows in (links, x, c)]
+    own = jnp.concatenate([x, c], axis=1)
+    outgoing = pack(links, mate_links, own, mate_x, mate_c)
+    halos = []
+    for hop, rows in enumerate(outgoing, 1):
+        up = [(2 * q, 2 * (q + hop)) for q in range(CHIPS - hop)]
+        down = [(2 * (q + hop) + 1, 2 * q + 1) for q in range(CHIPS - hop)]
+        halos.append(lax.ppermute(rows, "space", up + down))
+    here, turned, x_half, c_half = stage(links, mate_links, own, mate_x, mate_c, outgoing[3])
+    *halos, here, turned, x_half, c_half = lax.optimization_barrier((*halos, here, turned, x_half, c_half))
+    halos += [lax.ppermute(rows, "space", mates) for rows in halos] + [here]
+    terms = kernel_grad(links, mate_links, c_half, turned, halos)
     got_terms = lax.all_to_all(terms, "space", 0, 0, tiled=True, axis_index_groups=same_core)
-    grad_in, mate_grad_in = taps_product(True, links, mate_links, c_half, weight, halo_c, terms)
-    got_terms, grad_in, mate_grad_in = lax.optimization_barrier((got_terms, grad_in, mate_grad_in))
+    grad_in, mate_grad_in = taps_product(True, links, mate_links, c_half, weight, halos, terms)
+    conv_out, mate_conv_out = taps_product(False, links, mate_links, x_half, weight, halos, terms)
+    got_terms, grad_in, mate_grad_in, conv_out, mate_conv_out = lax.optimization_barrier(
+        (got_terms, grad_in, mate_grad_in, conv_out, mate_conv_out)
+    )
     scene_terms = lax.all_to_all(scene_sum(got_terms), "dp", 0, 0, tiled=True)
-    conv_out, mate_conv_out = taps_product(False, links, mate_links, x_half, weight, halo_c, *halo_x, outgoing_x[4])
-    scene_terms, conv_out, mate_conv_out = lax.optimization_barrier((scene_terms, conv_out, mate_conv_out))
     whole = lax.all_to_all(whole_sum(grad_scale, scene_terms), "space", 0, 0, tiled=True)
     grad_in = (grad_in + lax.ppermute(mate_grad_in, "space", mates)).astype(bf16)
     conv_out = (conv_out + lax.ppermute(mate_conv_out, "space", mates)).astype(bf16)

time: 107 us -> 105 us (0.981)
  starting transfers between devices: 41.2 us -> 33.3 us
  waiting for transfers between devices: 33.2 us -> 39.7 us
  Pallas kernels: 27.6 us -> 25.8 us
  other arithmetic: 1.51 us -> 3.23 us
  local copies, waits for them, and re-layouts: 2 us -> 0.76 us
    all_to_all x1 -> x0, waiting for transfers between devices: 10.2 us -> none  [body(): halo_c = lax.all_to_all(outgoing_c, 'space', 0, 0, tiled=True)]
    all_to_all x1 -> x0, starting transfers between devices: 8.64 us -> none  [body(): halo_c = lax.all_to_all(outgoing_c, 'space', 0, 0, tiled=True)]
    all_to_all x1, waiting for transfers between devices: 0.01 us -> 8.14 us  [body(): scene_terms = lax.all_to_all(scene_sum(got_terms), 'dp', 0, 0, tiled=True)]
    ppermute x6 -> x11, waiting for transfers between devices: 1.43 us -> 6.72 us  [the longest x4 5.62 us: body(): halos.append(lax.ppermute(rows, 'space', up + down))]
    all_to_all x1, waiting for transfers between devices: 10.8 us -> 14.7 us  [body(): lax.all_to_all(terms, 'space', 0, 0, tiled=True, axis_index_groups=same_c...]
    pallas_call x3 -> x2, Pallas kernels: 6.01 us -> 3.24 us  [the longest x1 1.67 us: stage(): pl.pallas_call(stage_kernel, out_shape=(jax.ShapeDtypeStruct((256, 256),...]
    all_to_all x1, starting transfers between devices: 3.84 us -> 5.17 us  [body(): lax.all_to_all(whole_sum(grad_scale, scene_terms), 'space', 0, 0, tiled=T...]
    unnamed x30 -> x32, local copies, waits for them, and re-layouts: 2 us -> 0.76 us
  transfers between devices with their start and end apart: 12 -> 16, of which waited for: 5 -> 6; matrix products, arithmetic and copies ran while one was open for 1% -> 3% of each run, Pallas kernels for 19% -> 17%
where the time goes in v3:
time: 105 us; the launch traced here: 104 us
  waiting for transfers between devices  39.7 us (38%)
  starting transfers between devices  33.3 us (32%)
  Pallas kernels  25.8 us (25%)
  other arithmetic  3.23 us (3%)
  between operations  1.1 us (1%)
    all_to_all x1, waiting for transfers between devices, body(): lax.all_to_all(terms, 'space', 0, 0, tiled=True, axis_index_groups=same_c...  14.7 us
    pallas_call x2, Pallas kernels, taps_product(): pl.pallas_call(functools.partial(taps_kernel, turned), out_shape=(jax.Sha...  13.7 us
    all_to_all x1, waiting for transfers between devices, body(): lax.all_to_all(whole_sum(grad_scale, scene_terms), 'space', 0, 0, tiled=T...  10.1 us
    all_to_all x1, waiting for transfers between devices, body(): scene_terms = lax.all_to_all(scene_sum(got_terms), 'dp', 0, 0, tiled=True)  8.14 us
    all_to_all x1, starting transfers between devices, body(): scene_terms = lax.all_to_all(scene_sum(got_terms), 'dp', 0, 0, tiled=True)  8.13 us
    ppermute x4, waiting for transfers between devices, body(): halos.append(lax.ppermute(rows, 'space', up + down))  5.62 us
    pallas_call x1, Pallas kernels, kernel_grad(): pl.pallas_call(kernel_grad_kernel, out_shape=jax.ShapeDtypeStruct((CHIPS,...  5.53 us
    all_to_all x1, starting transfers between devices, body(): lax.all_to_all(whole_sum(grad_scale, scene_terms), 'space', 0, 0, tiled=T...  5.17 us
  transfers between devices with their start and end apart: 16, of which 6 were waited for; matrix products, arithmetic and copies ran while one was open for 3% of the time, Pallas kernels for 17%

profile of v3, /device:TPU:1, one launch (start us, length us, event | category | flops | bytes accessed | tf_op | source)
XLA Modules:
  0.0 103.9 jit_solution(1172916790674754748)
XLA Ops:
  0.6 3.3 %collective-permute-start.1 = (bf16[512,256]{1,0:T(8,128)(2,1)}, bf16[512,256]{1,0:T(8,128)(2,1)S(1)}, u32[]{:S(2)}, u32[]{:S(2)}) collective-permute-start(bf16[512,256]{1,0:T(8,128)(2,1)} %bitcast.8), channel_id=1, source_target_pairs={{0,8},{8,0},{16,24},{24,16},{32,40},{40,32},{48,56},{56,48},{64,72... | collective-permute-start | bytes 786440 | tf_op jit(solution)/shard_map/ppermute | solution.py:512
  4.1 0.7 maximum_bitcast_fusion.links_ref
  4.7 0.4 collective-permute-start
  5.1 1.1 %pad_maximum_fusion.own_ref = bf16[512,512]{1,0:T(8,128)(2,1)S(1)} fusion(bf16[512,256]{1,0:T(8,128)(2,1)} %bitcast.11, bf16[512,256]{1,0:T(8,128)(2,1)} %bitcast.9), kind=kLoop, calls=%fused_computation | loop fusion | flops 1048576 | bytes 1048576 | tf_op jit(solution)/shard_map/concatenate | solution.py:513
  6.2 1.6 %shard_map.67 = (bf16[256,512]{1,0:T(8,128)(2,1)S(1)}, bf16[192,512]{1,0:T(8,128)(2,1)S(1)}, bf16[64,512]{1,0:T(8,128)(2,1)S(1)}, bf16[16,512]{1,0:T(8,128)(2,1)S(1)}) custom-call(s32[27]{0:T(128)S(1)} %maximum_bitcast_fusion.links_ref, s32[27]{0:T(128)S(1)} %collective-permute-done.mate_links_ref, bf16[512,512]{1,0:T(8,128)(2,1)S(1)} %pad_maximum_fusion.own_ref, ...), custom_call_target="tpu_custom_call" | custom-call | flops 2500000000 | bytes 1048576 | tf_op jit(solution)/shard_map/pallas_call | solution.py:132
  7.8 1.3 %collective-permute-start.3 = (bf16[256,512]{1,0:T(8,128)(2,1)S(1)}, bf16[256,512]{1,0:T(8,128)(2,1)S(1)}, u32[]{:S(2)}, u32[]{:S(2)}) collective-permute-start(bf16[256,512]{1,0:T(8,128)(2,1)S(1)} %get-tuple-element.28), channel_id=1, source_target_pairs={{0,16},{16,32},{32,48},{48,64},{64,80},{80,96},{96,112},{112,128},... | collective-permute-start | bytes 786440 | tf_op jit(solution)/shard_map/ppermute | solution.py:519
  9.1 1.3 %collective-permute-start.4 = (bf16[192,512]{1,0:T(8,128)(2,1)S(1)}, bf16[192,512]{1,0:T(8,128)(2,1)S(1)}, u32[]{:S(2)}, u32[]{:S(2)}) collective-permute-start(bf16[192,512]{1,0:T(8,128)(2,1)S(1)} %get-tuple-element.29), channel_id=1, source_target_pairs={{0,32},{16,48},{32,64},{48,80},{64,96},{80,112},{96,128},{112,144}... | collective-permute-start | bytes 589832 | tf_op jit(solution)/shard_map/ppermute | solution.py:519
  10.4 1.3 %collective-permute-start.6 = (bf16[16,512]{1,0:T(8,128)(2,1)S(1)}, bf16[16,512]{1,0:T(8,128)(2,1)S(1)}, u32[]{:S(2)}, u32[]{:S(2)}) collective-permute-start(bf16[16,512]{1,0:T(8,128)(2,1)S(1)} %get-tuple-element.31._), channel_id=1, source_target_pairs={{0,64},{16,80},{32,96},{48,112},{64,128},{80,144},{96,160},{112,17... | collective-permute-start | bytes 49160 | tf_op jit(solution)/shard_map/ppermute | solution.py:519
  11.7 1.3 %collective-permute-start.5 = (bf16[64,512]{1,0:T(8,128)(2,1)S(1)}, bf16[64,512]{1,0:T(8,128)(2,1)S(1)}, u32[]{:S(2)}, u32[]{:S(2)}) collective-permute-start(bf16[64,512]{1,0:T(8,128)(2,1)S(1)} %get-tuple-element.30), channel_id=1, source_target_pairs={{0,48},{16,64},{32,80},{48,96},{64,112},{80,128},{96,144},{112,160... | collective-permute-start | bytes 196616 | tf_op jit(solution)/shard_map/ppermute | solution.py:519
  13.0 1.7 %shard_map.68 = (bf16[256,256]{1,0:T(8,128)(2,1)S(1)}, bf16[2,256,512]{2,1,0:T(8,128)(2,1)S(1)}, bf16[2,512,128]{2,1,0:T(8,128)(2,1)S(1)}, bf16[2,512,128]{2,1,0:T(8,128)(2,1)S(1)}) custom-call(s32[27]{0:T(128)S(1)} %maximum_bitcast_fusion.links_ref, s32[27]{0:T(128)S(1)} %collective-permute-done.mate_links_ref, ...), custom_call_target="tpu_custom_call" | custom-call | flops 1500000000 | bytes 1048576 | tf_op jit(solution)/shard_map/pallas_call | solution.py:177
  14.7 0.7 copy-done.10
  15.4 1.8 %collective-permute-done.6.rest_3_ = bf16[16,512]{1,0:T(8,128)(2,1)S(1)} collective-permute-done((bf16[16,512]{1,0:T(8,128)(2,1)S(1)}, bf16[16,512]{1,0:T(8,128)(2,1)S(1)}, u32[]{:S(2)}, u32[]{:S(2)}) %collective-permute-start.6) | collective-permute-done | bytes 16416 | tf_op jit(solution)/shard_map/ppermute | solution.py:519
  17.2 3.8 %collective-permute-done.5.rest_2_ = bf16[64,512]{1,0:T(8,128)(2,1)S(1)} collective-permute-done((bf16[64,512]{1,0:T(8,128)(2,1)S(1)}, bf16[64,512]{1,0:T(8,128)(2,1)S(1)}, u32[]{:S(2)}, u32[]{:S(2)}) %collective-permute-start.5) | collective-permute-done | bytes 65568 | tf_op jit(solution)/shard_map/ppermute | solution.py:519
  21.1 3.7 %collective-permute-start.7 = (bf16[256,512]{1,0:T(8,128)(2,1)S(1)}, bf16[256,512]{1,0:T(8,128)(2,1)S(1)}, u32[]{:S(2)}, u32[]{:S(2)}) collective-permute-start(bf16[256,512]{1,0:T(8,128)(2,1)S(1)} %collective-permute-done.3.rest_0_), channel_id=1, source_target_pairs={{0,8},{8,0},{16,24},{24,16},{32,40},{40,32},{48,56},{56,48},{64,72... | collective-permute-start | bytes 786440 | tf_op jit(solution)/shard_map/ppermute | solution.py:522
  24.8 0.4 collective-permute-start.9
  25.4 1.1 %collective-permute-done.10.rest_7_ = bf16[16,512]{1,0:T(8,128)(2,1)S(1)} collective-permute-done((bf16[16,512]{1,0:T(8,128)(2,1)S(1)}, bf16[16,512]{1,0:T(8,128)(2,1)S(1)}, u32[]{:S(2)}, u32[]{:S(2)}) %collective-permute-start.10) | collective-permute-done | bytes 16416 | tf_op jit(solution)/shard_map/ppermute | solution.py:522
  26.5 5.5 %shard_map.69.rest_9_ = s16[16,448,128]{2,1,0:T(8,128)(2,1)} custom-call(s32[27]{0:T(128)S(1)} %maximum_bitcast_fusion.links_ref, s32[27]{0:T(128)S(1)} %collective-permute-done.mate_links_ref, bf16[2,512,128]{2,1,0:T(8,128)(2,1)S(1)} %get-tuple-element.36.c_half_ref.half_ref, bf16[2,256,512]{2,1,0:T(8,128)(2,1)S(1)} %get-tuple-element.37.turned_ref, ...), custom_call_target="tpu_custom_call" | custom-call | flops 6000000000 | bytes 1048576 | tf_op jit(solution)/shard_map/pallas_call | solution.py:341
  32.1 4.9 %all-to-all-start = ((s16[16,448,128]{2,1,0:T(8,128)(2,1)}), s16[16,448,128]{2,1,0:T(8,128)(2,1)S(1)}, u32[]{:S(2)}, u32[]{:S(2)}) async-start(s16[16,448,128]{2,1,0:T(8,128)(2,1)} %shard_map.69.rest_9_), calls=%async_computation | async-start | bytes 3670016 | tf_op jit(solution)/shard_map/all_to_all | solution.py:524
  37.1 7.2 %shard_map.70 = (f32[512,256]{1,0:T(8,128)}, f32[512,256]{1,0:T(8,128)}) custom-call(s32[27]{0:T(128)} %copy-done.8, s32[27]{0:T(128)} %copy-done.9, bf16[2,512,128]{2,1,0:T(8,128)(2,1)} %copy-done.11, bf16[27,256,256]{2,1,0:T(8,128)(2,1)} %weight_ref.3, bf16[256,512]{1,0:T(8,128)(2,1)} %copy-done, bf16[192,512]{1,0:T(8,128)(2,1)} %copy-done.2, ...), custom_call_target="tpu_custom_call" | custom-call | flops 6000000000 | bytes 1048576 | tf_op jit(solution)/shard_map/pallas_call | solution.py:397
  44.3 6.5 %shard_map.71 = (f32[512,256]{1,0:T(8,128)}, f32[512,256]{1,0:T(8,128)}) custom-call(s32[27]{0:T(128)} %copy-done.8, s32[27]{0:T(128)} %copy-done.9, bf16[2,512,128]{2,1,0:T(8,128)(2,1)} %copy-done.10, bf16[27,256,256]{2,1,0:T(8,128)(2,1)} %weight_ref.3, bf16[256,512]{1,0:T(8,128)(2,1)} %copy-done, bf16[192,512]{1,0:T(8,128)(2,1)} %copy-done.2, ...), custom_call_target="tpu_custom_call" | custom-call | flops 6000000000 | bytes 1048576 | tf_op jit(solution)/shard_map/pallas_call | solution.py:397
  50.8 14.7 %all-to-all-done.got_ref = s16[16,448,128]{2,1,0:T(8,128)(2,1)S(1)} async-done(((s16[16,448,128]{2,1,0:T(8,128)(2,1)}), s16[16,448,128]{2,1,0:T(8,128)(2,1)S(1)}, u32[]{:S(2)}, u32[]{:S(2)}) %all-to-all-start) | async-done | bytes 1835040 | tf_op jit(solution)/shard_map/all_to_all | solution.py:524
  65.5 1.4 %collective-permute-start.12 = (f32[512,256]{1,0:T(8,128)}, f32[512,256]{1,0:T(8,128)S(1)}, u32[]{:S(2)}, u32[]{:S(2)}) collective-permute-start(f32[512,256]{1,0:T(8,128)} %get-tuple-element.51), channel_id=1, source_target_pairs={{0,8},{8,0},{16,24},{24,16},{32,40},{40,32},{48,56},{56,48},{64,72... | collective-permute-start | bytes 1572872 | tf_op jit(solution)/shard_map/ppermute | solution.py:532
  66.9 1.3 %shard_map.72 = s16[8,64,128]{2,1,0:T(8,128)(2,1)} custom-call(s16[16,448,128]{2,1,0:T(8,128)(2,1)S(1)} %all-to-all-done.got_ref), custom_call_target="tpu_custom_call" | custom-call | flops 2500000000 | bytes 1048576 | tf_op jit(solution)/shard_map/pallas_call | solution.py:439
  68.2 8.1 %all-to-all-start.1 = ((s16[8,64,128]{2,1,0:T(8,128)(2,1)}), s16[8,64,128]{2,1,0:T(8,128)(2,1)S(1)}, u32[]{:S(2)}, u32[]{:S(2)}) async-start(s16[8,64,128]{2,1,0:T(8,128)(2,1)} %shard_map.72), calls=%async_computation.1 | async-start | bytes 262144 | tf_op jit(solution)/shard_map/all_to_all | solution.py:530
  76.4 0.4 collective-permute-start.11
  76.7 8.1 %all-to-all-done.1.got_ref = s16[8,64,128]{2,1,0:T(8,128)(2,1)S(1)} async-done(((s16[8,64,128]{2,1,0:T(8,128)(2,1)}), s16[8,64,128]{2,1,0:T(8,128)(2,1)S(1)}, u32[]{:S(2)}, u32[]{:S(2)}) %all-to-all-start.1) | async-done | bytes 131104 | tf_op jit(solution)/shard_map/all_to_all | solution.py:530
  84.9 0.9 shard_map.73
  85.8 5.2 %all-to-all-start.2 = ((s16[32,64,128]{2,1,0:T(8,128)(2,1)}), s16[32,64,128]{2,1,0:T(8,128)(2,1)S(1)}, u32[]{:S(2)}, u32[]{:S(2)}) async-start(s16[32,64,128]{2,1,0:T(8,128)(2,1)} %shard_map.73), calls=%async_computation.2 | async-start | bytes 1048576 | tf_op jit(solution)/shard_map/all_to_all | solution.py:531
  91.0 0.8 fusion.1
  91.8 0.8 fusion
  92.5 10.1 %all-to-all-done.2.got_ref = s16[32,64,128]{2,1,0:T(8,128)(2,1)S(1)} async-done(((s16[32,64,128]{2,1,0:T(8,128)(2,1)}), s16[32,64,128]{2,1,0:T(8,128)(2,1)S(1)}, u32[]{:S(2)}, u32[]{:S(2)}) %all-to-all-start.2) | async-done | bytes 524320 | tf_op jit(solution)/shard_map/all_to_all | solution.py:531
  102.7 1.0 %shard_map.74 = f32[864,256]{1,0:T(8,128)} custom-call(s16[32,64,128]{2,1,0:T(8,128)(2,1)S(1)} %all-to-all-done.2.got_ref), custom_call_target="tpu_custom_call" | custom-call | tf_op jit(solution)/shard_map/pallas_call | solution.py:494
  (44 shorter events, 0.4 us)
Async XLA Ops:
  0.6 5.6 %collective-permute-start.1 = (bf16[512,256]{1,0:T(8,128)(2,1)}, bf16[512,256]{1,0:T(8,128)(2,1)S(1)}, u32[]{:S(2)}, u32[]{:S(2)}) collective-permute-start(bf16[512,256]{1,0:T(8,128)(2,1)} %bitcast.8), channel_id=1, source_target_pairs={{0,8},{8,0},{16,24},{24,16},{32,40},{40,32},{48,56},{56,48},{64,72... | collective-permute-start | bytes 786440 | tf_op jit(solution)/shard_map/ppermute | solution.py:512
  4.0 2.3 %collective-permute-start.2 = (bf16[512,256]{1,0:T(8,128)(2,1)}, bf16[512,256]{1,0:T(8,128)(2,1)S(1)}, u32[]{:S(2)}, u32[]{:S(2)}) collective-permute-start(bf16[512,256]{1,0:T(8,128)(2,1)} %bitcast.10), channel_id=1, source_target_pairs={{0,8},{8,0},{16,24},{24,16},{32,40},{40,32},{48,56},{56,48},{64,72... | collective-permute-start | bytes 786440 | tf_op jit(solution)/shard_map/ppermute | solution.py:512
  4.7 21.8 %copy-start.8 = (s32[27]{0:T(128)}, s32[27]{0:T(128)S(1)}, u32[]{:S(2)}) copy-start(s32[27]{0:T(128)S(1)} %maximum_bitcast_fusion.links_ref) | copy-start | bytes 328
  4.7 1.5 %collective-permute-start = (s32[27]{0:T(128)S(1)}, s32[27]{0:T(128)S(1)}, u32[]{:S(2)}, u32[]{:S(2)}) collective-permute-start(s32[27]{0:T(128)S(1)} %maximum_bitcast_fusion.links_ref), channel_id=1, source_target_pairs={{0,8},{8,0},{16,24},{24,16},{32,40},{40,32},{48,56},{56,48},{64,72... | collective-permute-start | bytes 332 | tf_op jit(solution)/shard_map/ppermute | solution.py:512
  6.2 20.3 %copy-start.9 = (s32[27]{0:T(128)}, s32[27]{0:T(128)S(1)}, u32[]{:S(2)}) copy-start(s32[27]{0:T(128)S(1)} %collective-permute-done.mate_links_ref) | copy-start | bytes 328
  7.8 13.2 %collective-permute-start.3 = (bf16[256,512]{1,0:T(8,128)(2,1)S(1)}, bf16[256,512]{1,0:T(8,128)(2,1)S(1)}, u32[]{:S(2)}, u32[]{:S(2)}) collective-permute-start(bf16[256,512]{1,0:T(8,128)(2,1)S(1)} %get-tuple-element.28), channel_id=1, source_target_pairs={{0,16},{16,32},{32,48},{48,64},{64,80},{80,96},{96,112},{112,128},... | collective-permute-start | bytes 786440 | tf_op jit(solution)/shard_map/ppermute | solution.py:519
  9.1 11.9 %collective-permute-start.4 = (bf16[192,512]{1,0:T(8,128)(2,1)S(1)}, bf16[192,512]{1,0:T(8,128)(2,1)S(1)}, u32[]{:S(2)}, u32[]{:S(2)}) collective-permute-start(bf16[192,512]{1,0:T(8,128)(2,1)S(1)} %get-tuple-element.29), channel_id=1, source_target_pairs={{0,32},{16,48},{32,64},{48,80},{64,96},{80,112},{96,128},{112,144}... | collective-permute-start | bytes 589832 | tf_op jit(solution)/shard_map/ppermute | solution.py:519
  10.4 6.8 %collective-permute-start.6 = (bf16[16,512]{1,0:T(8,128)(2,1)S(1)}, bf16[16,512]{1,0:T(8,128)(2,1)S(1)}, u32[]{:S(2)}, u32[]{:S(2)}) collective-permute-start(bf16[16,512]{1,0:T(8,128)(2,1)S(1)} %get-tuple-element.31._), channel_id=1, source_target_pairs={{0,64},{16,80},{32,96},{48,112},{64,128},{80,144},{96,160},{112,17... | collective-permute-start | bytes 49160 | tf_op jit(solution)/shard_map/ppermute | solution.py:519
  11.7 9.3 %collective-permute-start.5 = (bf16[64,512]{1,0:T(8,128)(2,1)S(1)}, bf16[64,512]{1,0:T(8,128)(2,1)S(1)}, u32[]{:S(2)}, u32[]{:S(2)}) collective-permute-start(bf16[64,512]{1,0:T(8,128)(2,1)S(1)} %get-tuple-element.30), channel_id=1, source_target_pairs={{0,48},{16,64},{32,80},{48,96},{64,112},{80,128},{96,144},{112,160... | collective-permute-start | bytes 196616 | tf_op jit(solution)/shard_map/ppermute | solution.py:519
  14.7 0.7 copy-start.10
  15.4 16.6 %copy-start.11 = (bf16[2,512,128]{2,1,0:T(8,128)(2,1)}, bf16[2,512,128]{2,1,0:T(8,128)(2,1)S(1)}, u32[]{:S(2)}) copy-start(bf16[2,512,128]{2,1,0:T(8,128)(2,1)S(1)} %get-tuple-element.36.c_half_ref.half_ref) | copy-start | bytes 786436
  15.4 16.7 %copy-start.12 = (bf16[256,256]{1,0:T(8,128)(2,1)}, bf16[256,256]{1,0:T(8,128)(2,1)S(1)}, u32[]{:S(2)}) copy-start(bf16[256,256]{1,0:T(8,128)(2,1)S(1)} %get-tuple-element.42.rest_8_) | copy-start | bytes 393220
  17.2 14.9 %copy-start.6 = (bf16[16,512]{1,0:T(8,128)(2,1)}, bf16[16,512]{1,0:T(8,128)(2,1)S(1)}, u32[]{:S(2)}) copy-start(bf16[16,512]{1,0:T(8,128)(2,1)S(1)} %collective-permute-done.6.rest_3_) | copy-start | bytes 49156
  21.0 11.1 %copy-start.4 = (bf16[64,512]{1,0:T(8,128)(2,1)}, bf16[64,512]{1,0:T(8,128)(2,1)S(1)}, u32[]{:S(2)}) copy-start(bf16[64,512]{1,0:T(8,128)(2,1)S(1)} %collective-permute-done.5.rest_2_) | copy-start | bytes 196612
  21.0 11.1 %copy-start.2 = (bf16[192,512]{1,0:T(8,128)(2,1)}, bf16[192,512]{1,0:T(8,128)(2,1)S(1)}, u32[]{:S(2)}) copy-start(bf16[192,512]{1,0:T(8,128)(2,1)S(1)} %collective-permute-done.4.rest_1_) | copy-start | bytes 589828
  21.0 11.1 %copy-start = (bf16[256,512]{1,0:T(8,128)(2,1)}, bf16[256,512]{1,0:T(8,128)(2,1)S(1)}, u32[]{:S(2)}) copy-start(bf16[256,512]{1,0:T(8,128)(2,1)S(1)} %collective-permute-done.3.rest_0_) | copy-start | bytes 786436
  21.1 5.4 %collective-permute-start.7 = (bf16[256,512]{1,0:T(8,128)(2,1)S(1)}, bf16[256,512]{1,0:T(8,128)(2,1)S(1)}, u32[]{:S(2)}, u32[]{:S(2)}) collective-permute-start(bf16[256,512]{1,0:T(8,128)(2,1)S(1)} %collective-permute-done.3.rest_0_), channel_id=1, source_target_pairs={{0,8},{8,0},{16,24},{24,16},{32,40},{40,32},{48,56},{56,48},{64,72... | collective-permute-start | bytes 786440 | tf_op jit(solution)/shard_map/ppermute | solution.py:522
  24.7 1.7 %collective-permute-start.8 = (bf16[192,512]{1,0:T(8,128)(2,1)S(1)}, bf16[192,512]{1,0:T(8,128)(2,1)S(1)}, u32[]{:S(2)}, u32[]{:S(2)}) collective-permute-start(bf16[192,512]{1,0:T(8,128)(2,1)S(1)} %collective-permute-done.4.rest_1_), channel_id=1, source_target_pairs={{0,8},{8,0},{16,24},{24,16},{32,40},{40,32},{48,56},{56,48},{64,72... | collective-permute-start | bytes 589832 | tf_op jit(solution)/shard_map/ppermute | solution.py:522
  24.8 1.6 %collective-permute-start.9 = (bf16[64,512]{1,0:T(8,128)(2,1)S(1)}, bf16[64,512]{1,0:T(8,128)(2,1)S(1)}, u32[]{:S(2)}, u32[]{:S(2)}) collective-permute-start(bf16[64,512]{1,0:T(8,128)(2,1)S(1)} %collective-permute-done.5.rest_2_), channel_id=1, source_target_pairs={{0,8},{8,0},{16,24},{24,16},{32,40},{40,32},{48,56},{56,48},{64,72... | collective-permute-start | bytes 196616 | tf_op jit(solution)/shard_map/ppermute | solution.py:522
  25.3 1.2 %collective-permute-start.10 = (bf16[16,512]{1,0:T(8,128)(2,1)S(1)}, bf16[16,512]{1,0:T(8,128)(2,1)S(1)}, u32[]{:S(2)}, u32[]{:S(2)}) collective-permute-start(bf16[16,512]{1,0:T(8,128)(2,1)S(1)} %collective-permute-done.6.rest_3_), channel_id=1, source_target_pairs={{0,8},{8,0},{16,24},{24,16},{32,40},{40,32},{48,56},{56,48},{64,72... | collective-permute-start | bytes 49160 | tf_op jit(solution)/shard_map/ppermute | solution.py:522
  26.4 5.7 %copy-start.7 = (bf16[16,512]{1,0:T(8,128)(2,1)}, bf16[16,512]{1,0:T(8,128)(2,1)S(1)}, u32[]{:S(2)}) copy-start(bf16[16,512]{1,0:T(8,128)(2,1)S(1)} %collective-permute-done.10.rest_7_) | copy-start | bytes 49156
  26.4 5.7 %copy-start.5 = (bf16[64,512]{1,0:T(8,128)(2,1)}, bf16[64,512]{1,0:T(8,128)(2,1)S(1)}, u32[]{:S(2)}) copy-start(bf16[64,512]{1,0:T(8,128)(2,1)S(1)} %collective-permute-done.9.rest_6_) | copy-start | bytes 196612
  26.5 5.7 %copy-start.3 = (bf16[192,512]{1,0:T(8,128)(2,1)}, bf16[192,512]{1,0:T(8,128)(2,1)S(1)}, u32[]{:S(2)}) copy-start(bf16[192,512]{1,0:T(8,128)(2,1)S(1)} %collective-permute-done.8.rest_5_) | copy-start | bytes 589828
  26.5 5.6 %copy-start.1 = (bf16[256,512]{1,0:T(8,128)(2,1)}, bf16[256,512]{1,0:T(8,128)(2,1)S(1)}, u32[]{:S(2)}) copy-start(bf16[256,512]{1,0:T(8,128)(2,1)S(1)} %collective-permute-done.7.rest_4_) | copy-start | bytes 786436
  32.1 33.4 %all-to-all-start = ((s16[16,448,128]{2,1,0:T(8,128)(2,1)}), s16[16,448,128]{2,1,0:T(8,128)(2,1)S(1)}, u32[]{:S(2)}, u32[]{:S(2)}) async-start(s16[16,448,128]{2,1,0:T(8,128)(2,1)} %shard_map.69.rest_9_), calls=%async_computation | async-start | bytes 3670016 | tf_op jit(solution)/shard_map/all_to_all | solution.py:524
  65.5 10.8 %copy-start.15 = (f32[512,256]{1,0:T(8,128)S(1)}, f32[512,256]{1,0:T(8,128)}, u32[]{:S(2)}) copy-start(f32[512,256]{1,0:T(8,128)} %get-tuple-element.49) | copy-start | bytes 1572868
  65.5 25.5 %collective-permute-start.12 = (f32[512,256]{1,0:T(8,128)}, f32[512,256]{1,0:T(8,128)S(1)}, u32[]{:S(2)}, u32[]{:S(2)}) collective-permute-start(f32[512,256]{1,0:T(8,128)} %get-tuple-element.51), channel_id=1, source_target_pairs={{0,8},{8,0},{16,24},{24,16},{32,40},{40,32},{48,56},{56,48},{64,72... | collective-permute-start | bytes 1572872 | tf_op jit(solution)/shard_map/ppermute | solution.py:532
  68.2 16.6 %all-to-all-start.1 = ((s16[8,64,128]{2,1,0:T(8,128)(2,1)}), s16[8,64,128]{2,1,0:T(8,128)(2,1)S(1)}, u32[]{:S(2)}, u32[]{:S(2)}) async-start(s16[8,64,128]{2,1,0:T(8,128)(2,1)} %shard_map.72), calls=%async_computation.1 | async-start | bytes 262144 | tf_op jit(solution)/shard_map/all_to_all | solution.py:530
  76.4 14.6 %copy-start.14 = (f32[512,256]{1,0:T(8,128)S(1)}, f32[512,256]{1,0:T(8,128)}, u32[]{:S(2)}) copy-start(f32[512,256]{1,0:T(8,128)} %get-tuple-element.50) | copy-start | bytes 1572868
  76.4 15.4 %collective-permute-start.11 = (f32[512,256]{1,0:T(8,128)S(1)}, f32[512,256]{1,0:T(8,128)S(1)}, u32[]{:S(2)}, u32[]{:S(2)}) collective-permute-start(f32[512,256]{1,0:T(8,128)S(1)} %copy-done.15), channel_id=1, source_target_pairs={{0,8},{8,0},{16,24},{24,16},{32,40},{40,32},{48,56},{56,48},{64,72... | collective-permute-start | bytes 1572872 | tf_op jit(solution)/shard_map/ppermute | solution.py:533
  85.8 6.0 %copy-start.13 = (f32[512,256]{1,0:T(8,128)S(1)}, f32[512,256]{1,0:T(8,128)}, u32[]{:S(2)}) copy-start(f32[512,256]{1,0:T(8,128)} %get-tuple-element.48) | copy-start | bytes 1572868
  85.8 16.8 %all-to-all-start.2 = ((s16[32,64,128]{2,1,0:T(8,128)(2,1)}), s16[32,64,128]{2,1,0:T(8,128)(2,1)S(1)}, u32[]{:S(2)}, u32[]{:S(2)}) async-start(s16[32,64,128]{2,1,0:T(8,128)(2,1)} %shard_map.73), calls=%async_computation.2 | async-start | bytes 1048576 | tf_op jit(solution)/shard_map/all_to_all | solution.py:531

commit v4 on v3

--- a/solution.py
+++ b/solution.py
@@ -211,12 +211,14 @@
     return jnp.exp2(code * (1.0 / 256.0)) * (1.0 / LEVELS)
 
 
-def fill(brick, links, fetch, own_rows, plane, low, high, shifted_low, shifted_high, padded):
+def fill(brick, links, fetch, ready, own_rows, plane, low, high, shifted_low, shifted_high, padded):
     plane[...] = jnp.zeros_like(plane)
     low[...] = jnp.zeros_like(low)
     high[...] = jnp.zeros_like(high)
     for x in range(8):
         plane[pl.ds((x + 1) * 80 + 8, 64), :] = own_rows(x * 64)
+    for copy in ready:
+        copy.wait()
     for k, dx, dy, dz in OFFSETS:
         source = links[k]
 
@@ -256,13 +258,14 @@
                 padded[brick, x * 64 : x * 64 + 64, at : at + HALF] = source[pl.ds(x * 80 + j * 8, 64), :].astype(bf16)
 
 
-def fill_both(core, links_ref, mate_links_ref, half_ref, fetch, scratch):
+def fill_both(core, links_ref, mate_links_ref, half_ref, halo_copies, fetch, scratch):
     for brick in range(2):
 
         def rows(first, brick=brick):
             return half_ref[brick, pl.ds(first, 64), :].astype(f32)
 
-        fill(brick, [jnp.where(core == brick, links_ref[k], mate_links_ref[k]) for k in range(27)], fetch, rows, *scratch)
+        links = [jnp.where(core == brick, links_ref[k], mate_links_ref[k]) for k in range(27)]
+        fill(brick, links, fetch, halo_copies if brick == 0 else [], rows, *scratch)
 
 
 def take_halos(tensor, own, halos, slots, sems):
@@ -310,9 +313,7 @@
     halo_copies, fetch = take_halos(1, own, halos, slots, halo_sems)
     for copy in halo_copies:
         copy.start()
-    for copy in halo_copies:
-        copy.wait()
-    fill_both(lax.rem(own, 2), links_ref, mate_links_ref, c_half_ref, fetch, scratch)
+    fill_both(lax.rem(own, 2), links_ref, mate_links_ref, c_half_ref, halo_copies, fetch, scratch)
     for i in range(3):
         window = slice(i * 64, i * 64 + 512)
         term = jnp.dot(turned_ref[0], padded[0, window, :], preferred_element_type=f32)
@@ -373,9 +374,7 @@
     padded = scratch[-1]
     for copy in halo_copies + copies:
         copy.start()
-    for copy in halo_copies:
-        copy.wait()
-    fill_both(core, links_ref, mate_links_ref, half_ref, fetch, scratch)
+    fill_both(core, links_ref, mate_links_ref, half_ref, halo_copies, fetch, scratch)
     for copy in copies:
         copy.wait()
     for to_mate, out in ((0, out_ref), (1, mate_out_ref)):
@@ -452,14 +451,14 @@
     for scene in range(1, SCENES):
         total += plain_block(got_ref[scene])
     block = coded_block(total * scale)
-    for target in range(SPACE):
+    for target in range(CHIPS):
         out_ref[target] = block
 
 
 def whole_sum(scale, got):
     return pl.pallas_call(
         functools.partial(whole_kernel, scale),
-        out_shape=jax.ShapeDtypeStruct((SPACE, 64, HALF), i16),
+        out_shape=jax.ShapeDtypeStruct((CHIPS, 64, HALF), i16),
         in_specs=[vmem()],
         out_specs=vmem(),
         compiler_params=params(LW),
@@ -467,38 +466,38 @@
     )(got)
 
 
-def place_kernel(got_ref, out_ref, whole, sems):
-    scene = position()[1]
+def place_kernel(got_ref, mate_ref, out_ref, whole, sems):
+    space, scene = position()
+    core = lax.rem(space, 2)
     outs = [
         pltpu.make_async_copy(whole.at[pl.ds(t * 128, size), :], out_ref.at[pl.ds(t * 128, size), :], sems.at[t])
         for t, size in enumerate((128,) * 6 + (96,))
     ]
-    steps = [step_of(plain(got_ref[source, 48:64, :])[8:9]) for source in range(SPACE)]
+    both = ((got_ref, pl.multiple_of(core * HALF, HALF)), (mate_ref, pl.multiple_of((1 - core) * HALF, HALF)))
+    steps = [[step_of(plain(ref[chip, 48:64, :])[8:9]) for chip in range(CHIPS)] for ref, _ in both]
     for t in range(0, 7, 2):
         for chip in range(CHIPS):
             rest = first_unit(chip, scene)
-            for half in range(2):
-                source = 2 * chip + half
-                lanes = slice(half * HALF, (half + 1) * HALF)
-                values = plain(got_ref[source, t * 8 : t * 8 + 16, :]) * steps[source]
+            for n, (ref, at_lane) in enumerate(both):
+                values = plain(ref[chip, t * 8 : t * 8 + 16, :]) * steps[n][chip]
                 for now in range(t, min(t + 2, 7)):
                     at = pl.multiple_of((16 * now + rest) * 8, 8)
-                    whole[pl.ds(at, 8), lanes] = values[(now - t) * 8 : (now - t + 1) * 8]
+                    whole[pl.ds(at, 8), pl.ds(at_lane, HALF)] = values[(now - t) * 8 : (now - t + 1) * 8]
         for now in range(t, min(t + 2, 7)):
             outs[now].start()
     for copy in outs:
         copy.wait()
 
 
-def place(got):
+def place(got, mate):
     return pl.pallas_call(
         place_kernel,
         out_shape=jax.ShapeDtypeStruct((864, 256), f32),
-        in_specs=[vmem()],
+        in_specs=[vmem(), vmem()],
         out_specs=hbm(),
         scratch_shapes=[pltpu.VMEM((896, 256), f32), pltpu.SemaphoreType.DMA((7,))],
         compiler_params=params(8),
-    )(got)
+    )(got, mate)
 
 
 def body(features, grad_out, weight, neighbours):
@@ -528,10 +527,12 @@
         (got_terms, grad_in, mate_grad_in, conv_out, mate_conv_out)
     )
     scene_terms = lax.all_to_all(scene_sum(got_terms), "dp", 0, 0, tiled=True)
-    whole = lax.all_to_all(whole_sum(grad_scale, scene_terms), "space", 0, 0, tiled=True)
+    whole = whole_sum(grad_scale, scene_terms)
+    whole = lax.all_to_all(whole, "space", 0, 0, tiled=True, axis_index_groups=same_core)
+    mate_whole = lax.ppermute(whole, "space", mates)
     grad_in = (grad_in + lax.ppermute(mate_grad_in, "space", mates)).astype(bf16)
     conv_out = (conv_out + lax.ppermute(mate_conv_out, "space", mates)).astype(bf16)
-    return conv_out[None, None], grad_in[None, None], place(whole)
+    return conv_out[None, None], grad_in[None, None], place(whole, mate_whole)
 
 
 def solution(mesh):

time: 105 us -> 101 us (0.962)
  waiting for transfers between devices: 39.7 us -> 28 us
  blocking collectives: 0 us -> 10.7 us
  Pallas kernels: 25.8 us -> 24.6 us
    all_to_all x0 -> x1, blocking collectives: none -> 10.7 us  [body(): lax.all_to_all(whole, 'space', 0, 0, tiled=True, axis_index_groups=same_c...]
    all_to_all x1 -> x0, waiting for transfers between devices: 10.1 us -> none  [body(): lax.all_to_all(whole_sum(grad_scale, scene_terms), 'space', 0, 0, tiled=T...]
    all_to_all x1 -> x0, starting transfers between devices: 5.17 us -> none  [body(): lax.all_to_all(whole_sum(grad_scale, scene_terms), 'space', 0, 0, tiled=T...]
    ppermute x0 -> x1, starting transfers between devices: none -> 4.14 us  [body(): mate_whole = lax.ppermute(whole, 'space', mates)]
    all_to_all x1, waiting for transfers between devices: 8.14 us -> 6.1 us  [body(): scene_terms = lax.all_to_all(scene_sum(got_terms), 'dp', 0, 0, tiled=True)]
  transfers between devices with their start and end apart: 16 -> 16, of which waited for: 6 -> 5; matrix products, arithmetic and copies ran while one was open for 3% -> 3% of each run, Pallas kernels for 17% -> 15%
where the time goes in v4:
time: 101 us
  starting transfers between devices  32.4 us (32%)
  waiting for transfers between devices  28 us (28%)
  Pallas kernels  24.6 us (24%)
  blocking collectives  10.7 us (11%)
  other arithmetic  3.24 us (3%)
  between operations  1.1 us (1%)
    all_to_all x1, waiting for transfers between devices, body(): lax.all_to_all(terms, 'space', 0, 0, tiled=True, axis_index_groups=same_c...  15.2 us
    pallas_call x2, Pallas kernels, taps_product(): pl.pallas_call(functools.partial(taps_kernel, turned), out_shape=(jax.Sha...  13.3 us
    all_to_all x1, blocking collectives, body(): lax.all_to_all(whole, 'space', 0, 0, tiled=True, axis_index_groups=same_c...  10.7 us
    all_to_all x1, starting transfers between devices, body(): scene_terms = lax.all_to_all(scene_sum(got_terms), 'dp', 0, 0, tiled=True)  8.18 us
    all_to_all x1, waiting for transfers between devices, body(): scene_terms = lax.all_to_all(scene_sum(got_terms), 'dp', 0, 0, tiled=True)  6.1 us
    ppermute x4, waiting for transfers between devices, body(): halos.append(lax.ppermute(rows, 'space', up + down))  5.59 us
    pallas_call x1, Pallas kernels, kernel_grad(): pl.pallas_call(kernel_grad_kernel, out_shape=jax.ShapeDtypeStruct((CHIPS,...  5.5 us
    ppermute x4, starting transfers between devices, body(): halos.append(lax.ppermute(rows, 'space', up + down))  5.17 us
  transfers between devices with their start and end apart: 16, of which 5 were waited for; matrix products, arithmetic and copies ran while one was open for 3% of the time, Pallas kernels for 15%

profile of v4, /device:TPU:1, one launch (start us, length us, event | category | flops | bytes accessed | tf_op | source)
XLA Modules:
  0.0 100.8 jit_solution(16873883391912471418)
XLA Ops:
  0.6 3.3 %collective-permute-start.1 = (bf16[512,256]{1,0:T(8,128)(2,1)}, bf16[512,256]{1,0:T(8,128)(2,1)S(1)}, u32[]{:S(2)}, u32[]{:S(2)}) collective-permute-start(bf16[512,256]{1,0:T(8,128)(2,1)} %bitcast.8), channel_id=1, source_target_pairs={{0,8},{8,0},{16,24},{24,16},{32,40},{40,32},{48,56},{56,48},{64,72... | collective-permute-start | bytes 786440 | tf_op jit(solution)/shard_map/ppermute | solution.py:511
  4.0 0.1 collective-permute-start.2
  4.1 0.7 maximum_bitcast_fusion.links_ref
  4.7 0.4 collective-permute-start
  5.1 1.1 %pad_maximum_fusion.own_ref = bf16[512,512]{1,0:T(8,128)(2,1)S(1)} fusion(bf16[512,256]{1,0:T(8,128)(2,1)} %bitcast.11, bf16[512,256]{1,0:T(8,128)(2,1)} %bitcast.9), kind=kLoop, calls=%fused_computation | loop fusion | flops 1048576 | bytes 1048576 | tf_op jit(solution)/shard_map/concatenate | solution.py:512
  6.2 1.6 %shard_map.67 = (bf16[256,512]{1,0:T(8,128)(2,1)S(1)}, bf16[192,512]{1,0:T(8,128)(2,1)S(1)}, bf16[64,512]{1,0:T(8,128)(2,1)S(1)}, bf16[16,512]{1,0:T(8,128)(2,1)S(1)}) custom-call(s32[27]{0:T(128)S(1)} %maximum_bitcast_fusion.links_ref, s32[27]{0:T(128)S(1)} %collective-permute-done.mate_links_ref, bf16[512,512]{1,0:T(8,128)(2,1)S(1)} %pad_maximum_fusion.own_ref, ...), custom_call_target="tpu_custom_call" | custom-call | flops 2500000000 | bytes 1048576 | tf_op jit(solution)/shard_map/pallas_call | solution.py:132
  7.8 1.3 %collective-permute-start.3 = (bf16[256,512]{1,0:T(8,128)(2,1)S(1)}, bf16[256,512]{1,0:T(8,128)(2,1)S(1)}, u32[]{:S(2)}, u32[]{:S(2)}) collective-permute-start(bf16[256,512]{1,0:T(8,128)(2,1)S(1)} %get-tuple-element.28), channel_id=1, source_target_pairs={{0,16},{16,32},{32,48},{48,64},{64,80},{80,96},{96,112},{112,128},... | collective-permute-start | bytes 786440 | tf_op jit(solution)/shard_map/ppermute | solution.py:518
  9.1 1.3 %collective-permute-start.4 = (bf16[192,512]{1,0:T(8,128)(2,1)S(1)}, bf16[192,512]{1,0:T(8,128)(2,1)S(1)}, u32[]{:S(2)}, u32[]{:S(2)}) collective-permute-start(bf16[192,512]{1,0:T(8,128)(2,1)S(1)} %get-tuple-element.29), channel_id=1, source_target_pairs={{0,32},{16,48},{32,64},{48,80},{64,96},{80,112},{96,128},{112,144}... | collective-permute-start | bytes 589832 | tf_op jit(solution)/shard_map/ppermute | solution.py:518
  10.4 1.3 %collective-permute-start.6 = (bf16[16,512]{1,0:T(8,128)(2,1)S(1)}, bf16[16,512]{1,0:T(8,128)(2,1)S(1)}, u32[]{:S(2)}, u32[]{:S(2)}) collective-permute-start(bf16[16,512]{1,0:T(8,128)(2,1)S(1)} %get-tuple-element.31._), channel_id=1, source_target_pairs={{0,64},{16,80},{32,96},{48,112},{64,128},{80,144},{96,160},{112,17... | collective-permute-start | bytes 49160 | tf_op jit(solution)/shard_map/ppermute | solution.py:518
  11.7 1.3 %collective-permute-start.5 = (bf16[64,512]{1,0:T(8,128)(2,1)S(1)}, bf16[64,512]{1,0:T(8,128)(2,1)S(1)}, u32[]{:S(2)}, u32[]{:S(2)}) collective-permute-start(bf16[64,512]{1,0:T(8,128)(2,1)S(1)} %get-tuple-element.30), channel_id=1, source_target_pairs={{0,48},{16,64},{32,80},{48,96},{64,112},{80,128},{96,144},{112,160... | collective-permute-start | bytes 196616 | tf_op jit(solution)/shard_map/ppermute | solution.py:518
  13.0 1.7 %shard_map.68 = (bf16[256,256]{1,0:T(8,128)(2,1)S(1)}, bf16[2,256,512]{2,1,0:T(8,128)(2,1)S(1)}, bf16[2,512,128]{2,1,0:T(8,128)(2,1)S(1)}, bf16[2,512,128]{2,1,0:T(8,128)(2,1)S(1)}) custom-call(s32[27]{0:T(128)S(1)} %maximum_bitcast_fusion.links_ref, s32[27]{0:T(128)S(1)} %collective-permute-done.mate_links_ref, ...), custom_call_target="tpu_custom_call" | custom-call | flops 1500000000 | bytes 1048576 | tf_op jit(solution)/shard_map/pallas_call | solution.py:177
  14.7 0.7 copy-done.10
  15.4 1.8 %collective-permute-done.6.rest_3_ = bf16[16,512]{1,0:T(8,128)(2,1)S(1)} collective-permute-done((bf16[16,512]{1,0:T(8,128)(2,1)S(1)}, bf16[16,512]{1,0:T(8,128)(2,1)S(1)}, u32[]{:S(2)}, u32[]{:S(2)}) %collective-permute-start.6) | collective-permute-done | bytes 16416 | tf_op jit(solution)/shard_map/ppermute | solution.py:518
  17.2 3.8 %collective-permute-done.5.rest_2_ = bf16[64,512]{1,0:T(8,128)(2,1)S(1)} collective-permute-done((bf16[64,512]{1,0:T(8,128)(2,1)S(1)}, bf16[64,512]{1,0:T(8,128)(2,1)S(1)}, u32[]{:S(2)}, u32[]{:S(2)}) %collective-permute-start.5) | collective-permute-done | bytes 65568 | tf_op jit(solution)/shard_map/ppermute | solution.py:518
  21.0 3.7 %collective-permute-start.7 = (bf16[256,512]{1,0:T(8,128)(2,1)S(1)}, bf16[256,512]{1,0:T(8,128)(2,1)S(1)}, u32[]{:S(2)}, u32[]{:S(2)}) collective-permute-start(bf16[256,512]{1,0:T(8,128)(2,1)S(1)} %collective-permute-done.3.rest_0_), channel_id=1, source_target_pairs={{0,8},{8,0},{16,24},{24,16},{32,40},{40,32},{48,56},{56,48},{64,72... | collective-permute-start | bytes 786440 | tf_op jit(solution)/shard_map/ppermute | solution.py:521
  24.8 0.4 collective-permute-start.9
  25.4 1.1 %collective-permute-done.10.rest_7_ = bf16[16,512]{1,0:T(8,128)(2,1)S(1)} collective-permute-done((bf16[16,512]{1,0:T(8,128)(2,1)S(1)}, bf16[16,512]{1,0:T(8,128)(2,1)S(1)}, u32[]{:S(2)}, u32[]{:S(2)}) %collective-permute-start.10) | collective-permute-done | bytes 16416 | tf_op jit(solution)/shard_map/ppermute | solution.py:521
  26.5 5.5 %shard_map.69.rest_9_ = s16[16,448,128]{2,1,0:T(8,128)(2,1)} custom-call(s32[27]{0:T(128)S(1)} %maximum_bitcast_fusion.links_ref, s32[27]{0:T(128)S(1)} %collective-permute-done.mate_links_ref, bf16[2,512,128]{2,1,0:T(8,128)(2,1)S(1)} %get-tuple-element.36.c_half_ref.half_ref, bf16[2,256,512]{2,1,0:T(8,128)(2,1)S(1)} %get-tuple-element.37.turned_ref, ...), custom_call_target="tpu_custom_call" | custom-call | flops 6000000000 | bytes 1048576 | tf_op jit(solution)/shard_map/pallas_call | solution.py:342
  32.1 5.0 %all-to-all-start = ((s16[16,448,128]{2,1,0:T(8,128)(2,1)}), s16[16,448,128]{2,1,0:T(8,128)(2,1)S(1)}, u32[]{:S(2)}, u32[]{:S(2)}) async-start(s16[16,448,128]{2,1,0:T(8,128)(2,1)} %shard_map.69.rest_9_), calls=%async_computation | async-start | bytes 3670016 | tf_op jit(solution)/shard_map/all_to_all | solution.py:523
  37.1 6.9 %shard_map.70 = (f32[512,256]{1,0:T(8,128)}, f32[512,256]{1,0:T(8,128)}) custom-call(s32[27]{0:T(128)} %copy-done.8, s32[27]{0:T(128)} %copy-done.9, bf16[2,512,128]{2,1,0:T(8,128)(2,1)} %copy-done.11, bf16[27,256,256]{2,1,0:T(8,128)(2,1)} %weight_ref.3, bf16[256,512]{1,0:T(8,128)(2,1)} %copy-done, bf16[192,512]{1,0:T(8,128)(2,1)} %copy-done.2, ...), custom_call_target="tpu_custom_call" | custom-call | flops 6000000000 | bytes 1048576 | tf_op jit(solution)/shard_map/pallas_call | solution.py:396
  44.0 6.3 %shard_map.71 = (f32[512,256]{1,0:T(8,128)}, f32[512,256]{1,0:T(8,128)}) custom-call(s32[27]{0:T(128)} %copy-done.8, s32[27]{0:T(128)} %copy-done.9, bf16[2,512,128]{2,1,0:T(8,128)(2,1)} %copy-done.10, bf16[27,256,256]{2,1,0:T(8,128)(2,1)} %weight_ref.3, bf16[256,512]{1,0:T(8,128)(2,1)} %copy-done, bf16[192,512]{1,0:T(8,128)(2,1)} %copy-done.2, ...), custom_call_target="tpu_custom_call" | custom-call | flops 6000000000 | bytes 1048576 | tf_op jit(solution)/shard_map/pallas_call | solution.py:396
  50.4 15.2 %all-to-all-done.got_ref = s16[16,448,128]{2,1,0:T(8,128)(2,1)S(1)} async-done(((s16[16,448,128]{2,1,0:T(8,128)(2,1)}), s16[16,448,128]{2,1,0:T(8,128)(2,1)S(1)}, u32[]{:S(2)}, u32[]{:S(2)}) %all-to-all-start) | async-done | bytes 1835040 | tf_op jit(solution)/shard_map/all_to_all | solution.py:523
  65.5 1.3 %shard_map.72 = s16[8,64,128]{2,1,0:T(8,128)(2,1)} custom-call(s16[16,448,128]{2,1,0:T(8,128)(2,1)S(1)} %all-to-all-done.got_ref), custom_call_target="tpu_custom_call" | custom-call | flops 2500000000 | bytes 1048576 | tf_op jit(solution)/shard_map/pallas_call | solution.py:438
  66.9 8.2 %all-to-all-start.1 = ((s16[8,64,128]{2,1,0:T(8,128)(2,1)}), s16[8,64,128]{2,1,0:T(8,128)(2,1)S(1)}, u32[]{:S(2)}, u32[]{:S(2)}) async-start(s16[8,64,128]{2,1,0:T(8,128)(2,1)} %shard_map.72), calls=%async_computation.1 | async-start | bytes 262144 | tf_op jit(solution)/shard_map/all_to_all | solution.py:529
  75.1 1.7 %collective-permute-start.12 = (f32[512,256]{1,0:T(8,128)S(1)}, f32[512,256]{1,0:T(8,128)S(1)}, u32[]{:S(2)}, u32[]{:S(2)}) collective-permute-start(f32[512,256]{1,0:T(8,128)S(1)} %copy-done.16), channel_id=1, source_target_pairs={{0,8},{8,0},{16,24},{24,16},{32,40},{40,32},{48,56},{56,48},{64,72... | collective-permute-start | bytes 1572872 | tf_op jit(solution)/shard_map/ppermute | solution.py:533
  76.8 0.1 collective-permute-start.11
  76.9 6.1 %all-to-all-done.1.got_ref = s16[8,64,128]{2,1,0:T(8,128)(2,1)S(1)} async-done(((s16[8,64,128]{2,1,0:T(8,128)(2,1)}), s16[8,64,128]{2,1,0:T(8,128)(2,1)S(1)}, u32[]{:S(2)}, u32[]{:S(2)}) %all-to-all-start.1) | async-done | bytes 131104 | tf_op jit(solution)/shard_map/all_to_all | solution.py:529
  83.1 10.7 %all_to_all.15.got_ref = s16[16,64,128]{2,1,0:T(8,128)(2,1)S(1)} all-to-all(s16[16,64,128]{2,1,0:T(8,128)(2,1)S(1)} %shard_map.73), channel_id=1, replica_groups={{0,16,32,48,64,80,96,112,128,144,160,176,192,208,224,240},{8,24,40,56,7..., dimensions={0} | all-to-all | bytes 524288 | tf_op jit(solution)/shard_map/all_to_all | solution.py:531
  93.8 4.1 %collective-permute-start.13 = (s16[16,64,128]{2,1,0:T(8,128)(2,1)S(1)}, s16[16,64,128]{2,1,0:T(8,128)(2,1)S(1)}, u32[]{:S(2)}, u32[]{:S(2)}) collective-permute-start(s16[16,64,128]{2,1,0:T(8,128)(2,1)S(1)} %all_to_all.15.got_ref), channel_id=1, source_target_pairs={{0,8},{8,0},{16,24},{24,16},{32,40},{40,32},{48,56},{56,48},{64,72... | collective-permute-start | bytes 786440 | tf_op jit(solution)/shard_map/ppermute | solution.py:532
  97.9 0.8 fusion.1
  98.7 0.8 fusion
  99.5 1.2 %shard_map.74 = f32[864,256]{1,0:T(8,128)} custom-call(s16[16,64,128]{2,1,0:T(8,128)(2,1)S(1)} %all_to_all.15.got_ref, s16[16,64,128]{2,1,0:T(8,128)(2,1)S(1)} %collective-permute-done.13.mate_ref), custom_call_target="tpu_custom_call" | custom-call | tf_op jit(solution)/shard_map/pallas_call | solution.py:493
  (47 shorter events, 0.4 us)
Async XLA Ops:
  0.6 5.6 %collective-permute-start.1 = (bf16[512,256]{1,0:T(8,128)(2,1)}, bf16[512,256]{1,0:T(8,128)(2,1)S(1)}, u32[]{:S(2)}, u32[]{:S(2)}) collective-permute-start(bf16[512,256]{1,0:T(8,128)(2,1)} %bitcast.8), channel_id=1, source_target_pairs={{0,8},{8,0},{16,24},{24,16},{32,40},{40,32},{48,56},{56,48},{64,72... | collective-permute-start | bytes 786440 | tf_op jit(solution)/shard_map/ppermute | solution.py:511
  4.0 2.3 %collective-permute-start.2 = (bf16[512,256]{1,0:T(8,128)(2,1)}, bf16[512,256]{1,0:T(8,128)(2,1)S(1)}, u32[]{:S(2)}, u32[]{:S(2)}) collective-permute-start(bf16[512,256]{1,0:T(8,128)(2,1)} %bitcast.10), channel_id=1, source_target_pairs={{0,8},{8,0},{16,24},{24,16},{32,40},{40,32},{48,56},{56,48},{64,72... | collective-permute-start | bytes 786440 | tf_op jit(solution)/shard_map/ppermute | solution.py:511
  4.7 21.8 %copy-start.8 = (s32[27]{0:T(128)}, s32[27]{0:T(128)S(1)}, u32[]{:S(2)}) copy-start(s32[27]{0:T(128)S(1)} %maximum_bitcast_fusion.links_ref) | copy-start | bytes 328
  4.7 1.5 %collective-permute-start = (s32[27]{0:T(128)S(1)}, s32[27]{0:T(128)S(1)}, u32[]{:S(2)}, u32[]{:S(2)}) collective-permute-start(s32[27]{0:T(128)S(1)} %maximum_bitcast_fusion.links_ref), channel_id=1, source_target_pairs={{0,8},{8,0},{16,24},{24,16},{32,40},{40,32},{48,56},{56,48},{64,72... | collective-permute-start | bytes 332 | tf_op jit(solution)/shard_map/ppermute | solution.py:511
  6.2 20.3 %copy-start.9 = (s32[27]{0:T(128)}, s32[27]{0:T(128)S(1)}, u32[]{:S(2)}) copy-start(s32[27]{0:T(128)S(1)} %collective-permute-done.mate_links_ref) | copy-start | bytes 328
  7.8 13.2 %collective-permute-start.3 = (bf16[256,512]{1,0:T(8,128)(2,1)S(1)}, bf16[256,512]{1,0:T(8,128)(2,1)S(1)}, u32[]{:S(2)}, u32[]{:S(2)}) collective-permute-start(bf16[256,512]{1,0:T(8,128)(2,1)S(1)} %get-tuple-element.28), channel_id=1, source_target_pairs={{0,16},{16,32},{32,48},{48,64},{64,80},{80,96},{96,112},{112,128},... | collective-permute-start | bytes 786440 | tf_op jit(solution)/shard_map/ppermute | solution.py:518
  9.1 11.9 %collective-permute-start.4 = (bf16[192,512]{1,0:T(8,128)(2,1)S(1)}, bf16[192,512]{1,0:T(8,128)(2,1)S(1)}, u32[]{:S(2)}, u32[]{:S(2)}) collective-permute-start(bf16[192,512]{1,0:T(8,128)(2,1)S(1)} %get-tuple-element.29), channel_id=1, source_target_pairs={{0,32},{16,48},{32,64},{48,80},{64,96},{80,112},{96,128},{112,144}... | collective-permute-start | bytes 589832 | tf_op jit(solution)/shard_map/ppermute | solution.py:518
  10.4 6.8 %collective-permute-start.6 = (bf16[16,512]{1,0:T(8,128)(2,1)S(1)}, bf16[16,512]{1,0:T(8,128)(2,1)S(1)}, u32[]{:S(2)}, u32[]{:S(2)}) collective-permute-start(bf16[16,512]{1,0:T(8,128)(2,1)S(1)} %get-tuple-element.31._), channel_id=1, source_target_pairs={{0,64},{16,80},{32,96},{48,112},{64,128},{80,144},{96,160},{112,17... | collective-permute-start | bytes 49160 | tf_op jit(solution)/shard_map/ppermute | solution.py:518
  11.7 9.3 %collective-permute-start.5 = (bf16[64,512]{1,0:T(8,128)(2,1)S(1)}, bf16[64,512]{1,0:T(8,128)(2,1)S(1)}, u32[]{:S(2)}, u32[]{:S(2)}) collective-permute-start(bf16[64,512]{1,0:T(8,128)(2,1)S(1)} %get-tuple-element.30), channel_id=1, source_target_pairs={{0,48},{16,64},{32,80},{48,96},{64,112},{80,128},{96,144},{112,160... | collective-permute-start | bytes 196616 | tf_op jit(solution)/shard_map/ppermute | solution.py:518
  15.4 16.6 %copy-start.11 = (bf16[2,512,128]{2,1,0:T(8,128)(2,1)}, bf16[2,512,128]{2,1,0:T(8,128)(2,1)S(1)}, u32[]{:S(2)}) copy-start(bf16[2,512,128]{2,1,0:T(8,128)(2,1)S(1)} %get-tuple-element.36.c_half_ref.half_ref) | copy-start | bytes 786436
  15.4 16.6 %copy-start.12 = (bf16[256,256]{1,0:T(8,128)(2,1)}, bf16[256,256]{1,0:T(8,128)(2,1)S(1)}, u32[]{:S(2)}) copy-start(bf16[256,256]{1,0:T(8,128)(2,1)S(1)} %get-tuple-element.42.rest_8_) | copy-start | bytes 393220
  17.2 14.9 %copy-start.6 = (bf16[16,512]{1,0:T(8,128)(2,1)}, bf16[16,512]{1,0:T(8,128)(2,1)S(1)}, u32[]{:S(2)}) copy-start(bf16[16,512]{1,0:T(8,128)(2,1)S(1)} %collective-permute-done.6.rest_3_) | copy-start | bytes 49156
  21.0 11.0 %copy-start.4 = (bf16[64,512]{1,0:T(8,128)(2,1)}, bf16[64,512]{1,0:T(8,128)(2,1)S(1)}, u32[]{:S(2)}) copy-start(bf16[64,512]{1,0:T(8,128)(2,1)S(1)} %collective-permute-done.5.rest_2_) | copy-start | bytes 196612
  21.0 11.1 %copy-start.2 = (bf16[192,512]{1,0:T(8,128)(2,1)}, bf16[192,512]{1,0:T(8,128)(2,1)S(1)}, u32[]{:S(2)}) copy-start(bf16[192,512]{1,0:T(8,128)(2,1)S(1)} %collective-permute-done.4.rest_1_) | copy-start | bytes 589828
  21.0 11.1 %copy-start = (bf16[256,512]{1,0:T(8,128)(2,1)}, bf16[256,512]{1,0:T(8,128)(2,1)S(1)}, u32[]{:S(2)}) copy-start(bf16[256,512]{1,0:T(8,128)(2,1)S(1)} %collective-permute-done.3.rest_0_) | copy-start | bytes 786436
  21.0 5.4 %collective-permute-start.7 = (bf16[256,512]{1,0:T(8,128)(2,1)S(1)}, bf16[256,512]{1,0:T(8,128)(2,1)S(1)}, u32[]{:S(2)}, u32[]{:S(2)}) collective-permute-start(bf16[256,512]{1,0:T(8,128)(2,1)S(1)} %collective-permute-done.3.rest_0_), channel_id=1, source_target_pairs={{0,8},{8,0},{16,24},{24,16},{32,40},{40,32},{48,56},{56,48},{64,72... | collective-permute-start | bytes 786440 | tf_op jit(solution)/shard_map/ppermute | solution.py:521
  24.7 1.7 %collective-permute-start.8 = (bf16[192,512]{1,0:T(8,128)(2,1)S(1)}, bf16[192,512]{1,0:T(8,128)(2,1)S(1)}, u32[]{:S(2)}, u32[]{:S(2)}) collective-permute-start(bf16[192,512]{1,0:T(8,128)(2,1)S(1)} %collective-permute-done.4.rest_1_), channel_id=1, source_target_pairs={{0,8},{8,0},{16,24},{24,16},{32,40},{40,32},{48,56},{56,48},{64,72... | collective-permute-start | bytes 589832 | tf_op jit(solution)/shard_map/ppermute | solution.py:521
  24.8 1.6 %collective-permute-start.9 = (bf16[64,512]{1,0:T(8,128)(2,1)S(1)}, bf16[64,512]{1,0:T(8,128)(2,1)S(1)}, u32[]{:S(2)}, u32[]{:S(2)}) collective-permute-start(bf16[64,512]{1,0:T(8,128)(2,1)S(1)} %collective-permute-done.5.rest_2_), channel_id=1, source_target_pairs={{0,8},{8,0},{16,24},{24,16},{32,40},{40,32},{48,56},{56,48},{64,72... | collective-permute-start | bytes 196616 | tf_op jit(solution)/shard_map/ppermute | solution.py:521
  25.3 1.2 %collective-permute-start.10 = (bf16[16,512]{1,0:T(8,128)(2,1)S(1)}, bf16[16,512]{1,0:T(8,128)(2,1)S(1)}, u32[]{:S(2)}, u32[]{:S(2)}) collective-permute-start(bf16[16,512]{1,0:T(8,128)(2,1)S(1)} %collective-permute-done.6.rest_3_), channel_id=1, source_target_pairs={{0,8},{8,0},{16,24},{24,16},{32,40},{40,32},{48,56},{56,48},{64,72... | collective-permute-start | bytes 49160 | tf_op jit(solution)/shard_map/ppermute | solution.py:521
  26.4 5.6 %copy-start.7 = (bf16[16,512]{1,0:T(8,128)(2,1)}, bf16[16,512]{1,0:T(8,128)(2,1)S(1)}, u32[]{:S(2)}) copy-start(bf16[16,512]{1,0:T(8,128)(2,1)S(1)} %collective-permute-done.10.rest_7_) | copy-start | bytes 49156
  26.4 5.6 %copy-start.5 = (bf16[64,512]{1,0:T(8,128)(2,1)}, bf16[64,512]{1,0:T(8,128)(2,1)S(1)}, u32[]{:S(2)}) copy-start(bf16[64,512]{1,0:T(8,128)(2,1)S(1)} %collective-permute-done.9.rest_6_) | copy-start | bytes 196612
  26.4 5.6 %copy-start.3 = (bf16[192,512]{1,0:T(8,128)(2,1)}, bf16[192,512]{1,0:T(8,128)(2,1)S(1)}, u32[]{:S(2)}) copy-start(bf16[192,512]{1,0:T(8,128)(2,1)S(1)} %collective-permute-done.8.rest_5_) | copy-start | bytes 589828
  26.5 5.6 %copy-start.1 = (bf16[256,512]{1,0:T(8,128)(2,1)}, bf16[256,512]{1,0:T(8,128)(2,1)S(1)}, u32[]{:S(2)}) copy-start(bf16[256,512]{1,0:T(8,128)(2,1)S(1)} %collective-permute-done.7.rest_4_) | copy-start | bytes 786436
  32.1 33.4 %all-to-all-start = ((s16[16,448,128]{2,1,0:T(8,128)(2,1)}), s16[16,448,128]{2,1,0:T(8,128)(2,1)S(1)}, u32[]{:S(2)}, u32[]{:S(2)}) async-start(s16[16,448,128]{2,1,0:T(8,128)(2,1)} %shard_map.69.rest_9_), calls=%async_computation | async-start | bytes 3670016 | tf_op jit(solution)/shard_map/all_to_all | solution.py:523
  65.5 9.5 %copy-start.16 = (f32[512,256]{1,0:T(8,128)S(1)}, f32[512,256]{1,0:T(8,128)}, u32[]{:S(2)}) copy-start(f32[512,256]{1,0:T(8,128)} %get-tuple-element.51) | copy-start | bytes 1572868
  65.5 11.3 %copy-start.15 = (f32[512,256]{1,0:T(8,128)S(1)}, f32[512,256]{1,0:T(8,128)}, u32[]{:S(2)}) copy-start(f32[512,256]{1,0:T(8,128)} %get-tuple-element.49) | copy-start | bytes 1572868
  66.9 16.1 %all-to-all-start.1 = ((s16[8,64,128]{2,1,0:T(8,128)(2,1)}), s16[8,64,128]{2,1,0:T(8,128)(2,1)S(1)}, u32[]{:S(2)}, u32[]{:S(2)}) async-start(s16[8,64,128]{2,1,0:T(8,128)(2,1)} %shard_map.72), calls=%async_computation.1 | async-start | bytes 262144 | tf_op jit(solution)/shard_map/all_to_all | solution.py:529
  75.0 22.9 %copy-start.14 = (f32[512,256]{1,0:T(8,128)S(1)}, f32[512,256]{1,0:T(8,128)}, u32[]{:S(2)}) copy-start(f32[512,256]{1,0:T(8,128)} %get-tuple-element.50) | copy-start | bytes 1572868
  75.1 22.9 %collective-permute-start.12 = (f32[512,256]{1,0:T(8,128)S(1)}, f32[512,256]{1,0:T(8,128)S(1)}, u32[]{:S(2)}, u32[]{:S(2)}) collective-permute-start(f32[512,256]{1,0:T(8,128)S(1)} %copy-done.16), channel_id=1, source_target_pairs={{0,8},{8,0},{16,24},{24,16},{32,40},{40,32},{48,56},{56,48},{64,72... | collective-permute-start | bytes 1572872 | tf_op jit(solution)/shard_map/ppermute | solution.py:533
  76.8 21.9 %collective-permute-start.11 = (f32[512,256]{1,0:T(8,128)S(1)}, f32[512,256]{1,0:T(8,128)S(1)}, u32[]{:S(2)}, u32[]{:S(2)}) collective-permute-start(f32[512,256]{1,0:T(8,128)S(1)} %copy-done.15), channel_id=1, source_target_pairs={{0,8},{8,0},{16,24},{24,16},{32,40},{40,32},{48,56},{56,48},{64,72... | collective-permute-start | bytes 1572872 | tf_op jit(solution)/shard_map/ppermute | solution.py:534
  83.1 15.6 %copy-start.13 = (f32[512,256]{1,0:T(8,128)S(1)}, f32[512,256]{1,0:T(8,128)}, u32[]{:S(2)}) copy-start(f32[512,256]{1,0:T(8,128)} %get-tuple-element.48) | copy-start | bytes 1572868
  93.8 5.7 %collective-permute-start.13 = (s16[16,64,128]{2,1,0:T(8,128)(2,1)S(1)}, s16[16,64,128]{2,1,0:T(8,128)(2,1)S(1)}, u32[]{:S(2)}, u32[]{:S(2)}) collective-permute-start(s16[16,64,128]{2,1,0:T(8,128)(2,1)S(1)} %all_to_all.15.got_ref), channel_id=1, source_target_pairs={{0,8},{8,0},{16,24},{24,16},{32,40},{40,32},{48,56},{56,48},{64,72... | collective-permute-start | bytes 786440 | tf_op jit(solution)/shard_map/ppermute | solution.py:532
  (1 other events, 0.7 us)

commit v5 on v4

--- a/solution.py
+++ b/solution.py
@@ -523,15 +523,13 @@
     got_terms = lax.all_to_all(terms, "space", 0, 0, tiled=True, axis_index_groups=same_core)
     grad_in, mate_grad_in = taps_product(True, links, mate_links, c_half, weight, halos, terms)
     conv_out, mate_conv_out = taps_product(False, links, mate_links, x_half, weight, halos, terms)
-    got_terms, grad_in, mate_grad_in, conv_out, mate_conv_out = lax.optimization_barrier(
-        (got_terms, grad_in, mate_grad_in, conv_out, mate_conv_out)
-    )
+    grad_in = (grad_in + lax.ppermute(mate_grad_in, "space", mates)).astype(bf16)
+    conv_out = (conv_out + lax.ppermute(mate_conv_out, "space", mates)).astype(bf16)
+    got_terms, grad_in, conv_out = lax.optimization_barrier((got_terms, grad_in, conv_out))
     scene_terms = lax.all_to_all(scene_sum(got_terms), "dp", 0, 0, tiled=True)
     whole = whole_sum(grad_scale, scene_terms)
     whole = lax.all_to_all(whole, "space", 0, 0, tiled=True, axis_index_groups=same_core)
     mate_whole = lax.ppermute(whole, "space", mates)
-    grad_in = (grad_in + lax.ppermute(mate_grad_in, "space", mates)).astype(bf16)
-    conv_out = (conv_out + lax.ppermute(mate_conv_out, "space", mates)).astype(bf16)
     return conv_out[None, None], grad_in[None, None], place(whole, mate_whole)
 
 

time: 101 us -> 100 us (0.990)
  blocking collectives: 10.7 us -> 26.5 us
  starting transfers between devices: 32.4 us -> 23.1 us
  waiting for transfers between devices: 28 us -> 19.8 us
  other arithmetic: 3.24 us -> 4.31 us
    all_to_all x0 -> x1, blocking collectives: none -> 15.9 us  [body(): scene_terms = lax.all_to_all(scene_sum(got_terms), 'dp', 0, 0, tiled=True)]
    all_to_all x1 -> x0, starting transfers between devices: 8.18 us -> none  [body(): scene_terms = lax.all_to_all(scene_sum(got_terms), 'dp', 0, 0, tiled=True)]
    all_to_all x1 -> x0, waiting for transfers between devices: 6.1 us -> none  [body(): scene_terms = lax.all_to_all(scene_sum(got_terms), 'dp', 0, 0, tiled=True)]
    all_to_all x1, waiting for transfers between devices: 15.2 us -> 10.6 us  [body(): lax.all_to_all(terms, 'space', 0, 0, tiled=True, axis_index_groups=same_c...]
    convert_element_type x0 -> x2, other arithmetic: none -> 2.59 us  [the longest x1 1.83 us: body(): (grad_in + lax.ppermute(mate_grad_in, 'space', mates)).astype(bf16)]
    ppermute x1, starting transfers between devices: 1.72 us -> 0.14 us  [body(): lax.ppermute(mate_grad_in, 'space', mates)]
    broadcast_in_dim x2 -> x0, other arithmetic: 1.52 us -> none  [body(): return (conv_out[None, None], grad_in[None, None], place(whole, mate_whole))]
    ppermute x1, waiting for transfers between devices: 0.01 us -> 1.31 us  [body(): lax.ppermute(mate_grad_in, 'space', mates)]
  transfers between devices with their start and end apart: 16 -> 15, of which waited for: 5 -> 6; matrix products, arithmetic and copies ran while one was open for 3% -> 4% of each run, Pallas kernels for 15% -> 15%
where the time goes in v5:
time: 100 us; the launch traced here: 99.4 us
  blocking collectives  26.5 us (26%)
  Pallas kernels  23.9 us (24%)
  starting transfers between devices  23.1 us (23%)
  waiting for transfers between devices  19.8 us (20%)
  other arithmetic  4.31 us (4%)
  between operations  1.08 us (1%)
    all_to_all x1, blocking collectives, body(): scene_terms = lax.all_to_all(scene_sum(got_terms), 'dp', 0, 0, tiled=True)  15.9 us
    pallas_call x2, Pallas kernels, taps_product(): pl.pallas_call(functools.partial(taps_kernel, turned), out_shape=(jax.Sha...  13.2 us
    all_to_all x1, waiting for transfers between devices, body(): lax.all_to_all(terms, 'space', 0, 0, tiled=True, axis_index_groups=same_c...  10.6 us
    all_to_all x1, blocking collectives, body(): lax.all_to_all(whole, 'space', 0, 0, tiled=True, axis_index_groups=same_c...  10.6 us
    ppermute x4, waiting for transfers between devices, body(): halos.append(lax.ppermute(rows, 'space', up + down))  5.64 us
    pallas_call x1, Pallas kernels, kernel_grad(): pl.pallas_call(kernel_grad_kernel, out_shape=jax.ShapeDtypeStruct((CHIPS,...  5.54 us
    ppermute x4, starting transfers between devices, body(): halos.append(lax.ppermute(rows, 'space', up + down))  5.17 us
    all_to_all x1, starting transfers between devices, body(): lax.all_to_all(terms, 'space', 0, 0, tiled=True, axis_index_groups=same_c...  4.91 us
  transfers between devices with their start and end apart: 15, of which 6 were waited for; matrix products, arithmetic and copies ran while one was open for 4% of the time, Pallas kernels for 15%

profile of v5, /device:TPU:1, one launch (start us, length us, event | category | flops | bytes accessed | tf_op | source)
XLA Modules:
  0.0 99.4 jit_solution(16533142847756632052)
XLA Ops:
  0.6 3.3 %collective-permute-start.1 = (bf16[512,256]{1,0:T(8,128)(2,1)}, bf16[512,256]{1,0:T(8,128)(2,1)S(1)}, u32[]{:S(2)}, u32[]{:S(2)}) collective-permute-start(bf16[512,256]{1,0:T(8,128)(2,1)} %bitcast.8), channel_id=1, source_target_pairs={{0,8},{8,0},{16,24},{24,16},{32,40},{40,32},{48,56},{56,48},{64,72... | collective-permute-start | bytes 786440 | tf_op jit(solution)/shard_map/ppermute | solution.py:511
  4.1 0.7 maximum_bitcast_fusion.links_ref
  4.7 0.4 collective-permute-start
  5.1 1.1 %pad_maximum_fusion.own_ref = bf16[512,512]{1,0:T(8,128)(2,1)S(1)} fusion(bf16[512,256]{1,0:T(8,128)(2,1)} %bitcast.11, bf16[512,256]{1,0:T(8,128)(2,1)} %bitcast.9), kind=kLoop, calls=%fused_computation | loop fusion | flops 1048576 | bytes 1048576 | tf_op jit(solution)/shard_map/concatenate | solution.py:512
  6.2 1.6 %shard_map.67 = (bf16[256,512]{1,0:T(8,128)(2,1)S(1)}, bf16[192,512]{1,0:T(8,128)(2,1)S(1)}, bf16[64,512]{1,0:T(8,128)(2,1)S(1)}, bf16[16,512]{1,0:T(8,128)(2,1)S(1)}) custom-call(s32[27]{0:T(128)S(1)} %maximum_bitcast_fusion.links_ref, s32[27]{0:T(128)S(1)} %collective-permute-done.mate_links_ref, bf16[512,512]{1,0:T(8,128)(2,1)S(1)} %pad_maximum_fusion.own_ref, ...), custom_call_target="tpu_custom_call" | custom-call | flops 2500000000 | bytes 1048576 | tf_op jit(solution)/shard_map/pallas_call | solution.py:132
  7.8 1.3 %collective-permute-start.3 = (bf16[256,512]{1,0:T(8,128)(2,1)S(1)}, bf16[256,512]{1,0:T(8,128)(2,1)S(1)}, u32[]{:S(2)}, u32[]{:S(2)}) collective-permute-start(bf16[256,512]{1,0:T(8,128)(2,1)S(1)} %get-tuple-element.26), channel_id=1, source_target_pairs={{0,16},{16,32},{32,48},{48,64},{64,80},{80,96},{96,112},{112,128},... | collective-permute-start | bytes 786440 | tf_op jit(solution)/shard_map/ppermute | solution.py:518
  9.1 1.3 %collective-permute-start.4 = (bf16[192,512]{1,0:T(8,128)(2,1)S(1)}, bf16[192,512]{1,0:T(8,128)(2,1)S(1)}, u32[]{:S(2)}, u32[]{:S(2)}) collective-permute-start(bf16[192,512]{1,0:T(8,128)(2,1)S(1)} %get-tuple-element.27), channel_id=1, source_target_pairs={{0,32},{16,48},{32,64},{48,80},{64,96},{80,112},{96,128},{112,144}... | collective-permute-start | bytes 589832 | tf_op jit(solution)/shard_map/ppermute | solution.py:518
  10.4 1.3 %collective-permute-start.6 = (bf16[16,512]{1,0:T(8,128)(2,1)S(1)}, bf16[16,512]{1,0:T(8,128)(2,1)S(1)}, u32[]{:S(2)}, u32[]{:S(2)}) collective-permute-start(bf16[16,512]{1,0:T(8,128)(2,1)S(1)} %get-tuple-element.29._), channel_id=1, source_target_pairs={{0,64},{16,80},{32,96},{48,112},{64,128},{80,144},{96,160},{112,17... | collective-permute-start | bytes 49160 | tf_op jit(solution)/shard_map/ppermute | solution.py:518
  11.7 1.3 %collective-permute-start.5 = (bf16[64,512]{1,0:T(8,128)(2,1)S(1)}, bf16[64,512]{1,0:T(8,128)(2,1)S(1)}, u32[]{:S(2)}, u32[]{:S(2)}) collective-permute-start(bf16[64,512]{1,0:T(8,128)(2,1)S(1)} %get-tuple-element.28), channel_id=1, source_target_pairs={{0,48},{16,64},{32,80},{48,96},{64,112},{80,128},{96,144},{112,160... | collective-permute-start | bytes 196616 | tf_op jit(solution)/shard_map/ppermute | solution.py:518
  13.0 1.7 %shard_map.68 = (bf16[256,256]{1,0:T(8,128)(2,1)S(1)}, bf16[2,256,512]{2,1,0:T(8,128)(2,1)S(1)}, bf16[2,512,128]{2,1,0:T(8,128)(2,1)S(1)}, bf16[2,512,128]{2,1,0:T(8,128)(2,1)S(1)}) custom-call(s32[27]{0:T(128)S(1)} %maximum_bitcast_fusion.links_ref, s32[27]{0:T(128)S(1)} %collective-permute-done.mate_links_ref, ...), custom_call_target="tpu_custom_call" | custom-call | flops 1500000000 | bytes 1048576 | tf_op jit(solution)/shard_map/pallas_call | solution.py:177
  14.7 0.7 copy-done.11
  15.4 1.8 %collective-permute-done.6.rest_3_ = bf16[16,512]{1,0:T(8,128)(2,1)S(1)} collective-permute-done((bf16[16,512]{1,0:T(8,128)(2,1)S(1)}, bf16[16,512]{1,0:T(8,128)(2,1)S(1)}, u32[]{:S(2)}, u32[]{:S(2)}) %collective-permute-start.6) | collective-permute-done | bytes 16416 | tf_op jit(solution)/shard_map/ppermute | solution.py:518
  17.2 3.8 %collective-permute-done.5.rest_2_ = bf16[64,512]{1,0:T(8,128)(2,1)S(1)} collective-permute-done((bf16[64,512]{1,0:T(8,128)(2,1)S(1)}, bf16[64,512]{1,0:T(8,128)(2,1)S(1)}, u32[]{:S(2)}, u32[]{:S(2)}) %collective-permute-start.5) | collective-permute-done | bytes 65568 | tf_op jit(solution)/shard_map/ppermute | solution.py:518
  21.1 3.7 %collective-permute-start.7 = (bf16[256,512]{1,0:T(8,128)(2,1)S(1)}, bf16[256,512]{1,0:T(8,128)(2,1)S(1)}, u32[]{:S(2)}, u32[]{:S(2)}) collective-permute-start(bf16[256,512]{1,0:T(8,128)(2,1)S(1)} %collective-permute-done.3.rest_0_), channel_id=1, source_target_pairs={{0,8},{8,0},{16,24},{24,16},{32,40},{40,32},{48,56},{56,48},{64,72... | collective-permute-start | bytes 786440 | tf_op jit(solution)/shard_map/ppermute | solution.py:521
  24.9 0.4 collective-permute-start.9
  25.4 1.1 %collective-permute-done.10.rest_7_ = bf16[16,512]{1,0:T(8,128)(2,1)S(1)} collective-permute-done((bf16[16,512]{1,0:T(8,128)(2,1)S(1)}, bf16[16,512]{1,0:T(8,128)(2,1)S(1)}, u32[]{:S(2)}, u32[]{:S(2)}) %collective-permute-start.10) | collective-permute-done | bytes 16416 | tf_op jit(solution)/shard_map/ppermute | solution.py:521
  26.5 5.5 %shard_map.69.rest_9_ = s16[16,448,128]{2,1,0:T(8,128)(2,1)} custom-call(s32[27]{0:T(128)S(1)} %maximum_bitcast_fusion.links_ref, s32[27]{0:T(128)S(1)} %collective-permute-done.mate_links_ref, bf16[2,512,128]{2,1,0:T(8,128)(2,1)S(1)} %get-tuple-element.34.c_half_ref.half_ref, bf16[2,256,512]{2,1,0:T(8,128)(2,1)S(1)} %get-tuple-element.35.turned_ref, ...), custom_call_target="tpu_custom_call" | custom-call | flops 6000000000 | bytes 1048576 | tf_op jit(solution)/shard_map/pallas_call | solution.py:342
  32.2 4.9 %all-to-all-start = ((s16[16,448,128]{2,1,0:T(8,128)(2,1)}), s16[16,448,128]{2,1,0:T(8,128)(2,1)S(1)}, u32[]{:S(2)}, u32[]{:S(2)}) async-start(s16[16,448,128]{2,1,0:T(8,128)(2,1)} %shard_map.69.rest_9_), calls=%async_computation | async-start | bytes 3670016 | tf_op jit(solution)/shard_map/all_to_all | solution.py:523
  37.1 6.3 %shard_map.71 = (f32[512,256]{1,0:T(8,128)}, f32[512,256]{1,0:T(8,128)}) custom-call(s32[27]{0:T(128)} %copy-done.8, s32[27]{0:T(128)} %copy-done.9, bf16[2,512,128]{2,1,0:T(8,128)(2,1)} %copy-done.11, bf16[27,256,256]{2,1,0:T(8,128)(2,1)} %weight_ref.3, bf16[256,512]{1,0:T(8,128)(2,1)} %copy-done, bf16[192,512]{1,0:T(8,128)(2,1)} %copy-done.2, ...), custom_call_target="tpu_custom_call" | custom-call | flops 6000000000 | bytes 1048576 | tf_op jit(solution)/shard_map/pallas_call | solution.py:396
  43.4 0.6 collective-permute-start.12
  44.0 6.9 %shard_map.70 = (f32[512,256]{1,0:T(8,128)}, f32[512,256]{1,0:T(8,128)}) custom-call(s32[27]{0:T(128)} %copy-done.8, s32[27]{0:T(128)} %copy-done.9, bf16[2,512,128]{2,1,0:T(8,128)(2,1)} %copy-done.10, bf16[27,256,256]{2,1,0:T(8,128)(2,1)} %weight_ref.3, bf16[256,512]{1,0:T(8,128)(2,1)} %copy-done, bf16[192,512]{1,0:T(8,128)(2,1)} %copy-done.2, ...), custom_call_target="tpu_custom_call" | custom-call | flops 6000000000 | bytes 1048576 | tf_op jit(solution)/shard_map/pallas_call | solution.py:396
  50.9 0.1 collective-permute-start.11
  51.1 0.8 add_convert_fusion
  51.8 1.3 %collective-permute-done.11 = f32[512,256]{1,0:T(8,128)S(1)} collective-permute-done((f32[512,256]{1,0:T(8,128)}, f32[512,256]{1,0:T(8,128)S(1)}, u32[]{:S(2)}, u32[]{:S(2)}) %collective-permute-start.11) | collective-permute-done | bytes 524320 | tf_op jit(solution)/shard_map/ppermute | solution.py:526
  53.1 1.8 %add_convert_fusion.1 = bf16[512,256]{1,0:T(8,128)(2,1)} fusion(f32[512,256]{1,0:T(8,128)} %get-tuple-element.41, f32[512,256]{1,0:T(8,128)S(1)} %collective-permute-done.11), kind=kLoop, calls=%fused_computation.2 | loop fusion | flops 262144 | bytes 1310720 | tf_op jit(solution)/shard_map/convert_element_type | solution.py:526
  55.0 10.6 %all-to-all-done.got_ref = s16[16,448,128]{2,1,0:T(8,128)(2,1)S(1)} async-done(((s16[16,448,128]{2,1,0:T(8,128)(2,1)}), s16[16,448,128]{2,1,0:T(8,128)(2,1)S(1)}, u32[]{:S(2)}, u32[]{:S(2)}) %all-to-all-start) | async-done | bytes 1835040 | tf_op jit(solution)/shard_map/all_to_all | solution.py:523
  65.5 0.7 shard_map.72
  66.2 15.9 %all_to_all.15.got_ref = s16[8,64,128]{2,1,0:T(8,128)(2,1)S(1)} all-to-all(s16[8,64,128]{2,1,0:T(8,128)(2,1)S(1)} %shard_map.72), channel_id=1, replica_groups=mesh['space'=32,'dp'=8] {'dp'}, dimensions={0} | all-to-all | bytes 262144 | tf_op jit(solution)/shard_map/all_to_all | solution.py:529
  82.2 10.6 %all_to_all.16.got_ref = s16[16,64,128]{2,1,0:T(8,128)(2,1)S(1)} all-to-all(s16[16,64,128]{2,1,0:T(8,128)(2,1)S(1)} %shard_map.73), channel_id=1, replica_groups={{0,16,32,48,64,80,96,112,128,144,160,176,192,208,224,240},{8,24,40,56,7..., dimensions={0} | all-to-all | bytes 524288 | tf_op jit(solution)/shard_map/all_to_all | solution.py:531
  92.8 4.1 %collective-permute-start.13 = (s16[16,64,128]{2,1,0:T(8,128)(2,1)S(1)}, s16[16,64,128]{2,1,0:T(8,128)(2,1)S(1)}, u32[]{:S(2)}, u32[]{:S(2)}) collective-permute-start(s16[16,64,128]{2,1,0:T(8,128)(2,1)S(1)} %all_to_all.16.got_ref), channel_id=1, source_target_pairs={{0,8},{8,0},{16,24},{24,16},{32,40},{40,32},{48,56},{56,48},{64,72... | collective-permute-start | bytes 786440 | tf_op jit(solution)/shard_map/ppermute | solution.py:532
  96.9 1.2 %collective-permute-done.13.mate_ref = s16[16,64,128]{2,1,0:T(8,128)(2,1)S(1)} collective-permute-done((s16[16,64,128]{2,1,0:T(8,128)(2,1)S(1)}, s16[16,64,128]{2,1,0:T(8,128)(2,1)S(1)}, u32[]{:S(2)}, u32[]{:S(2)}) %collective-permute-start.13) | collective-permute-done | bytes 262176 | tf_op jit(solution)/shard_map/ppermute | solution.py:532
  98.1 1.2 %shard_map.74 = f32[864,256]{1,0:T(8,128)} custom-call(s16[16,64,128]{2,1,0:T(8,128)(2,1)S(1)} %all_to_all.16.got_ref, s16[16,64,128]{2,1,0:T(8,128)(2,1)S(1)} %collective-permute-done.13.mate_ref), custom_call_target="tpu_custom_call" | custom-call | tf_op jit(solution)/shard_map/pallas_call | solution.py:493
  (40 shorter events, 0.5 us)
Async XLA Ops:
  0.6 5.6 %collective-permute-start.1 = (bf16[512,256]{1,0:T(8,128)(2,1)}, bf16[512,256]{1,0:T(8,128)(2,1)S(1)}, u32[]{:S(2)}, u32[]{:S(2)}) collective-permute-start(bf16[512,256]{1,0:T(8,128)(2,1)} %bitcast.8), channel_id=1, source_target_pairs={{0,8},{8,0},{16,24},{24,16},{32,40},{40,32},{48,56},{56,48},{64,72... | collective-permute-start | bytes 786440 | tf_op jit(solution)/shard_map/ppermute | solution.py:511
  4.0 2.3 %collective-permute-start.2 = (bf16[512,256]{1,0:T(8,128)(2,1)}, bf16[512,256]{1,0:T(8,128)(2,1)S(1)}, u32[]{:S(2)}, u32[]{:S(2)}) collective-permute-start(bf16[512,256]{1,0:T(8,128)(2,1)} %bitcast.10), channel_id=1, source_target_pairs={{0,8},{8,0},{16,24},{24,16},{32,40},{40,32},{48,56},{56,48},{64,72... | collective-permute-start | bytes 786440 | tf_op jit(solution)/shard_map/ppermute | solution.py:511
  4.7 21.8 %copy-start.8 = (s32[27]{0:T(128)}, s32[27]{0:T(128)S(1)}, u32[]{:S(2)}) copy-start(s32[27]{0:T(128)S(1)} %maximum_bitcast_fusion.links_ref) | copy-start | bytes 328
  4.7 1.5 %collective-permute-start = (s32[27]{0:T(128)S(1)}, s32[27]{0:T(128)S(1)}, u32[]{:S(2)}, u32[]{:S(2)}) collective-permute-start(s32[27]{0:T(128)S(1)} %maximum_bitcast_fusion.links_ref), channel_id=1, source_target_pairs={{0,8},{8,0},{16,24},{24,16},{32,40},{40,32},{48,56},{56,48},{64,72... | collective-permute-start | bytes 332 | tf_op jit(solution)/shard_map/ppermute | solution.py:511
  6.2 20.3 %copy-start.9 = (s32[27]{0:T(128)}, s32[27]{0:T(128)S(1)}, u32[]{:S(2)}) copy-start(s32[27]{0:T(128)S(1)} %collective-permute-done.mate_links_ref) | copy-start | bytes 328
  7.8 13.2 %collective-permute-start.3 = (bf16[256,512]{1,0:T(8,128)(2,1)S(1)}, bf16[256,512]{1,0:T(8,128)(2,1)S(1)}, u32[]{:S(2)}, u32[]{:S(2)}) collective-permute-start(bf16[256,512]{1,0:T(8,128)(2,1)S(1)} %get-tuple-element.26), channel_id=1, source_target_pairs={{0,16},{16,32},{32,48},{48,64},{64,80},{80,96},{96,112},{112,128},... | collective-permute-start | bytes 786440 | tf_op jit(solution)/shard_map/ppermute | solution.py:518
  9.1 11.9 %collective-permute-start.4 = (bf16[192,512]{1,0:T(8,128)(2,1)S(1)}, bf16[192,512]{1,0:T(8,128)(2,1)S(1)}, u32[]{:S(2)}, u32[]{:S(2)}) collective-permute-start(bf16[192,512]{1,0:T(8,128)(2,1)S(1)} %get-tuple-element.27), channel_id=1, source_target_pairs={{0,32},{16,48},{32,64},{48,80},{64,96},{80,112},{96,128},{112,144}... | collective-permute-start | bytes 589832 | tf_op jit(solution)/shard_map/ppermute | solution.py:518
  10.4 6.8 %collective-permute-start.6 = (bf16[16,512]{1,0:T(8,128)(2,1)S(1)}, bf16[16,512]{1,0:T(8,128)(2,1)S(1)}, u32[]{:S(2)}, u32[]{:S(2)}) collective-permute-start(bf16[16,512]{1,0:T(8,128)(2,1)S(1)} %get-tuple-element.29._), channel_id=1, source_target_pairs={{0,64},{16,80},{32,96},{48,112},{64,128},{80,144},{96,160},{112,17... | collective-permute-start | bytes 49160 | tf_op jit(solution)/shard_map/ppermute | solution.py:518
  11.7 9.3 %collective-permute-start.5 = (bf16[64,512]{1,0:T(8,128)(2,1)S(1)}, bf16[64,512]{1,0:T(8,128)(2,1)S(1)}, u32[]{:S(2)}, u32[]{:S(2)}) collective-permute-start(bf16[64,512]{1,0:T(8,128)(2,1)S(1)} %get-tuple-element.28), channel_id=1, source_target_pairs={{0,48},{16,64},{32,80},{48,96},{64,112},{80,128},{96,144},{112,160... | collective-permute-start | bytes 196616 | tf_op jit(solution)/shard_map/ppermute | solution.py:518
  14.7 0.7 copy-start.11
  15.4 16.7 %copy-start.10 = (bf16[2,512,128]{2,1,0:T(8,128)(2,1)}, bf16[2,512,128]{2,1,0:T(8,128)(2,1)S(1)}, u32[]{:S(2)}) copy-start(bf16[2,512,128]{2,1,0:T(8,128)(2,1)S(1)} %get-tuple-element.34.c_half_ref.half_ref) | copy-start | bytes 786436
  15.4 16.7 %copy-start.12 = (bf16[256,256]{1,0:T(8,128)(2,1)}, bf16[256,256]{1,0:T(8,128)(2,1)S(1)}, u32[]{:S(2)}) copy-start(bf16[256,256]{1,0:T(8,128)(2,1)S(1)} %get-tuple-element.40.rest_8_) | copy-start | bytes 393220
  17.2 14.9 %copy-start.6 = (bf16[16,512]{1,0:T(8,128)(2,1)}, bf16[16,512]{1,0:T(8,128)(2,1)S(1)}, u32[]{:S(2)}) copy-start(bf16[16,512]{1,0:T(8,128)(2,1)S(1)} %collective-permute-done.6.rest_3_) | copy-start | bytes 49156
  21.0 11.1 %copy-start.4 = (bf16[64,512]{1,0:T(8,128)(2,1)}, bf16[64,512]{1,0:T(8,128)(2,1)S(1)}, u32[]{:S(2)}) copy-start(bf16[64,512]{1,0:T(8,128)(2,1)S(1)} %collective-permute-done.5.rest_2_) | copy-start | bytes 196612
  21.1 11.1 %copy-start.2 = (bf16[192,512]{1,0:T(8,128)(2,1)}, bf16[192,512]{1,0:T(8,128)(2,1)S(1)}, u32[]{:S(2)}) copy-start(bf16[192,512]{1,0:T(8,128)(2,1)S(1)} %collective-permute-done.4.rest_1_) | copy-start | bytes 589828
  21.1 11.1 %copy-start = (bf16[256,512]{1,0:T(8,128)(2,1)}, bf16[256,512]{1,0:T(8,128)(2,1)S(1)}, u32[]{:S(2)}) copy-start(bf16[256,512]{1,0:T(8,128)(2,1)S(1)} %collective-permute-done.3.rest_0_) | copy-start | bytes 786436
  21.1 5.4 %collective-permute-start.7 = (bf16[256,512]{1,0:T(8,128)(2,1)S(1)}, bf16[256,512]{1,0:T(8,128)(2,1)S(1)}, u32[]{:S(2)}, u32[]{:S(2)}) collective-permute-start(bf16[256,512]{1,0:T(8,128)(2,1)S(1)} %collective-permute-done.3.rest_0_), channel_id=1, source_target_pairs={{0,8},{8,0},{16,24},{24,16},{32,40},{40,32},{48,56},{56,48},{64,72... | collective-permute-start | bytes 786440 | tf_op jit(solution)/shard_map/ppermute | solution.py:521
  24.8 1.7 %collective-permute-start.8 = (bf16[192,512]{1,0:T(8,128)(2,1)S(1)}, bf16[192,512]{1,0:T(8,128)(2,1)S(1)}, u32[]{:S(2)}, u32[]{:S(2)}) collective-permute-start(bf16[192,512]{1,0:T(8,128)(2,1)S(1)} %collective-permute-done.4.rest_1_), channel_id=1, source_target_pairs={{0,8},{8,0},{16,24},{24,16},{32,40},{40,32},{48,56},{56,48},{64,72... | collective-permute-start | bytes 589832 | tf_op jit(solution)/shard_map/ppermute | solution.py:521
  24.9 1.6 %collective-permute-start.9 = (bf16[64,512]{1,0:T(8,128)(2,1)S(1)}, bf16[64,512]{1,0:T(8,128)(2,1)S(1)}, u32[]{:S(2)}, u32[]{:S(2)}) collective-permute-start(bf16[64,512]{1,0:T(8,128)(2,1)S(1)} %collective-permute-done.5.rest_2_), channel_id=1, source_target_pairs={{0,8},{8,0},{16,24},{24,16},{32,40},{40,32},{48,56},{56,48},{64,72... | collective-permute-start | bytes 196616 | tf_op jit(solution)/shard_map/ppermute | solution.py:521
  25.3 1.2 %collective-permute-start.10 = (bf16[16,512]{1,0:T(8,128)(2,1)S(1)}, bf16[16,512]{1,0:T(8,128)(2,1)S(1)}, u32[]{:S(2)}, u32[]{:S(2)}) collective-permute-start(bf16[16,512]{1,0:T(8,128)(2,1)S(1)} %collective-permute-done.6.rest_3_), channel_id=1, source_target_pairs={{0,8},{8,0},{16,24},{24,16},{32,40},{40,32},{48,56},{56,48},{64,72... | collective-permute-start | bytes 49160 | tf_op jit(solution)/shard_map/ppermute | solution.py:521
  26.5 5.7 %copy-start.7 = (bf16[16,512]{1,0:T(8,128)(2,1)}, bf16[16,512]{1,0:T(8,128)(2,1)S(1)}, u32[]{:S(2)}) copy-start(bf16[16,512]{1,0:T(8,128)(2,1)S(1)} %collective-permute-done.10.rest_7_) | copy-start | bytes 49156
  26.5 5.7 %copy-start.5 = (bf16[64,512]{1,0:T(8,128)(2,1)}, bf16[64,512]{1,0:T(8,128)(2,1)S(1)}, u32[]{:S(2)}) copy-start(bf16[64,512]{1,0:T(8,128)(2,1)S(1)} %collective-permute-done.9.rest_6_) | copy-start | bytes 196612
  26.5 5.7 %copy-start.3 = (bf16[192,512]{1,0:T(8,128)(2,1)}, bf16[192,512]{1,0:T(8,128)(2,1)S(1)}, u32[]{:S(2)}) copy-start(bf16[192,512]{1,0:T(8,128)(2,1)S(1)} %collective-permute-done.8.rest_5_) | copy-start | bytes 589828
  26.5 5.7 %copy-start.1 = (bf16[256,512]{1,0:T(8,128)(2,1)}, bf16[256,512]{1,0:T(8,128)(2,1)S(1)}, u32[]{:S(2)}) copy-start(bf16[256,512]{1,0:T(8,128)(2,1)S(1)} %collective-permute-done.7.rest_4_) | copy-start | bytes 786436
  32.2 33.4 %all-to-all-start = ((s16[16,448,128]{2,1,0:T(8,128)(2,1)}), s16[16,448,128]{2,1,0:T(8,128)(2,1)S(1)}, u32[]{:S(2)}, u32[]{:S(2)}) async-start(s16[16,448,128]{2,1,0:T(8,128)(2,1)} %shard_map.69.rest_9_), calls=%async_computation | async-start | bytes 3670016 | tf_op jit(solution)/shard_map/all_to_all | solution.py:523
  43.4 7.7 %copy-start.13 = (f32[512,256]{1,0:T(8,128)S(1)}, f32[512,256]{1,0:T(8,128)}, u32[]{:S(2)}) copy-start(f32[512,256]{1,0:T(8,128)} %get-tuple-element.44) | copy-start | bytes 1572868
  43.4 7.7 %collective-permute-start.12 = (f32[512,256]{1,0:T(8,128)}, f32[512,256]{1,0:T(8,128)S(1)}, u32[]{:S(2)}, u32[]{:S(2)}) collective-permute-start(f32[512,256]{1,0:T(8,128)} %get-tuple-element.45), channel_id=1, source_target_pairs={{0,8},{8,0},{16,24},{24,16},{32,40},{40,32},{48,56},{56,48},{64,72... | collective-permute-start | bytes 1572872 | tf_op jit(solution)/shard_map/ppermute | solution.py:527
  50.9 2.2 %collective-permute-start.11 = (f32[512,256]{1,0:T(8,128)}, f32[512,256]{1,0:T(8,128)S(1)}, u32[]{:S(2)}, u32[]{:S(2)}) collective-permute-start(f32[512,256]{1,0:T(8,128)} %get-tuple-element.42), channel_id=1, source_target_pairs={{0,8},{8,0},{16,24},{24,16},{32,40},{40,32},{48,56},{56,48},{64,72... | collective-permute-start | bytes 1572872 | tf_op jit(solution)/shard_map/ppermute | solution.py:526
  92.8 5.3 %collective-permute-start.13 = (s16[16,64,128]{2,1,0:T(8,128)(2,1)S(1)}, s16[16,64,128]{2,1,0:T(8,128)(2,1)S(1)}, u32[]{:S(2)}, u32[]{:S(2)}) collective-permute-start(s16[16,64,128]{2,1,0:T(8,128)(2,1)S(1)} %all_to_all.16.got_ref), channel_id=1, source_target_pairs={{0,8},{8,0},{16,24},{24,16},{32,40},{40,32},{48,56},{56,48},{64,72... | collective-permute-start | bytes 786440 | tf_op jit(solution)/shard_map/ppermute | solution.py:532

commit v6 on v5

--- a/solution.py
+++ b/solution.py
@@ -105,9 +105,9 @@
     chip = own // 2
     for group in range(4):
         lanes = slice(group * HALF, (group + 1) * HALF)
-        parts[core, group] = own_ref[:, lanes].astype(f32)
+        parts[core, group, 0:512, :] = own_ref[:, lanes].astype(f32)
         mate_ref, at = (mate_x_ref, lanes) if group < 2 else (mate_c_ref, slice(lanes.start - 256, lanes.stop - 256))
-        parts[1 - core, group] = mate_ref[:, at].astype(f32)
+        parts[1 - core, group, 0:512, :] = mate_ref[:, at].astype(f32)
     for brick in range(2):
         for k, *shifts in OFFSETS:
             target = jnp.where(core == brick, links_ref[k], mate_links_ref[k])
@@ -134,7 +134,7 @@
         out_shape=tuple(jax.ShapeDtypeStruct((rows, 512), bf16) for rows in ROWS),
         in_specs=[smem(), smem()] + [vmem()] * 3,
         out_specs=(vmem(),) * 4,
-        scratch_shapes=[pltpu.VMEM((2, 4, 512, HALF), f32)],
+        scratch_shapes=[pltpu.VMEM((2, 4, 576, HALF), f32)],
         compiler_params=params(LQ),
         cost_estimate=cost(2.5),
     )(links, mate_links, own, mate_x, mate_c)
@@ -156,8 +156,8 @@
             c_half_ref[1 - here] = mate_c_ref[:, lanes]
 
     for brick in range(2):
-        parts[brick, 0] = x_half_ref[brick].astype(f32)
-        parts[brick, 1] = c_half_ref[brick].astype(f32)
+        parts[brick, 0, 0:512, :] = x_half_ref[brick].astype(f32)
+        parts[brick, 1, 0:512, :] = c_half_ref[brick].astype(f32)
         for k, *shifts in OFFSETS:
             target = jnp.where(core == brick, links_ref[k], mate_links_ref[k])
 
@@ -184,7 +184,7 @@
         ),
         in_specs=[smem(), smem()] + [vmem()] * 3 + [anywhere()],
         out_specs=(vmem(),) * 4,
-        scratch_shapes=[pltpu.VMEM((2, 2, 512, HALF), f32)],
+        scratch_shapes=[pltpu.VMEM((2, 2, 576, HALF), f32)],
         compiler_params=params(LP),
         cost_estimate=cost(1.5),
     )(links, mate_links, own, mate_x, mate_c, after)
@@ -297,11 +297,11 @@
 
 HALO_SCRATCH = [pltpu.VMEM((HERE + 256, HALF), bf16), pltpu.SemaphoreType.DMA((9,))]
 FILL_SCRATCH = [
-    pltpu.VMEM((832, HALF), f32),
+    pltpu.VMEM((840, HALF), f32),
     pltpu.VMEM((104, HALF), f32),
     pltpu.VMEM((104, HALF), f32),
-    pltpu.VMEM((832, HALF), f32),
-    pltpu.VMEM((832, HALF), f32),
+    pltpu.VMEM((840, HALF), f32),
+    pltpu.VMEM((840, HALF), f32),
     pltpu.VMEM((2, 640, 9 * HALF), bf16),
 ]
 

time: 100 us -> 100 us (level)
  no operation moved by 1% of the time
where the time goes in v6:
time: 100 us; the launch traced here: 99.4 us
  blocking collectives  26.5 us (26%)
  Pallas kernels  24 us (24%)
  starting transfers between devices  23.2 us (23%)
  waiting for transfers between devices  19.7 us (20%)
  other arithmetic  4.31 us (4%)
  between operations  1.08 us (1%)
    all_to_all x1, blocking collectives, body(): scene_terms = lax.all_to_all(scene_sum(got_terms), 'dp', 0, 0, tiled=True)  15.9 us
    pallas_call x2, Pallas kernels, taps_product(): pl.pallas_call(functools.partial(taps_kernel, turned), out_shape=(jax.Sha...  13.3 us
    all_to_all x1, blocking collectives, body(): lax.all_to_all(whole, 'space', 0, 0, tiled=True, axis_index_groups=same_c...  10.6 us
    all_to_all x1, waiting for transfers between devices, body(): lax.all_to_all(terms, 'space', 0, 0, tiled=True, axis_index_groups=same_c...  10.5 us
    ppermute x4, waiting for transfers between devices, body(): halos.append(lax.ppermute(rows, 'space', up + down))  5.62 us
    pallas_call x1, Pallas kernels, kernel_grad(): pl.pallas_call(kernel_grad_kernel, out_shape=jax.ShapeDtypeStruct((CHIPS,...  5.53 us
    ppermute x4, starting transfers between devices, body(): halos.append(lax.ppermute(rows, 'space', up + down))  5.17 us
    all_to_all x1, starting transfers between devices, body(): lax.all_to_all(terms, 'space', 0, 0, tiled=True, axis_index_groups=same_c...  4.93 us
  transfers between devices with their start and end apart: 15, of which 6 were waited for; matrix products, arithmetic and copies ran while one was open for 4% of the time, Pallas kernels for 15%

profile of v6, /device:TPU:1, one launch (start us, length us, event | category | flops | bytes accessed | tf_op | source)
XLA Modules:
  0.0 99.4 jit_solution(12753493748304277153)
XLA Ops:
  0.6 3.3 %collective-permute-start.1 = (bf16[512,256]{1,0:T(8,128)(2,1)}, bf16[512,256]{1,0:T(8,128)(2,1)S(1)}, u32[]{:S(2)}, u32[]{:S(2)}) collective-permute-start(bf16[512,256]{1,0:T(8,128)(2,1)} %bitcast.8), channel_id=1, source_target_pairs={{0,8},{8,0},{16,24},{24,16},{32,40},{40,32},{48,56},{56,48},{64,72... | collective-permute-start | bytes 786440 | tf_op jit(solution)/shard_map/ppermute | solution.py:511
  4.1 0.7 maximum_bitcast_fusion.links_ref
  4.7 0.4 collective-permute-start
  5.1 1.1 %pad_maximum_fusion.own_ref = bf16[512,512]{1,0:T(8,128)(2,1)S(1)} fusion(bf16[512,256]{1,0:T(8,128)(2,1)} %bitcast.11, bf16[512,256]{1,0:T(8,128)(2,1)} %bitcast.9), kind=kLoop, calls=%fused_computation | loop fusion | flops 1048576 | bytes 1048576 | tf_op jit(solution)/shard_map/concatenate | solution.py:512
  6.2 1.6 %shard_map.67 = (bf16[256,512]{1,0:T(8,128)(2,1)S(1)}, bf16[192,512]{1,0:T(8,128)(2,1)S(1)}, bf16[64,512]{1,0:T(8,128)(2,1)S(1)}, bf16[16,512]{1,0:T(8,128)(2,1)S(1)}) custom-call(s32[27]{0:T(128)S(1)} %maximum_bitcast_fusion.links_ref, s32[27]{0:T(128)S(1)} %collective-permute-done.mate_links_ref, bf16[512,512]{1,0:T(8,128)(2,1)S(1)} %pad_maximum_fusion.own_ref, ...), custom_call_target="tpu_custom_call" | custom-call | flops 2500000000 | bytes 1048576 | tf_op jit(solution)/shard_map/pallas_call | solution.py:132
  7.8 1.3 %collective-permute-start.3 = (bf16[256,512]{1,0:T(8,128)(2,1)S(1)}, bf16[256,512]{1,0:T(8,128)(2,1)S(1)}, u32[]{:S(2)}, u32[]{:S(2)}) collective-permute-start(bf16[256,512]{1,0:T(8,128)(2,1)S(1)} %get-tuple-element.26), channel_id=1, source_target_pairs={{0,16},{16,32},{32,48},{48,64},{64,80},{80,96},{96,112},{112,128},... | collective-permute-start | bytes 786440 | tf_op jit(solution)/shard_map/ppermute | solution.py:518
  9.1 1.3 %collective-permute-start.4 = (bf16[192,512]{1,0:T(8,128)(2,1)S(1)}, bf16[192,512]{1,0:T(8,128)(2,1)S(1)}, u32[]{:S(2)}, u32[]{:S(2)}) collective-permute-start(bf16[192,512]{1,0:T(8,128)(2,1)S(1)} %get-tuple-element.27), channel_id=1, source_target_pairs={{0,32},{16,48},{32,64},{48,80},{64,96},{80,112},{96,128},{112,144}... | collective-permute-start | bytes 589832 | tf_op jit(solution)/shard_map/ppermute | solution.py:518
  10.4 1.3 %collective-permute-start.6 = (bf16[16,512]{1,0:T(8,128)(2,1)S(1)}, bf16[16,512]{1,0:T(8,128)(2,1)S(1)}, u32[]{:S(2)}, u32[]{:S(2)}) collective-permute-start(bf16[16,512]{1,0:T(8,128)(2,1)S(1)} %get-tuple-element.29._), channel_id=1, source_target_pairs={{0,64},{16,80},{32,96},{48,112},{64,128},{80,144},{96,160},{112,17... | collective-permute-start | bytes 49160 | tf_op jit(solution)/shard_map/ppermute | solution.py:518
  11.7 1.3 %collective-permute-start.5 = (bf16[64,512]{1,0:T(8,128)(2,1)S(1)}, bf16[64,512]{1,0:T(8,128)(2,1)S(1)}, u32[]{:S(2)}, u32[]{:S(2)}) collective-permute-start(bf16[64,512]{1,0:T(8,128)(2,1)S(1)} %get-tuple-element.28), channel_id=1, source_target_pairs={{0,48},{16,64},{32,80},{48,96},{64,112},{80,128},{96,144},{112,160... | collective-permute-start | bytes 196616 | tf_op jit(solution)/shard_map/ppermute | solution.py:518
  13.0 1.7 %shard_map.68 = (bf16[256,256]{1,0:T(8,128)(2,1)S(1)}, bf16[2,256,512]{2,1,0:T(8,128)(2,1)S(1)}, bf16[2,512,128]{2,1,0:T(8,128)(2,1)S(1)}, bf16[2,512,128]{2,1,0:T(8,128)(2,1)S(1)}) custom-call(s32[27]{0:T(128)S(1)} %maximum_bitcast_fusion.links_ref, s32[27]{0:T(128)S(1)} %collective-permute-done.mate_links_ref, ...), custom_call_target="tpu_custom_call" | custom-call | flops 1500000000 | bytes 1048576 | tf_op jit(solution)/shard_map/pallas_call | solution.py:177
  14.7 0.7 copy-done.11
  15.4 1.8 %collective-permute-done.6.rest_3_ = bf16[16,512]{1,0:T(8,128)(2,1)S(1)} collective-permute-done((bf16[16,512]{1,0:T(8,128)(2,1)S(1)}, bf16[16,512]{1,0:T(8,128)(2,1)S(1)}, u32[]{:S(2)}, u32[]{:S(2)}) %collective-permute-start.6) | collective-permute-done | bytes 16416 | tf_op jit(solution)/shard_map/ppermute | solution.py:518
  17.2 3.8 %collective-permute-done.5.rest_2_ = bf16[64,512]{1,0:T(8,128)(2,1)S(1)} collective-permute-done((bf16[64,512]{1,0:T(8,128)(2,1)S(1)}, bf16[64,512]{1,0:T(8,128)(2,1)S(1)}, u32[]{:S(2)}, u32[]{:S(2)}) %collective-permute-start.5) | collective-permute-done | bytes 65568 | tf_op jit(solution)/shard_map/ppermute | solution.py:518
  21.0 3.7 %collective-permute-start.7 = (bf16[256,512]{1,0:T(8,128)(2,1)S(1)}, bf16[256,512]{1,0:T(8,128)(2,1)S(1)}, u32[]{:S(2)}, u32[]{:S(2)}) collective-permute-start(bf16[256,512]{1,0:T(8,128)(2,1)S(1)} %collective-permute-done.3.rest_0_), channel_id=1, source_target_pairs={{0,8},{8,0},{16,24},{24,16},{32,40},{40,32},{48,56},{56,48},{64,72... | collective-permute-start | bytes 786440 | tf_op jit(solution)/shard_map/ppermute | solution.py:521
  24.9 0.4 collective-permute-start.9
  25.4 1.1 %collective-permute-done.10.rest_7_ = bf16[16,512]{1,0:T(8,128)(2,1)S(1)} collective-permute-done((bf16[16,512]{1,0:T(8,128)(2,1)S(1)}, bf16[16,512]{1,0:T(8,128)(2,1)S(1)}, u32[]{:S(2)}, u32[]{:S(2)}) %collective-permute-start.10) | collective-permute-done | bytes 16416 | tf_op jit(solution)/shard_map/ppermute | solution.py:521
  26.5 5.5 %shard_map.69.rest_9_ = s16[16,448,128]{2,1,0:T(8,128)(2,1)} custom-call(s32[27]{0:T(128)S(1)} %maximum_bitcast_fusion.links_ref, s32[27]{0:T(128)S(1)} %collective-permute-done.mate_links_ref, bf16[2,512,128]{2,1,0:T(8,128)(2,1)S(1)} %get-tuple-element.34.c_half_ref.half_ref, bf16[2,256,512]{2,1,0:T(8,128)(2,1)S(1)} %get-tuple-element.35.turned_ref, ...), custom_call_target="tpu_custom_call" | custom-call | flops 6000000000 | bytes 1048576 | tf_op jit(solution)/shard_map/pallas_call | solution.py:342
  32.2 4.9 %all-to-all-start = ((s16[16,448,128]{2,1,0:T(8,128)(2,1)}), s16[16,448,128]{2,1,0:T(8,128)(2,1)S(1)}, u32[]{:S(2)}, u32[]{:S(2)}) async-start(s16[16,448,128]{2,1,0:T(8,128)(2,1)} %shard_map.69.rest_9_), calls=%async_computation | async-start | bytes 3670016 | tf_op jit(solution)/shard_map/all_to_all | solution.py:523
  37.1 6.4 %shard_map.71 = (f32[512,256]{1,0:T(8,128)}, f32[512,256]{1,0:T(8,128)}) custom-call(s32[27]{0:T(128)} %copy-done.8, s32[27]{0:T(128)} %copy-done.9, bf16[2,512,128]{2,1,0:T(8,128)(2,1)} %copy-done.11, bf16[27,256,256]{2,1,0:T(8,128)(2,1)} %weight_ref.3, bf16[256,512]{1,0:T(8,128)(2,1)} %copy-done, bf16[192,512]{1,0:T(8,128)(2,1)} %copy-done.2, ...), custom_call_target="tpu_custom_call" | custom-call | flops 6000000000 | bytes 1048576 | tf_op jit(solution)/shard_map/pallas_call | solution.py:396
  43.5 0.6 collective-permute-start.12
  44.1 6.9 %shard_map.70 = (f32[512,256]{1,0:T(8,128)}, f32[512,256]{1,0:T(8,128)}) custom-call(s32[27]{0:T(128)} %copy-done.8, s32[27]{0:T(128)} %copy-done.9, bf16[2,512,128]{2,1,0:T(8,128)(2,1)} %copy-done.10, bf16[27,256,256]{2,1,0:T(8,128)(2,1)} %weight_ref.3, bf16[256,512]{1,0:T(8,128)(2,1)} %copy-done, bf16[192,512]{1,0:T(8,128)(2,1)} %copy-done.2, ...), custom_call_target="tpu_custom_call" | custom-call | flops 6000000000 | bytes 1048576 | tf_op jit(solution)/shard_map/pallas_call | solution.py:396
  51.0 0.2 collective-permute-start.11
  51.1 0.8 add_convert_fusion
  51.9 1.3 %collective-permute-done.11 = f32[512,256]{1,0:T(8,128)S(1)} collective-permute-done((f32[512,256]{1,0:T(8,128)}, f32[512,256]{1,0:T(8,128)S(1)}, u32[]{:S(2)}, u32[]{:S(2)}) %collective-permute-start.11) | collective-permute-done | bytes 524320 | tf_op jit(solution)/shard_map/ppermute | solution.py:526
  53.2 1.8 %add_convert_fusion.1 = bf16[512,256]{1,0:T(8,128)(2,1)} fusion(f32[512,256]{1,0:T(8,128)} %get-tuple-element.41, f32[512,256]{1,0:T(8,128)S(1)} %collective-permute-done.11), kind=kLoop, calls=%fused_computation.2 | loop fusion | flops 262144 | bytes 1310720 | tf_op jit(solution)/shard_map/convert_element_type | solution.py:526
  55.0 10.5 %all-to-all-done.got_ref = s16[16,448,128]{2,1,0:T(8,128)(2,1)S(1)} async-done(((s16[16,448,128]{2,1,0:T(8,128)(2,1)}), s16[16,448,128]{2,1,0:T(8,128)(2,1)S(1)}, u32[]{:S(2)}, u32[]{:S(2)}) %all-to-all-start) | async-done | bytes 1835040 | tf_op jit(solution)/shard_map/all_to_all | solution.py:523
  65.5 0.7 shard_map.72
  66.2 15.9 %all_to_all.15.got_ref = s16[8,64,128]{2,1,0:T(8,128)(2,1)S(1)} all-to-all(s16[8,64,128]{2,1,0:T(8,128)(2,1)S(1)} %shard_map.72), channel_id=1, replica_groups=mesh['space'=32,'dp'=8] {'dp'}, dimensions={0} | all-to-all | bytes 262144 | tf_op jit(solution)/shard_map/all_to_all | solution.py:529
  82.2 10.6 %all_to_all.16.got_ref = s16[16,64,128]{2,1,0:T(8,128)(2,1)S(1)} all-to-all(s16[16,64,128]{2,1,0:T(8,128)(2,1)S(1)} %shard_map.73), channel_id=1, replica_groups={{0,16,32,48,64,80,96,112,128,144,160,176,192,208,224,240},{8,24,40,56,7..., dimensions={0} | all-to-all | bytes 524288 | tf_op jit(solution)/shard_map/all_to_all | solution.py:531
  92.8 4.1 %collective-permute-start.13 = (s16[16,64,128]{2,1,0:T(8,128)(2,1)S(1)}, s16[16,64,128]{2,1,0:T(8,128)(2,1)S(1)}, u32[]{:S(2)}, u32[]{:S(2)}) collective-permute-start(s16[16,64,128]{2,1,0:T(8,128)(2,1)S(1)} %all_to_all.16.got_ref), channel_id=1, source_target_pairs={{0,8},{8,0},{16,24},{24,16},{32,40},{40,32},{48,56},{56,48},{64,72... | collective-permute-start | bytes 786440 | tf_op jit(solution)/shard_map/ppermute | solution.py:532
  96.9 1.2 %collective-permute-done.13.mate_ref = s16[16,64,128]{2,1,0:T(8,128)(2,1)S(1)} collective-permute-done((s16[16,64,128]{2,1,0:T(8,128)(2,1)S(1)}, s16[16,64,128]{2,1,0:T(8,128)(2,1)S(1)}, u32[]{:S(2)}, u32[]{:S(2)}) %collective-permute-start.13) | collective-permute-done | bytes 262176 | tf_op jit(solution)/shard_map/ppermute | solution.py:532
  98.1 1.2 %shard_map.74 = f32[864,256]{1,0:T(8,128)} custom-call(s16[16,64,128]{2,1,0:T(8,128)(2,1)S(1)} %all_to_all.16.got_ref, s16[16,64,128]{2,1,0:T(8,128)(2,1)S(1)} %collective-permute-done.13.mate_ref), custom_call_target="tpu_custom_call" | custom-call | tf_op jit(solution)/shard_map/pallas_call | solution.py:493
  (40 shorter events, 0.5 us)
Async XLA Ops:
  0.6 5.6 %collective-permute-start.1 = (bf16[512,256]{1,0:T(8,128)(2,1)}, bf16[512,256]{1,0:T(8,128)(2,1)S(1)}, u32[]{:S(2)}, u32[]{:S(2)}) collective-permute-start(bf16[512,256]{1,0:T(8,128)(2,1)} %bitcast.8), channel_id=1, source_target_pairs={{0,8},{8,0},{16,24},{24,16},{32,40},{40,32},{48,56},{56,48},{64,72... | collective-permute-start | bytes 786440 | tf_op jit(solution)/shard_map/ppermute | solution.py:511
  4.0 2.3 %collective-permute-start.2 = (bf16[512,256]{1,0:T(8,128)(2,1)}, bf16[512,256]{1,0:T(8,128)(2,1)S(1)}, u32[]{:S(2)}, u32[]{:S(2)}) collective-permute-start(bf16[512,256]{1,0:T(8,128)(2,1)} %bitcast.10), channel_id=1, source_target_pairs={{0,8},{8,0},{16,24},{24,16},{32,40},{40,32},{48,56},{56,48},{64,72... | collective-permute-start | bytes 786440 | tf_op jit(solution)/shard_map/ppermute | solution.py:511
  4.7 21.8 %copy-start.8 = (s32[27]{0:T(128)}, s32[27]{0:T(128)S(1)}, u32[]{:S(2)}) copy-start(s32[27]{0:T(128)S(1)} %maximum_bitcast_fusion.links_ref) | copy-start | bytes 328
  4.7 1.5 %collective-permute-start = (s32[27]{0:T(128)S(1)}, s32[27]{0:T(128)S(1)}, u32[]{:S(2)}, u32[]{:S(2)}) collective-permute-start(s32[27]{0:T(128)S(1)} %maximum_bitcast_fusion.links_ref), channel_id=1, source_target_pairs={{0,8},{8,0},{16,24},{24,16},{32,40},{40,32},{48,56},{56,48},{64,72... | collective-permute-start | bytes 332 | tf_op jit(solution)/shard_map/ppermute | solution.py:511
  6.2 20.3 %copy-start.9 = (s32[27]{0:T(128)}, s32[27]{0:T(128)S(1)}, u32[]{:S(2)}) copy-start(s32[27]{0:T(128)S(1)} %collective-permute-done.mate_links_ref) | copy-start | bytes 328
  7.8 13.2 %collective-permute-start.3 = (bf16[256,512]{1,0:T(8,128)(2,1)S(1)}, bf16[256,512]{1,0:T(8,128)(2,1)S(1)}, u32[]{:S(2)}, u32[]{:S(2)}) collective-permute-start(bf16[256,512]{1,0:T(8,128)(2,1)S(1)} %get-tuple-element.26), channel_id=1, source_target_pairs={{0,16},{16,32},{32,48},{48,64},{64,80},{80,96},{96,112},{112,128},... | collective-permute-start | bytes 786440 | tf_op jit(solution)/shard_map/ppermute | solution.py:518
  9.1 11.9 %collective-permute-start.4 = (bf16[192,512]{1,0:T(8,128)(2,1)S(1)}, bf16[192,512]{1,0:T(8,128)(2,1)S(1)}, u32[]{:S(2)}, u32[]{:S(2)}) collective-permute-start(bf16[192,512]{1,0:T(8,128)(2,1)S(1)} %get-tuple-element.27), channel_id=1, source_target_pairs={{0,32},{16,48},{32,64},{48,80},{64,96},{80,112},{96,128},{112,144}... | collective-permute-start | bytes 589832 | tf_op jit(solution)/shard_map/ppermute | solution.py:518
  10.4 6.8 %collective-permute-start.6 = (bf16[16,512]{1,0:T(8,128)(2,1)S(1)}, bf16[16,512]{1,0:T(8,128)(2,1)S(1)}, u32[]{:S(2)}, u32[]{:S(2)}) collective-permute-start(bf16[16,512]{1,0:T(8,128)(2,1)S(1)} %get-tuple-element.29._), channel_id=1, source_target_pairs={{0,64},{16,80},{32,96},{48,112},{64,128},{80,144},{96,160},{112,17... | collective-permute-start | bytes 49160 | tf_op jit(solution)/shard_map/ppermute | solution.py:518
  11.7 9.3 %collective-permute-start.5 = (bf16[64,512]{1,0:T(8,128)(2,1)S(1)}, bf16[64,512]{1,0:T(8,128)(2,1)S(1)}, u32[]{:S(2)}, u32[]{:S(2)}) collective-permute-start(bf16[64,512]{1,0:T(8,128)(2,1)S(1)} %get-tuple-element.28), channel_id=1, source_target_pairs={{0,48},{16,64},{32,80},{48,96},{64,112},{80,128},{96,144},{112,160... | collective-permute-start | bytes 196616 | tf_op jit(solution)/shard_map/ppermute | solution.py:518
  14.7 0.7 copy-start.11
  15.4 16.7 %copy-start.10 = (bf16[2,512,128]{2,1,0:T(8,128)(2,1)}, bf16[2,512,128]{2,1,0:T(8,128)(2,1)S(1)}, u32[]{:S(2)}) copy-start(bf16[2,512,128]{2,1,0:T(8,128)(2,1)S(1)} %get-tuple-element.34.c_half_ref.half_ref) | copy-start | bytes 786436
  15.4 16.7 %copy-start.12 = (bf16[256,256]{1,0:T(8,128)(2,1)}, bf16[256,256]{1,0:T(8,128)(2,1)S(1)}, u32[]{:S(2)}) copy-start(bf16[256,256]{1,0:T(8,128)(2,1)S(1)} %get-tuple-element.40.rest_8_) | copy-start | bytes 393220
  17.2 14.9 %copy-start.6 = (bf16[16,512]{1,0:T(8,128)(2,1)}, bf16[16,512]{1,0:T(8,128)(2,1)S(1)}, u32[]{:S(2)}) copy-start(bf16[16,512]{1,0:T(8,128)(2,1)S(1)} %collective-permute-done.6.rest_3_) | copy-start | bytes 49156
  21.0 11.1 %copy-start.4 = (bf16[64,512]{1,0:T(8,128)(2,1)}, bf16[64,512]{1,0:T(8,128)(2,1)S(1)}, u32[]{:S(2)}) copy-start(bf16[64,512]{1,0:T(8,128)(2,1)S(1)} %collective-permute-done.5.rest_2_) | copy-start | bytes 196612
  21.0 11.1 %copy-start.2 = (bf16[192,512]{1,0:T(8,128)(2,1)}, bf16[192,512]{1,0:T(8,128)(2,1)S(1)}, u32[]{:S(2)}) copy-start(bf16[192,512]{1,0:T(8,128)(2,1)S(1)} %collective-permute-done.4.rest_1_) | copy-start | bytes 589828
  21.0 11.1 %copy-start = (bf16[256,512]{1,0:T(8,128)(2,1)}, bf16[256,512]{1,0:T(8,128)(2,1)S(1)}, u32[]{:S(2)}) copy-start(bf16[256,512]{1,0:T(8,128)(2,1)S(1)} %collective-permute-done.3.rest_0_) | copy-start | bytes 786436
  21.0 5.4 %collective-permute-start.7 = (bf16[256,512]{1,0:T(8,128)(2,1)S(1)}, bf16[256,512]{1,0:T(8,128)(2,1)S(1)}, u32[]{:S(2)}, u32[]{:S(2)}) collective-permute-start(bf16[256,512]{1,0:T(8,128)(2,1)S(1)} %collective-permute-done.3.rest_0_), channel_id=1, source_target_pairs={{0,8},{8,0},{16,24},{24,16},{32,40},{40,32},{48,56},{56,48},{64,72... | collective-permute-start | bytes 786440 | tf_op jit(solution)/shard_map/ppermute | solution.py:521
  24.8 1.7 %collective-permute-start.8 = (bf16[192,512]{1,0:T(8,128)(2,1)S(1)}, bf16[192,512]{1,0:T(8,128)(2,1)S(1)}, u32[]{:S(2)}, u32[]{:S(2)}) collective-permute-start(bf16[192,512]{1,0:T(8,128)(2,1)S(1)} %collective-permute-done.4.rest_1_), channel_id=1, source_target_pairs={{0,8},{8,0},{16,24},{24,16},{32,40},{40,32},{48,56},{56,48},{64,72... | collective-permute-start | bytes 589832 | tf_op jit(solution)/shard_map/ppermute | solution.py:521
  24.9 1.6 %collective-permute-start.9 = (bf16[64,512]{1,0:T(8,128)(2,1)S(1)}, bf16[64,512]{1,0:T(8,128)(2,1)S(1)}, u32[]{:S(2)}, u32[]{:S(2)}) collective-permute-start(bf16[64,512]{1,0:T(8,128)(2,1)S(1)} %collective-permute-done.5.rest_2_), channel_id=1, source_target_pairs={{0,8},{8,0},{16,24},{24,16},{32,40},{40,32},{48,56},{56,48},{64,72... | collective-permute-start | bytes 196616 | tf_op jit(solution)/shard_map/ppermute | solution.py:521
  25.3 1.2 %collective-permute-start.10 = (bf16[16,512]{1,0:T(8,128)(2,1)S(1)}, bf16[16,512]{1,0:T(8,128)(2,1)S(1)}, u32[]{:S(2)}, u32[]{:S(2)}) collective-permute-start(bf16[16,512]{1,0:T(8,128)(2,1)S(1)} %collective-permute-done.6.rest_3_), channel_id=1, source_target_pairs={{0,8},{8,0},{16,24},{24,16},{32,40},{40,32},{48,56},{56,48},{64,72... | collective-permute-start | bytes 49160 | tf_op jit(solution)/shard_map/ppermute | solution.py:521
  26.5 5.7 %copy-start.7 = (bf16[16,512]{1,0:T(8,128)(2,1)}, bf16[16,512]{1,0:T(8,128)(2,1)S(1)}, u32[]{:S(2)}) copy-start(bf16[16,512]{1,0:T(8,128)(2,1)S(1)} %collective-permute-done.10.rest_7_) | copy-start | bytes 49156
  26.5 5.7 %copy-start.5 = (bf16[64,512]{1,0:T(8,128)(2,1)}, bf16[64,512]{1,0:T(8,128)(2,1)S(1)}, u32[]{:S(2)}) copy-start(bf16[64,512]{1,0:T(8,128)(2,1)S(1)} %collective-permute-done.9.rest_6_) | copy-start | bytes 196612
  26.5 5.7 %copy-start.3 = (bf16[192,512]{1,0:T(8,128)(2,1)}, bf16[192,512]{1,0:T(8,128)(2,1)S(1)}, u32[]{:S(2)}) copy-start(bf16[192,512]{1,0:T(8,128)(2,1)S(1)} %collective-permute-done.8.rest_5_) | copy-start | bytes 589828
  26.5 5.6 %copy-start.1 = (bf16[256,512]{1,0:T(8,128)(2,1)}, bf16[256,512]{1,0:T(8,128)(2,1)S(1)}, u32[]{:S(2)}) copy-start(bf16[256,512]{1,0:T(8,128)(2,1)S(1)} %collective-permute-done.7.rest_4_) | copy-start | bytes 786436
  32.2 33.4 %all-to-all-start = ((s16[16,448,128]{2,1,0:T(8,128)(2,1)}), s16[16,448,128]{2,1,0:T(8,128)(2,1)S(1)}, u32[]{:S(2)}, u32[]{:S(2)}) async-start(s16[16,448,128]{2,1,0:T(8,128)(2,1)} %shard_map.69.rest_9_), calls=%async_computation | async-start | bytes 3670016 | tf_op jit(solution)/shard_map/all_to_all | solution.py:523
  43.5 7.7 %copy-start.13 = (f32[512,256]{1,0:T(8,128)S(1)}, f32[512,256]{1,0:T(8,128)}, u32[]{:S(2)}) copy-start(f32[512,256]{1,0:T(8,128)} %get-tuple-element.44) | copy-start | bytes 1572868
  43.5 7.7 %collective-permute-start.12 = (f32[512,256]{1,0:T(8,128)}, f32[512,256]{1,0:T(8,128)S(1)}, u32[]{:S(2)}, u32[]{:S(2)}) collective-permute-start(f32[512,256]{1,0:T(8,128)} %get-tuple-element.45), channel_id=1, source_target_pairs={{0,8},{8,0},{16,24},{24,16},{32,40},{40,32},{48,56},{56,48},{64,72... | collective-permute-start | bytes 1572872 | tf_op jit(solution)/shard_map/ppermute | solution.py:527
  51.0 2.2 %collective-permute-start.11 = (f32[512,256]{1,0:T(8,128)}, f32[512,256]{1,0:T(8,128)S(1)}, u32[]{:S(2)}, u32[]{:S(2)}) collective-permute-start(f32[512,256]{1,0:T(8,128)} %get-tuple-element.42), channel_id=1, source_target_pairs={{0,8},{8,0},{16,24},{24,16},{32,40},{40,32},{48,56},{56,48},{64,72... | collective-permute-start | bytes 1572872 | tf_op jit(solution)/shard_map/ppermute | solution.py:526
  92.8 5.3 %collective-permute-start.13 = (s16[16,64,128]{2,1,0:T(8,128)(2,1)S(1)}, s16[16,64,128]{2,1,0:T(8,128)(2,1)S(1)}, u32[]{:S(2)}, u32[]{:S(2)}) collective-permute-start(s16[16,64,128]{2,1,0:T(8,128)(2,1)S(1)} %all_to_all.16.got_ref), channel_id=1, source_target_pairs={{0,8},{8,0},{16,24},{24,16},{32,40},{40,32},{48,56},{56,48},{64,72... | collective-permute-start | bytes 786440 | tf_op jit(solution)/shard_map/ppermute | solution.py:532
